TPU v7x, 32 devices: a whole 2x2x4 slice. The times are simulated.
32 devices in a mesh: group: 2 (over core), expert: 16 (over z, y, x).
Axes of the slice: x: 2, y: 2, z: 4, core: 2. Of those that a mesh axis runs over, the one named last changes fastest.
Arguments:
- tokens: bfloat16 [32768, 768], P(('group', 'expert')), may hold values from -6 to 6
- gains: bfloat16 [2, 768], replicated, may hold values from 0.5 to 1.5
- qkv_weight: bfloat16 [768, 2304], replicated, may hold values from -0.21875 to 0.21875
- out_weight: bfloat16 [768, 768], replicated, may hold values from -6 to 6
- rel_bias: bfloat16 [32, 12], replicated, may hold values from -4 to 4
- router_weight: bfloat16 [768, 16], replicated, may hold values from -0.25 to 0.25
- w_in: bfloat16 [16, 768, 3072], P('expert'), may hold values from -0.21875 to 0.21875
- w_out: bfloat16 [16, 3072, 768], P('expert'), may hold values from -6 to 6
- routes: int32 [32768, 1], P(('group', 'expert')), may hold values from 0 to 15
- factors: int32 [32], P(('group', 'expert')), may hold values from 1 to 2, as said below
- cotangent: bfloat16 [32768, 768], P(('group', 'expert')), may hold values from -6 to 6
Outputs:
- output: bfloat16 [32768, 768], P(('group', 'expert'))
- grad_tokens: float32 [32768, 768], P(('group', 'expert'))
- grad_gains: float32 [2, 768], P('group', 'expert')
- grad_qkv: float32 [768, 2304], P('expert', 'group')
- grad_out_weight: float32 [768, 768], P('expert', 'group')
- grad_rel_bias: float32 [32, 12], replicated
- grad_router: float32 [768, 16], P('expert', 'group')
- grad_w_in: float32 [16, 768, 3072], P('expert', None, 'group')
- grad_w_out: float32 [16, 3072, 768], P('expert', 'group')
Inputs may be any that keep to these rules, and one draw needn't show every extreme that they name: `factors`: each sequence's capacity factor; within each run of 16 sequences, half have factor 1 and half factor 2.
All inputs are finite; a program needn't handle non-finite values.
Results may differ from a plain program's by a relative error of at most 0.019.
Values may be sent and summed in bfloat16 or wider, within the bound.
A program may use at most 320 MiB of HBM per device.

v0:
```python
import jax
import jax.numpy as jnp
from jax import lax
from jax.sharding import PartitionSpec as P

EPSILON = 1e-06
BOUNDARIES = (12, 16, 23, 32, 46, 64, 91)


def bucket_index(relative):
    distance = jnp.abs(relative)
    farther = jnp.full(relative.shape, 8, jnp.int32)
    for boundary in BOUNDARIES:
        farther = farther + (distance >= boundary).astype(jnp.int32)
    nearest = jnp.where(distance < 8, distance, farther)
    return nearest + 16 * (relative > 0).astype(jnp.int32)


def norm_rows(values, gain_row):
    return (
        values * lax.rsqrt(jnp.mean(values * values, axis=-1, keepdims=True) + EPSILON) * gain_row
    )


def per_device(
    tokens,
    gains,
    qkv_weight,
    out_weight,
    rel_bias,
    router_weight,
    w_in,
    w_out,
    routes,
    factors,
    cotangent,
):
    length, features = tokens.shape
    bucket_count, head_count = rel_bias.shape
    head_size = features // head_count
    expert_count = router_weight.shape[1]
    local_count = w_in.shape[0]
    hidden_width = w_in.shape[2]
    slot_count = 2 * length // expert_count
    query_rows = min(512, length)
    score_scale = head_size ** (-0.5)
    gain_rows = gains.astype(jnp.float32)
    inputs = tokens.astype(jnp.float32)
    normed_in = norm_rows(inputs, gain_rows[0]).astype(jnp.bfloat16)
    projected = jnp.dot(normed_in, qkv_weight, preferred_element_type=jnp.float32).astype(
        jnp.bfloat16
    )
    queries = projected[:, :features].reshape(length, head_count, head_size)
    keys_all = projected[:, features : 2 * features].reshape(length, head_count, head_size)
    values_all = projected[:, 2 * features :].reshape(length, head_count, head_size)
    row_index = jnp.arange(length, dtype=jnp.int32)
    bucket_ids = jnp.arange(bucket_count, dtype=jnp.int32)

    def bucket_onehot(offset):
        query_pos = offset + jnp.arange(query_rows, dtype=jnp.int32)
        block_buckets = bucket_index(row_index[None, :] - query_pos[:, None])
        return (block_buckets[None, :, :] == bucket_ids[:, None, None]).astype(jnp.bfloat16)

    def block_scores(offset, onehot):
        query_block = queries[offset : offset + query_rows]
        raw = jnp.einsum("qhd,khd->hqk", query_block, keys_all, preferred_element_type=jnp.float32)
        bias = jnp.einsum("cqk,ch->hqk", onehot, rel_bias, preferred_element_type=jnp.float32)
        return raw * score_scale + bias

    attended_parts = []
    log_totals = []
    for offset in range(0, length, query_rows):
        scores = block_scores(offset, bucket_onehot(offset))
        row_max = jnp.max(scores, axis=-1, keepdims=True)
        shifted_exp = jnp.exp(scores - row_max)
        row_sum = jnp.sum(shifted_exp, axis=-1, keepdims=True)
        weights = (shifted_exp / row_sum).astype(jnp.bfloat16)
        log_totals.append(row_max + jnp.log(row_sum))
        attended_parts.append(
            jnp.einsum(
                "hqk,khd->qhd", weights, values_all, preferred_element_type=jnp.float32
            ).astype(jnp.bfloat16)
        )
    attended = jnp.concatenate(attended_parts, axis=0).reshape(length, features)
    residual_one = inputs + jnp.dot(attended, out_weight, preferred_element_type=jnp.float32)
    hidden = norm_rows(residual_one, gain_rows[1]).astype(jnp.bfloat16)
    logits = jnp.dot(hidden, router_weight, preferred_element_type=jnp.float32)
    router_exp = jnp.exp(logits - jnp.max(logits, axis=-1, keepdims=True))
    router = router_exp / jnp.sum(router_exp, axis=-1, keepdims=True)
    routed = routes[:, 0]
    chosen = routed[:, None] == jnp.arange(expert_count, dtype=jnp.int32)[None, :]
    chosen_float = chosen.astype(jnp.float32)
    gate_value = jnp.sum(router * chosen_float, axis=-1)
    earlier = (row_index[:, None] > row_index[None, :]).astype(jnp.bfloat16)
    before = jnp.dot(earlier, chosen.astype(jnp.bfloat16), preferred_element_type=jnp.float32)
    place = jnp.sum(before * chosen_float, axis=-1)
    capacity = (factors[0] * (length // expert_count)).astype(jnp.float32)
    kept_mask = place < capacity
    target = jnp.where(
        kept_mask, routed * slot_count + place.astype(jnp.int32), expert_count * slot_count
    )
    slot_token = (
        jnp.full((expert_count * slot_count,), length, jnp.int32)
        .at[target]
        .set(row_index, mode="drop")
    )
    lookup = jnp.minimum(target, expert_count * slot_count - 1)
    kept_float = kept_mask.astype(jnp.float32)
    zero_row = jnp.zeros((1, features), jnp.bfloat16)
    outgoing = jnp.concatenate([hidden, zero_row], axis=0)[slot_token].reshape(
        expert_count, slot_count, features
    )
    received = lax.all_to_all(outgoing, "expert", split_axis=0, concat_axis=0, tiled=True)
    item_count = received.shape[1]
    grouped = received.reshape(-1, local_count, item_count, features)
    preact = jnp.einsum("njcd,jdf->njcf", grouped, w_in, preferred_element_type=jnp.float32)
    activated = jax.nn.gelu(preact).astype(jnp.bfloat16)
    produced = jnp.einsum(
        "njcf,jfd->njcd", activated, w_out, preferred_element_type=jnp.float32
    ).astype(jnp.bfloat16)
    returned = lax.all_to_all(
        produced.reshape(-1, item_count, features),
        "expert",
        split_axis=0,
        concat_axis=0,
        tiled=True,
    )
    brought = (
        returned.reshape(expert_count * slot_count, features)[lookup].astype(jnp.float32)
        * kept_float[:, None]
    )
    output = (residual_one + gate_value[:, None] * brought).astype(jnp.bfloat16)
    upstream = cotangent.astype(jnp.float32)
    dgate = jnp.sum(upstream * brought, axis=-1)
    dexp_rows = (upstream * (gate_value * kept_float)[:, None]).astype(jnp.bfloat16)
    dexp_send = jnp.concatenate([dexp_rows, zero_row], axis=0)[slot_token].reshape(
        expert_count, slot_count, features
    )
    dexp_recv = lax.all_to_all(dexp_send, "expert", split_axis=0, concat_axis=0, tiled=True)
    dgrouped = dexp_recv.reshape(-1, local_count, slot_count, features)
    hgrouped = received.reshape(-1, local_count, slot_count, features)
    preact = preact.reshape(-1, item_count, hidden_width).reshape(
        -1, local_count, slot_count, hidden_width
    )
    activated, gelu_back = jax.vjp(jax.nn.gelu, preact)
    activated = activated.astype(jnp.bfloat16)
    dactive = jnp.einsum("njcd,jfd->njcf", dgrouped, w_out, preferred_element_type=jnp.float32)
    dpre = gelu_back(dactive)[0].astype(jnp.bfloat16)
    grad_second = jnp.einsum(
        "njcf,njcd->jfd", activated, dgrouped, preferred_element_type=jnp.float32
    )
    grad_first = jnp.einsum("njcd,njcf->jdf", hgrouped, dpre, preferred_element_type=jnp.float32)
    dmoved = jnp.einsum("njcf,jdf->njcd", dpre, w_in, preferred_element_type=jnp.float32).astype(
        jnp.bfloat16
    )
    dreturned = lax.all_to_all(
        dmoved.reshape(-1, slot_count, features), "expert", split_axis=0, concat_axis=0, tiled=True
    )
    dexpert = (
        dreturned.reshape(expert_count * slot_count, features)[lookup].astype(jnp.float32)
        * kept_float[:, None]
    )
    dlogits = ((dgate * gate_value)[:, None] * (chosen_float - router)).astype(jnp.bfloat16)
    grad_router = jnp.einsum("td,te->de", hidden, dlogits, preferred_element_type=jnp.float32)
    dhidden = (
        jnp.einsum("te,de->td", dlogits, router_weight, preferred_element_type=jnp.float32)
        + dexpert
    )
    norm_two, back_two = jax.vjp(norm_rows, residual_one, gain_rows[1])
    dres_norm, dgain_two = back_two(dhidden)
    dres = upstream + dres_norm
    dbranch = dres.astype(jnp.bfloat16)
    grad_out = jnp.einsum("td,te->de", attended, dbranch, preferred_element_type=jnp.float32)
    datt = jnp.einsum("te,de->td", dbranch, out_weight, preferred_element_type=jnp.float32).astype(
        jnp.bfloat16
    )
    datt = datt.reshape(length, head_count, head_size)
    dkeys = jnp.zeros((length, head_count, head_size), jnp.float32)
    dvalues = jnp.zeros((length, head_count, head_size), jnp.float32)
    table_part = jnp.zeros((bucket_count, head_count), jnp.float32)
    dquery_parts = []
    for number, offset in enumerate(range(0, length, query_rows)):
        query_block = queries[offset : offset + query_rows]
        onehot = bucket_onehot(offset)
        probs = jnp.exp(block_scores(offset, onehot) - log_totals[number])
        weights = probs.astype(jnp.bfloat16)
        dout_block = datt[offset : offset + query_rows]
        dvalues = dvalues + jnp.einsum(
            "hqk,qhd->khd", weights, dout_block, preferred_element_type=jnp.float32
        )
        dprob = jnp.einsum(
            "qhd,khd->hqk", dout_block, values_all, preferred_element_type=jnp.float32
        )
        inner_sum = jnp.sum(probs * dprob, axis=-1, keepdims=True)
        dscores = (probs * (dprob - inner_sum)).astype(jnp.bfloat16)
        dquery_parts.append(
            jnp.einsum("hqk,khd->qhd", dscores, keys_all, preferred_element_type=jnp.float32)
            * score_scale
        )
        dkeys = (
            dkeys
            + jnp.einsum("hqk,qhd->khd", dscores, query_block, preferred_element_type=jnp.float32)
            * score_scale
        )
        table_part = table_part + jnp.einsum(
            "hqk,cqk->ch", dscores, onehot, preferred_element_type=jnp.float32
        )
    dqueries = jnp.concatenate(dquery_parts, axis=0)
    dqkv = jnp.concatenate(
        [
            dqueries.reshape(length, features),
            dkeys.reshape(length, features),
            dvalues.reshape(length, features),
        ],
        axis=1,
    ).astype(jnp.bfloat16)
    grad_proj = jnp.einsum("td,te->de", normed_in, dqkv, preferred_element_type=jnp.float32)
    dnormed = jnp.einsum("te,de->td", dqkv, qkv_weight, preferred_element_type=jnp.float32)
    norm_one, back_one = jax.vjp(norm_rows, inputs, gain_rows[0])
    dinput_norm, dgain_one = back_one(dnormed)
    grad_tokens = dres + dinput_norm
    grad_gain = jnp.stack([dgain_one, dgain_two], axis=0)
    grad_table = lax.psum(table_part, ("group", "expert"))
    expert_grads = (
        lax.psum_scatter(
            grad_first.astype(jnp.bfloat16), "group", scatter_dimension=2, tiled=True
        ).astype(jnp.float32),
        lax.psum_scatter(
            grad_second.astype(jnp.bfloat16), "group", scatter_dimension=1, tiled=True
        ).astype(jnp.float32),
    )
    partial_value = (
        lax.psum_scatter(grad_gain, "expert", scatter_dimension=1, tiled=True),
        lax.psum_scatter(grad_proj, "expert", scatter_dimension=0, tiled=True),
        lax.psum_scatter(grad_out, "expert", scatter_dimension=0, tiled=True),
        lax.psum_scatter(grad_router, "expert", scatter_dimension=0, tiled=True),
    )
    dense = (
        lax.psum_scatter(
            partial_value[0].astype(jnp.bfloat16), "group", scatter_dimension=0, tiled=True
        ).astype(jnp.float32),
        lax.psum_scatter(
            partial_value[1].astype(jnp.bfloat16), "group", scatter_dimension=1, tiled=True
        ).astype(jnp.float32),
        lax.psum_scatter(
            partial_value[2].astype(jnp.bfloat16), "group", scatter_dimension=1, tiled=True
        ).astype(jnp.float32),
        lax.psum_scatter(
            partial_value[3].astype(jnp.bfloat16), "group", scatter_dimension=1, tiled=True
        ).astype(jnp.float32),
    )
    return (
        output,
        grad_tokens,
        dense[0],
        dense[1],
        dense[2],
        grad_table,
        dense[3],
        expert_grads[0],
        expert_grads[1],
    )


def solution(mesh):
    return jax.shard_map(
        per_device,
        mesh=mesh,
        in_specs=(
            P(("group", "expert"), None),
            P(),
            P(),
            P(),
            P(),
            P(),
            P("expert", None, None),
            P("expert", None, None),
            P(("group", "expert"), None),
            P(("group", "expert")),
            P(("group", "expert"), None),
        ),
        out_specs=(
            P(("group", "expert"), None),
            P(("group", "expert"), None),
            P("group", "expert"),
            P("expert", "group"),
            P("expert", "group"),
            P(),
            P("expert", "group"),
            P("expert", None, "group"),
            P("expert", "group", None),
        ),
        check_vma=False,
    )
```

profile of v0, /device:TPU:0, one launch (start us, length us, event | category | flops | bytes accessed | tf_op | source)
XLA Modules:
  0.0 1235.8 jit_solution(12772221112867697548)
XLA Ops:
  10.4 4.3 convolution_convert_fusion
  19.6 3.4 fusion.77
  23.0 2.6 copy.54
  30.2 2.6 copy.52
  32.9 15.6 %fusion.3 = f32[512,1024,12]{0,2,1:T(8,128)} fusion(s32[512,1024]{0,1:T(8,128)} %fusion.76, bf16[32,12]{0,1:T(8,128)(2,1)S(1)} %copy-done.52), kind=kOutput, calls=%fused_computation.10 | convolution fusion | flops 419430400 | bytes 27263744 | tf_op jit(solution)/shard_map/cqk,ch->hqk/dot_general | solution.py:67
  48.5 30.4 %copy.55 = f32[512,1024,12]{1,0,2:T(8,128)} copy(f32[512,1024,12]{0,2,1:T(8,128)} %fusion.3) | data formatting | bytes 50331648 | tf_op jit(solution)/shard_map/cqk,ch->hqk/dot_general | solution.py:67
  78.9 15.6 %fusion.1 = f32[512,1024,12]{0,2,1:T(8,128)} fusion(s32[512,1024]{0,1:T(8,128)} %fusion.77, bf16[32,12]{0,1:T(8,128)(2,1)S(1)} %copy-done.52), kind=kOutput, calls=%fused_computation.7 | convolution fusion | flops 419430400 | bytes 27263744 | tf_op jit(solution)/shard_map/cqk,ch->hqk/dot_general | solution.py:67
  94.4 30.3 %copy.57 = f32[512,1024,12]{1,0,2:T(8,128)} copy(f32[512,1024,12]{0,2,1:T(8,128)} %fusion.1) | data formatting | bytes 50331648 | tf_op jit(solution)/shard_map/cqk,ch->hqk/dot_general | solution.py:67
  124.8 18.0 %fusion.142 = (f32[12,512]{1,0:T(8,128)}, f32[12,512,1024]{2,1,0:T(8,128)}) fusion(f32[512,1024,12]{1,0,2:T(8,128)} %copy.55, bf16[512,12,64]{0,2,1:T(8,128)(2,1)} %bitcast.195, bf16[1024,12,64]{0,2,1:T(8,128)(2,1)} %bitcast.183), kind=kOutput, calls=%fused_computation.198 | convolution fusion | flops 824174592 | bytes 52715520 | tf_op jit(solution)/shard_map/qhd,khd->hqk/dot_general | solution.py:66
  142.8 11.1 fusion.19
  153.9 11.3 fusion.104
  165.2 17.7 %fusion.141 = (f32[12,512]{1,0:T(8,128)}, f32[12,512,1024]{2,1,0:T(8,128)}) fusion(f32[512,1024,12]{1,0,2:T(8,128)} %copy.57, bf16[512,12,64]{0,2,1:T(8,128)(2,1)} %bitcast.193, bf16[1024,12,64]{0,2,1:T(8,128)(2,1)} %bitcast.184), kind=kOutput, calls=%fused_computation.197 | convolution fusion | flops 824174592 | bytes 52715520 | tf_op jit(solution)/shard_map/qhd,khd->hqk/dot_general | solution.py:66
  182.9 11.1 fusion.20
  194.0 10.5 fusion.105
  213.4 5.4 scatter_custom_fusion
  219.5 2.7 concatenate.18
  222.1 11.7 gather_fusion
  233.8 79.9 %all_to_all.20 = bf16[16,128,768]{2,1,0:T(8,128)(2,1)S(1)} all-to-all(bf16[16,128,768]{2,1,0:T(8,128)(2,1)} %bitcast.192), channel_id=1, replica_groups=mesh['group'=2,'expert'=16] {'expert'}, dimensions={0} | all-to-all | bytes 6291456 | tf_op jit(solution)/shard_map/all_to_all | solution.py:113
  315.4 15.7 %fusion.46 = f32[16,128,3072]{2,1,0:T(8,128)} fusion(bf16[16,128,768]{2,1,0:T(8,128)(2,1)S(1)} %all_to_all.20, bf16[1,768,3072]{2,1,0:T(8,128)(2,1)} %param.17), kind=kOutput, calls=%fused_computation.80 | convolution fusion | flops 9663676416 | bytes 33030144 | tf_op jit(solution)/shard_map/njcd,jdf->njcf/dot_general | solution.py:116
  331.0 20.4 %fusion.66 = bf16[16,128,768]{2,1,0:T(8,128)(2,1)} fusion(bf16[1,3072,768]{2,1,0:T(8,128)(2,1)S(1)} %bitcast.223, f32[16,128,3072]{2,1,0:T(8,128)} %fusion.46), kind=kOutput, calls=%fused_computation.104 | convolution fusion | flops 9721872384 | bytes 33030144 | tf_op jit(solution)/shard_map/njcf,jfd->njcd/dot_general | solution.py:118
  351.4 4.7 all-to-all-start.1
  358.6 57.5 %all-to-all-done.1 = bf16[16,128,768]{2,1,0:T(8,128)(2,1)} async-done(((bf16[16,128,768]{2,1,0:T(8,128)(2,1)}), bf16[16,128,768]{2,1,0:T(8,128)(2,1)}, u32[]{:S(2)}, u32[]{:S(2)}) %all-to-all-start.1) | async-done | bytes 3145760 | tf_op jit(solution)/shard_map/all_to_all | solution.py:121
  416.2 8.1 gather_fusion.1
  424.3 3.7 fusion.61
  429.2 11.7 gather_fusion.2
  440.9 85.0 %all_to_all.21 = bf16[16,128,768]{2,1,0:T(8,128)(2,1)S(1)} all-to-all(bf16[16,128,768]{2,1,0:T(8,128)(2,1)} %bitcast.191), channel_id=1, replica_groups=mesh['group'=2,'expert'=16] {'expert'}, dimensions={0} | all-to-all | bytes 6291456 | tf_op jit(solution)/shard_map/all_to_all | solution.py:139
  525.9 29.2 %fusion.14 = bf16[16,1,128,3072]{3,2,0,1:T(8,128)(2,1)} fusion(f32[16,128,3072]{2,1,0:T(8,128)} %fusion.46, bf16[16,128,768]{2,1,0:T(8,128)(2,1)S(1)} %all_to_all.21, bf16[1,3072,768]{2,1,0:T(8,128)(2,1)} %param.18), kind=kOutput, calls=%fused_computation.23 | convolution fusion | flops 9789505536 | bytes 45613056 | tf_op jit(solution)/shard_map/njcd,jfd->njcf/dot_general | solution.py:147
  555.2 14.1 %fusion.71 = bf16[16,128,768]{2,1,0:T(8,128)(2,1)} fusion(bf16[1,768,3072]{2,1,0:T(8,128)(2,1)S(1)} %bitcast.225, bf16[16,1,128,3072]{3,2,0,1:T(8,128)(2,1)} %fusion.14), kind=kOutput, calls=%fused_computation.105 | convolution fusion | flops 9665249280 | bytes 20447232 | tf_op jit(solution)/shard_map/njcf,jdf->njcd/dot_general | solution.py:153
  569.3 4.8 all-to-all-start.3
  578.2 2.9 fusion.137
  581.2 54.0 %all-to-all-done.3 = bf16[16,128,768]{2,1,0:T(8,128)(2,1)} async-done(((bf16[16,128,768]{2,1,0:T(8,128)(2,1)}), bf16[16,128,768]{2,1,0:T(8,128)(2,1)}, u32[]{:S(2)}, u32[]{:S(2)}) %all-to-all-start.3) | async-done | bytes 3145760 | tf_op jit(solution)/shard_map/all_to_all | solution.py:156
  635.2 8.1 gather_fusion.3
  643.4 4.5 multiply_reduce_fusion.2
  648.0 2.3 convert_add_fusion.1
  653.2 17.2 %multiply_reduce_fusion.1 = (f32[12,512]{1,0:T(8,128)}, f32[12,512,1024]{2,1,0:T(8,128)}) fusion(f32[12,512,1024]{2,1,0:T(8,128)} %get-tuple-element.35, f32[12,512]{1,0:T(8,128)} %log_add_fusion.1, bf16[512,12,64]{0,2,1:T(8,128)(2,1)} %bitcast.197, bf16[1024,12,64]{0,2,1:T(8,128)(2,1)} %bitcast.187), kind=kOutput, calls=%fused_computation.37 | convolution fusion | flops 824174592 | bytes 52740096 | tf_op jit(solution)/shard_map/qhd,khd->hqk/dot_general | solution.py:191
  670.5 21.8 %multiply_convert_fusion.1 = bf16[12,512,1024]{2,1,0:T(8,128)(2,1)} fusion(f32[12,512,1024]{2,1,0:T(8,128)} %get-tuple-element.42, f32[12,512,1024]{2,1,0:T(8,128)} %get-tuple-element.35, f32[12,512]{1,0:T(8,128)} %get-tuple-element.41, f32[12,512]{1,0:T(8,128)} %log_add_fusion.1), kind=kLoop, calls=%fused_computation.36 | loop fusion | flops 25165824 | bytes 62963712 | tf_op jit(solution)/shard_map/convert_element_type | solution.py:195
  692.3 9.4 fusion.102
  701.7 17.6 %multiply_reduce_fusion = (f32[12,512]{1,0:T(8,128)}, f32[12,512,1024]{2,1,0:T(8,128)}) fusion(f32[12,512,1024]{2,1,0:T(8,128)} %get-tuple-element.33, f32[12,512]{1,0:T(8,128)} %log_add_fusion, bf16[512,12,64]{0,2,1:T(8,128)(2,1)} %bitcast.199, bf16[1024,12,64]{0,2,1:T(8,128)(2,1)} %bitcast.188), kind=kOutput, calls=%fused_computation.34 | convolution fusion | flops 824174592 | bytes 52740096 | tf_op jit(solution)/shard_map/qhd,khd->hqk/dot_general | solution.py:191
  719.3 21.7 %multiply_convert_fusion = bf16[12,512,1024]{2,1,0:T(8,128)(2,1)} fusion(f32[12,512,1024]{2,1,0:T(8,128)} %get-tuple-element.44, f32[12,512,1024]{2,1,0:T(8,128)} %get-tuple-element.33, f32[12,512]{1,0:T(8,128)} %get-tuple-element.43, f32[12,512]{1,0:T(8,128)} %log_add_fusion), kind=kLoop, calls=%fused_computation.33 | loop fusion | flops 25165824 | bytes 62963712 | tf_op jit(solution)/shard_map/convert_element_type | solution.py:195
  741.0 9.6 fusion.103
  750.6 2.8 fusion.111
  753.5 7.2 fusion.144
  761.9 7.5 multiply_convert_fusion.2
  769.5 11.2 fusion.23
  780.7 10.9 add_convert_fusion
  792.8 7.0 fusion.96
  800.4 8.2 fusion.60
  809.7 15.6 %fusion.48 = bf16[1,768,3072]{2,1,0:T(8,128)(2,1)} fusion(bf16[16,128,768]{2,1,0:T(8,128)(2,1)} %copy-done.22, bf16[16,1,128,3072]{3,2,0,1:T(8,128)(2,1)} %fusion.14), kind=kOutput, calls=%fused_computation.82 | convolution fusion | flops 9666035712 | bytes 20447232 | tf_op jit(solution)/shard_map/njcd,njcf->jdf/dot_general | solution.py:152
  825.4 20.8 %fusion.51 = bf16[1,3072,768]{2,1,0:T(8,128)(2,1)} fusion(bf16[16,128,768]{2,1,0:T(8,128)(2,1)} %copy-done.23, f32[16,128,3072]{2,1,0:T(8,128)} %fusion.46), kind=kOutput, calls=%fused_computation.83 | convolution fusion | flops 9722658816 | bytes 33030144 | tf_op jit(solution)/shard_map/njcf,njcd->jfd/dot_general | solution.py:149
  849.5 23.4 %copy.58 = bf16[12,512,1024]{1,0,2:T(8,128)(2,1)} copy(bf16[12,512,1024]{2,1,0:T(8,128)(2,1)} %multiply_convert_fusion.1) | data formatting | bytes 25165824 | tf_op jit(solution)/shard_map/convert_element_type | solution.py:195
  872.9 23.0 %copy.59 = bf16[12,512,1024]{1,0,2:T(8,128)(2,1)} copy(bf16[12,512,1024]{2,1,0:T(8,128)(2,1)} %multiply_convert_fusion) | data formatting | bytes 25165824 | tf_op jit(solution)/shard_map/convert_element_type | solution.py:195
  896.0 13.1 %fusion.108 = f32[32,12]{0,1:T(8,128)S(1)} fusion(bf16[12,512,1024]{1,0,2:T(8,128)(2,1)} %copy.58, s32[512,1024]{0,1:T(8,128)} %fusion.76), kind=kOutput, calls=%fused_computation.143 | convolution fusion | flops 419430400 | bytes 14681600 | tf_op jit(solution)/shard_map/hqk,cqk->ch/dot_general | solution.py:205
  909.1 14.0 %fusion.110 = f32[32,12]{0,1:T(8,128)} fusion(f32[32,12]{0,1:T(8,128)S(1)} %fusion.108, bf16[12,512,1024]{1,0,2:T(8,128)(2,1)} %copy.59, s32[512,1024]{0,1:T(8,128)S(1)} %copy-done.11), kind=kOutput, calls=%fused_computation.145 | convolution fusion | flops 419430784 | bytes 14683136 | tf_op jit(solution)/shard_map/hqk,cqk->ch/dot_general | solution.py:205
  927.1 119.9 %reduce-scatter.17.cloned.1.call-done = f32[48,2304]{1,0:T(8,128)} async-done(((f32[768,2304]{1,0:T(8,128)}), f32[48,2304]{1,0:T(8,128)}) %reduce-scatter.17.cloned.1.call-update) | async-done | bytes 442384 | tf_op jit(solution)/shard_map/reduce_scatter | solution.py:234
  1050.8 5.8 fusion.63
  1056.6 39.6 %psum.7 = f32[32,12]{0,1:T(8,128)} all-reduce(f32[32,12]{0,1:T(8,128)} %fusion.110), channel_id=1, replica_groups=mesh['group'=2,'expert'=16] {'group','expert'}, use_global_device_ids=true, to_apply=%region_24.25 | all-reduce | flops 384 | bytes 3072 | tf_op jit(solution)/shard_map/psum | solution.py:223
  1096.2 75.8 %reduce-scatter.25.cloned.1.call-done = f32[48,2]{1,0:T(8,128)} async-done(((f32[768,2]{1,0:T(8,128)}), f32[48,2]{1,0:T(8,128)}) %reduce-scatter.25.cloned.1.call-update) | async-done | bytes 400
  1172.8 2.5 all-reduce.4
  1177.0 9.6 reduce-scatter.21.cloned.1.call-done
  1186.6 4.5 convert_element_type.368
  1191.1 11.5 reduce-scatter.23.cloned.1.call-done
  1202.6 4.2 convert_element_type.371
  1206.8 6.9 reduce-scatter.29.cloned.1.call-done
  1216.6 8.6 reduce-scatter.27.cloned.1.call-done
  (213 shorter events, 57.5 us)
Async XLA Ops:
  7.2 3.3 copy-start
  7.2 1.9 copy-start.16
  7.2 2.3 copy-start.63
  9.5 5.2 copy-start.56
  10.1 4.6 copy-start.53
  16.0 2.5 copy-start.41
  25.6 7.3 copy-start.52
  142.8 11.1 copy-start.6
  142.8 11.1 copy-start.32
  153.9 11.3 copy-start.34
  182.9 11.1 copy-start.7
  182.9 11.1 copy-start.33
  194.0 10.5 copy-start.35
  194.0 10.5 copy-start.29
  204.5 2.0 copy-start.17
  204.6 2.3 copy-start.64
  204.8 3.8 copy-start.26
  206.9 2.3 copy-start.37
  210.9 2.5 copy-start.43
  210.9 2.4 copy-start.45
  233.8 97.2 %slice-start = ((s8[4718592]{0:T(1024)(128)(4,1)}), s8[4194304]{0:T(1024)(128)(4,1)S(1)}, s32[]{:S(2)}) async-start(s8[4718592]{0:T(1024)(128)(4,1)} %bitcast.222), calls=%async_computation.20 | async-start | bytes 8388608
  315.4 15.7 %slice-start.1 = ((s8[4718592]{0:T(1024)(128)(4,1)}), s8[524288]{0:T(1024)(128)(4,1)S(1)}, s32[]{:S(2)}) async-start(s8[4718592]{0:T(1024)(128)(4,1)} %bitcast.222), calls=%async_computation.21 | async-start | bytes 1048576
  351.4 64.8 %all-to-all-start.1 = ((bf16[16,128,768]{2,1,0:T(8,128)(2,1)}), bf16[16,128,768]{2,1,0:T(8,128)(2,1)}, u32[]{:S(2)}, u32[]{:S(2)}) async-start(bf16[16,128,768]{2,1,0:T(8,128)(2,1)} %fusion.66), calls=%async_computation.1 | async-start | bytes 6291456 | tf_op jit(solution)/shard_map/all_to_all | solution.py:121
  440.9 114.3 %slice-start.2 = ((s8[4718592]{0:T(1024)(128)(4,1)}), s8[4194304]{0:T(1024)(128)(4,1)S(1)}, s32[]{:S(2)}) async-start(s8[4718592]{0:T(1024)(128)(4,1)} %bitcast.224), calls=%async_computation.22 | async-start | bytes 8388608
  525.9 29.3 %copy-start.23 = (bf16[16,128,768]{2,1,0:T(8,128)(2,1)}, bf16[16,128,768]{2,1,0:T(8,128)(2,1)S(1)}, u32[]{:S(2)}) copy-start(bf16[16,128,768]{2,1,0:T(8,128)(2,1)S(1)} %all_to_all.21) | copy-start | bytes 9437188
  525.9 29.3 %slice-start.3 = ((s8[4718592]{0:T(1024)(128)(4,1)}), s8[524288]{0:T(1024)(128)(4,1)S(1)}, s32[]{:S(2)}) async-start(s8[4718592]{0:T(1024)(128)(4,1)} %bitcast.224), calls=%async_computation.23 | async-start | bytes 1048576
  569.2 7.7 copy-start.46
  569.2 9.0 copy-start.44
  569.3 65.9 %all-to-all-start.3 = ((bf16[16,128,768]{2,1,0:T(8,128)(2,1)}), bf16[16,128,768]{2,1,0:T(8,128)(2,1)}, u32[]{:S(2)}, u32[]{:S(2)}) async-start(bf16[16,128,768]{2,1,0:T(8,128)(2,1)} %fusion.71), calls=%async_computation.3 | async-start | bytes 6291456 | tf_op jit(solution)/shard_map/all_to_all | solution.py:156
  574.1 274.0 %reduce-scatter.31.cloned.1.call-start = ((), (), s32[]{:S(2)}) async-start(), calls=%async_computation.19 | async-start | bytes 417792
  581.2 341.9 %reduce-scatter.19.cloned.1.call-start = ((), (), s32[]{:S(2)}) async-start(), calls=%async_computation.13 | async-start | bytes 2506752 | tf_op jit(solution)/shard_map/reduce_scatter | solution.py:235
  635.2 8.1 copy-start.38
  635.2 8.1 copy-start.40
  643.3 4.6 copy-start.59
  643.3 4.6 copy-start.4
  643.4 4.6 copy-start.8
  643.4 4.6 copy-start.15
  643.4 4.6 copy-start.47
  643.4 4.6 copy-start.48
  648.0 2.3 copy-start.65
  670.5 21.8 %copy-start.1 = (bf16[1024,768]{0,1:T(8,128)(2,1)S(1)}, bf16[1024,768]{0,1:T(8,128)(2,1)}, u32[]{:S(2)}) copy-start(bf16[1024,768]{0,1:T(8,128)(2,1)} %copy.54) | copy-start | bytes 4718596
  719.3 21.7 %copy-start.2 = (bf16[1024,768]{0,1:T(8,128)(2,1)S(1)}, bf16[1024,768]{0,1:T(8,128)(2,1)}, u32[]{:S(2)}) copy-start(bf16[1024,768]{0,1:T(8,128)(2,1)} %copy.54) | copy-start | bytes 4718596
  741.0 9.6 copy-start.10
  741.0 9.6 copy-start.27
  753.4 293.6 %reduce-scatter.17.cloned.1.call-start = ((), (), s32[]{:S(2)}) async-start(), calls=%async_computation.12 | async-start | bytes 7520256 | tf_op jit(solution)/shard_map/reduce_scatter | solution.py:234
  753.5 7.2 copy-start.20
  753.5 7.2 copy-start.21
  761.9 29.7 %copy-start.28 = (bf16[1024,12,64]{0,2,1:T(8,128)(2,1)}, bf16[1024,12,64]{0,2,1:T(8,128)(2,1)S(1)}, u32[]{:S(2)}) copy-start(bf16[1024,12,64]{0,2,1:T(8,128)(2,1)S(1)} %pad_maximum_fusion.4) | copy-start | bytes 4718596
  761.9 7.5 copy-start.14
  761.9 7.5 copy-start.31
  769.4 22.2 %copy-start.19 = (bf16[12,64,1024]{2,1,0:T(8,128)(2,1)}, bf16[12,64,1024]{2,1,0:T(8,128)(2,1)S(1)}, u32[]{:S(2)}) copy-start(bf16[12,64,1024]{2,1,0:T(8,128)(2,1)S(1)} %multiply_convert_fusion.2) | copy-start | bytes 4718596
  769.5 11.2 copy-start.13
  769.5 11.2 copy-start.30
  780.7 12.1 copy-start.18
  780.7 12.1 copy-start.54
  780.7 12.1 copy-start.57
  799.8 372.2 %reduce-scatter.25.cloned.1.call-start = ((), (), s32[]{:S(2)}) async-start(), calls=%async_computation.16 | async-start | bytes 417792
  809.7 376.9 %reduce-scatter.21.cloned.1.call-start = ((), (), s32[]{:S(2)}) async-start(), calls=%async_computation.14 | async-start | bytes 7077888 | tf_op jit(solution)/shard_map/reduce_scatter | solution.py:225
  825.4 377.2 %reduce-scatter.23.cloned.1.call-start = ((), (), s32[]{:S(2)}) async-start(), calls=%async_computation.15 | async-start | bytes 7077888 | tf_op jit(solution)/shard_map/reduce_scatter | solution.py:228
  846.2 367.4 %reduce-scatter.29.cloned.1.call-start = ((), (), s32[]{:S(2)}) async-start(), calls=%async_computation.18 | async-start | bytes 294912
  896.0 13.1 %copy-start.11 = (s32[512,1024]{0,1:T(8,128)S(1)}, s32[512,1024]{0,1:T(8,128)}, u32[]{:S(2)}) copy-start(s32[512,1024]{0,1:T(8,128)} %fusion.77) | copy-start | bytes 6291460
  909.0 17.4 %copy-start.51 = (f32[1024]{0:T(1024)S(1)}, f32[1024]{0:T(1024)}, u32[]{:S(2)}) copy-start(f32[1024]{0:T(1024)} %copy-done.50) | copy-start | bytes 12292
  926.4 298.8 %reduce-scatter.27.cloned.1.call-start = ((), (), s32[]{:S(2)}) async-start(), calls=%async_computation.17 | async-start | bytes 884736
  1050.8 122.0 %copy-start.60 = (bf16[48,16]{0,1:T(8,128)(2,1)S(1)}, bf16[48,16]{0,1:T(8,128)(2,1)}, u32[]{:S(2)}) copy-start(bf16[48,16]{0,1:T(8,128)(2,1)} %copy.71) | copy-start | bytes 4612
  (17 other events, 19.6 us)
Sparse Core Ops, SparseCore 0:
  581.3 139.7 reduce-scatter.30
  753.6 137.6 reduce-scatter.18
  896.6 150.4 reduce-scatter.16
  1051.6 120.3 reduce-scatter.24
  1174.8 11.7 reduce-scatter.20
  1188.7 13.7 reduce-scatter.22
  1204.9 8.7 reduce-scatter.28
  1216.0 9.1 reduce-scatter.26
where the time goes:
time: 1250 us; the launch traced here: 1240 us
  matrix products  357 us (29%)
  waiting for transfers between devices  344 us (28%)
  blocking collectives  207 us (17%)
  local copies, waits for them, and re-layouts  192 us (15%)
  other arithmetic  110 us (9%)
  between operations  16.6 us (1%)
    reduce_scatter x1, waiting for transfers between devices, per_device(): lax.psum_scatter(grad_proj, 'expert', scatter_dimension=0, tiled=True)  120 us
    unnamed x12, waiting for transfers between devices  91.4 us
    all_to_all x1, blocking collectives, per_device(): lax.all_to_all(dexp_send, 'expert', split_axis=0, concat_axis=0, tiled=True)  85 us
    all_to_all x1, blocking collectives, per_device(): lax.all_to_all(outgoing, 'expert', split_axis=0, concat_axis=0, tiled=True)  79.9 us
    dot_general x2, local copies, waits for them, and re-layouts, block_scores(): jnp.einsum('cqk,ch->hqk', onehot, rel_bias, preferred_element_type=jnp.fl...  60.8 us
    all_to_all x1, waiting for transfers between devices, per_device(): lax.all_to_all(produced.reshape(-1, item_count, features), 'expert', spli...  57.5 us
    all_to_all x1, waiting for transfers between devices, per_device(): lax.all_to_all(dmoved.reshape(-1, slot_count, features), 'expert', split_...  54 us
    convert_element_type x2, local copies, waits for them, and re-layouts, per_device(): dscores = (probs * (dprob - inner_sum)).astype(jnp.bfloat16)  46.4 us
  transfers between devices with their start and end apart: 10, of which 8 were waited for; matrix products, arithmetic and copies ran while one was open for 26% of the time, Pallas kernels for 0%

commit v1 on v0

v1 whole, which is shorter than its diff:
```python
import functools

import jax
import jax.numpy as jnp
from jax import lax
from jax.experimental import pallas as pl
from jax.experimental.pallas import tpu as pltpu
from jax.sharding import PartitionSpec as P

EPSILON = 1e-06
BOUNDARIES = (12, 16, 23, 32, 46, 64, 91)
F32 = jnp.float32
BF16 = jnp.bfloat16
LANES = 128
HEAD = 64
NT = (((1,), (1,)), ((), ()))
TN = (((0,), (0,)), ((), ()))
MIB = 2**20


def bucket_index(relative):
    distance = jnp.abs(relative)
    farther = jnp.full(relative.shape, 8, jnp.int32)
    for boundary in BOUNDARIES:
        farther = farther + (distance >= boundary).astype(jnp.int32)
    nearest = jnp.where(distance < 8, distance, farther)
    return nearest + 16 * (relative > 0).astype(jnp.int32)


def norm_rows(values, gain_row):
    return (
        values * lax.rsqrt(jnp.mean(values * values, axis=-1, keepdims=True) + EPSILON) * gain_row
    )


def attend_kernel(q_ref, k_ref, v_ref, line_ref, out_ref, kept_ref, slab_ref, *, rows):
    length = q_ref.shape[0]
    lane = lax.broadcasted_iota(jnp.int32, (1, LANES), 1)
    keys, values = k_ref[...], v_ref[...]
    for head in range(2):
        line = jnp.broadcast_to(line_ref[head], (rows, 2 * length))
        slab_ref[head] = pltpu.roll(line, 0, 1, stride=1, stride_axis=0)
    for step in range(length // rows):
        block = pl.ds(step * rows, rows)
        queries = q_ref[block, :].astype(F32) * HEAD**-0.5
        joined = []
        for head in range(2):
            mine = (lane < HEAD) if head == 0 else (lane >= HEAD)
            own = jnp.where(mine, queries, 0.0).astype(BF16)
            scores = lax.dot_general(own, keys, NT, preferred_element_type=F32)
            scores = scores + slab_ref[head, :, pl.ds(length - rows * step, length)]
            top = jnp.max(scores, axis=1, keepdims=True)
            raised = jnp.exp(scores - top)
            total = jnp.sum(raised, axis=1, keepdims=True)
            weights = (raised * (1.0 / total)).astype(BF16)
            kept_ref[head, block, :] = weights
            joined.append(jnp.dot(weights, values, preferred_element_type=F32))
        out_ref[block, :] = jnp.where(lane < HEAD, joined[0], joined[1]).astype(BF16)


def attend(projected, lines, rows):
    length, features = projected.shape[0], projected.shape[1] // 3
    heads = lines.shape[0]
    pairs = heads // 2
    return pl.pallas_call(
        functools.partial(attend_kernel, rows=rows),
        grid=(pairs,),
        in_specs=[
            pl.BlockSpec((length, LANES), lambda i: (0, i)),
            pl.BlockSpec((length, LANES), lambda i: (0, pairs + i)),
            pl.BlockSpec((length, LANES), lambda i: (0, 2 * pairs + i)),
            pl.BlockSpec((2, 1, 2 * length), lambda i: (i, 0, 0)),
        ],
        out_specs=[
            pl.BlockSpec((length, LANES), lambda i: (0, i)),
            pl.BlockSpec((2, length, length), lambda i: (i, 0, 0)),
        ],
        out_shape=[
            jax.ShapeDtypeStruct((length, features), BF16),
            jax.ShapeDtypeStruct((heads, length, length), BF16),
        ],
        scratch_shapes=[pltpu.VMEM((2, rows, 2 * length), F32)],
        compiler_params=pltpu.CompilerParams(vmem_limit_bytes=50 * MIB),
        cost_estimate=pl.CostEstimate(
            flops=16 * heads * length * length * HEAD,
            bytes_accessed=2 * heads * length * length + 8 * length * features,
            transcendentals=heads * length * length,
        ),
    )(projected, projected, projected, lines)


def attend_back_kernel(
    q_ref, k_ref, v_ref, out_ref, dout_ref, kept_ref, tile_ref,
    grad_ref, band_ref, far_ref, dscores_ref, *, rows,
):
    length = q_ref.shape[0]
    tiles = length // LANES
    inner = rows // LANES
    lane = lax.broadcasted_iota(jnp.int32, (1, LANES), 1)
    queries, values, dout = q_ref[...], v_ref[...], dout_ref[...]
    widened = jnp.concatenate([k_ref[...], tile_ref[...]], axis=1)
    dout_wide = dout.astype(F32)
    product = dout_wide * out_ref[...].astype(F32)
    dout_turned, queries_turned = dout.T, queries.T
    dqueries = [[], []]
    dkeys, dvalues = [], []
    for head in range(2):
        mine = (lane < HEAD) if head == 0 else (lane >= HEAD)
        inner_sum = jnp.sum(jnp.where(mine, product, 0.0), axis=1, keepdims=True)
        own = jnp.where(mine, dout_wide, 0.0).astype(BF16)
        band_ref[head] = jnp.zeros_like(band_ref[head])
        for step in range(length // rows):
            first = step * rows
            block = pl.ds(first, rows)
            dprob = lax.dot_general(
                own[first : first + rows], values, NT, preferred_element_type=F32
            )
            dscores = kept_ref[head, block, :].astype(F32) * (
                dprob - inner_sum[first : first + rows]
            )
            rounded = dscores.astype(BF16)
            dscores_ref[block, :] = rounded
            for part in range(inner):
                tile = step * inner + part
                low, high = max(tile - 1, 0), min(tile + 2, tiles)
                at = low - (tile - 1)
                band_ref[head, :, at * LANES : (at + high - low) * LANES] += dscores[
                    part * LANES : (part + 1) * LANES, low * LANES : high * LANES
                ]
            both = jnp.dot(rounded, widened, preferred_element_type=F32)
            dqueries[head].append(both[:, :LANES])
            for part in range(inner):
                far_ref[head, step * inner + part] = jnp.sum(
                    both[part * LANES : (part + 1) * LANES, LANES:], axis=0
                )
        half = slice(HEAD * head, HEAD * head + HEAD)
        dkeys.append(jnp.dot(queries_turned[half], dscores_ref[...], preferred_element_type=F32))
        dvalues.append(jnp.dot(dout_turned[half], kept_ref[head], preferred_element_type=F32))
    scale = HEAD**-0.5
    for step in range(length // rows):
        grad_ref[0, pl.ds(step * rows, rows), :] = (
            jnp.where(lane < HEAD, dqueries[0][step], dqueries[1][step]) * scale
        ).astype(BF16)
    grad_ref[1] = (jnp.concatenate(dkeys, axis=0) * scale).T.astype(BF16)
    grad_ref[2] = jnp.concatenate(dvalues, axis=0).T.astype(BF16)


def attend_back(projected, attended, datt, kept, rows):
    length, features = projected.shape[0], projected.shape[1] // 3
    heads = kept.shape[0]
    pairs = heads // 2
    tiles = length // LANES
    tile_of = (
        jnp.arange(length)[:, None] // LANES == jnp.arange(LANES)[None, :]
    ).astype(BF16)
    return pl.pallas_call(
        functools.partial(attend_back_kernel, rows=rows),
        grid=(pairs,),
        in_specs=[
            pl.BlockSpec((length, LANES), lambda i: (0, i)),
            pl.BlockSpec((length, LANES), lambda i: (0, pairs + i)),
            pl.BlockSpec((length, LANES), lambda i: (0, 2 * pairs + i)),
            pl.BlockSpec((length, LANES), lambda i: (0, i)),
            pl.BlockSpec((length, LANES), lambda i: (0, i)),
            pl.BlockSpec((2, length, length), lambda i: (i, 0, 0)),
            pl.BlockSpec((length, LANES), lambda i: (0, 0)),
        ],
        out_specs=[
            pl.BlockSpec((3, length, LANES), lambda i: (0, 0, i)),
            pl.BlockSpec((2, LANES, 3 * LANES), lambda i: (i, 0, 0)),
            pl.BlockSpec((2, tiles, LANES), lambda i: (i, 0, 0)),
        ],
        out_shape=[
            jax.ShapeDtypeStruct((3, length, features), BF16),
            jax.ShapeDtypeStruct((heads, LANES, 3 * LANES), F32),
            jax.ShapeDtypeStruct((heads, tiles, LANES), F32),
        ],
        scratch_shapes=[pltpu.VMEM((length, length), BF16)],
        compiler_params=pltpu.CompilerParams(vmem_limit_bytes=56 * MIB),
        cost_estimate=pl.CostEstimate(
            flops=32 * heads * length * length * HEAD,
            bytes_accessed=2 * heads * length * length + 18 * length * features,
            transcendentals=0,
        ),
    )(projected, projected, projected, attended, datt, kept, tile_of)


def bias_lines(rel_bias, length):
    relative = jnp.arange(2 * length, dtype=jnp.int32) - length
    onehot = (
        bucket_index(relative)[None, :]
        == jnp.arange(rel_bias.shape[0], dtype=jnp.int32)[:, None]
    ).astype(F32)
    return jnp.einsum(
        "ch,cr->hr", rel_bias.astype(F32), onehot, precision=lax.Precision.HIGHEST
    )[:, None, :]


def table_gradient(band, far, bucket_count):
    heads, tiles = far.shape[0], far.shape[1]
    relative = jnp.arange(3 * LANES)[None, :] - LANES - jnp.arange(LANES)[:, None]
    onehot = (bucket_index(relative)[:, :, None] == jnp.arange(bucket_count)).astype(F32)
    near = jnp.dot(
        band.reshape(heads, -1),
        onehot.reshape(-1, bucket_count),
        precision=lax.Precision.HIGHEST,
    )
    here = jnp.arange(tiles)[:, None]
    there = jnp.arange(LANES)[None, :]
    before = jnp.sum(jnp.where(there <= here - 2, far, 0.0), axis=(1, 2))
    after = jnp.sum(jnp.where(there >= here + 2, far, 0.0), axis=(1, 2))
    buckets = jnp.arange(bucket_count)
    last = bucket_index(jnp.array([-length_far(), length_far()], jnp.int32))
    return (
        near
        + before[:, None] * (buckets == last[0])
        + after[:, None] * (buckets == last[1])
    ).T


def length_far():
    return LANES


def expert_kernel(
    x_ref, c_ref, w_in_ref, w_out_ref, router_ref, mine_ref,
    made_ref, dmoved_ref, act_ref, dpre_ref, dexp_ref, drouter_ref, *, width, expert_count,
):
    x, c = x_ref[...], c_ref[...]
    router_weight = router_ref[...]
    lane = lax.broadcasted_iota(jnp.int32, (1, router_weight.shape[1]), 1)
    logits = jnp.dot(x, router_weight, preferred_element_type=F32)
    logits = jnp.where(lane < expert_count, logits, -jnp.inf)
    raised = jnp.exp(logits - jnp.max(logits, axis=-1, keepdims=True))
    router = raised / jnp.sum(raised, axis=-1, keepdims=True)
    chosen = mine_ref[...]
    gate = jnp.sum(router * chosen, axis=-1, keepdims=True)
    upstream = c.astype(F32)
    dexp = (gate * upstream).astype(BF16)
    dexp_ref[...] = dexp
    hidden_width = w_in_ref.shape[1]
    made = jnp.zeros(x.shape, F32)
    dmoved = jnp.zeros(x.shape, F32)
    root = (2.0 / jnp.pi) ** 0.5
    for first in range(0, hidden_width, width):
        part = slice(first, first + width)
        pre = jnp.dot(x, w_in_ref[:, part], preferred_element_type=F32)
        square = pre * pre
        turned = jnp.tanh(pre * (root + (root * 0.044715) * square))
        half = 0.5 + 0.5 * turned
        act = (pre * half).astype(BF16)
        slope = half + pre * (half * (1.0 - turned)) * (root + (3 * root * 0.044715) * square)
        act_ref[:, part] = act
        made = made + jnp.dot(act, w_out_ref[part, :], preferred_element_type=F32)
        dact = lax.dot_general(dexp, w_out_ref[part, :], NT, preferred_element_type=F32)
        dpre = (dact * slope).astype(BF16)
        dpre_ref[:, part] = dpre
        dmoved = dmoved + lax.dot_general(
            dpre, w_in_ref[:, part], NT, preferred_element_type=F32
        )
    made = made.astype(BF16)
    made_ref[...] = made
    dgate = jnp.sum(upstream * made.astype(F32), axis=-1, keepdims=True)
    dlogits = (dgate * gate * (chosen - router)).astype(BF16)
    dmoved_ref[...] = (
        dmoved + lax.dot_general(dlogits, router_weight, NT, preferred_element_type=F32)
    ).astype(BF16)

    @pl.when(pl.program_id(0) == 0)
    def _():
        drouter_ref[...] = jnp.zeros_like(drouter_ref)

    drouter_ref[...] += lax.dot_general(x, dlogits, TN, preferred_element_type=F32)


def run_expert(x, c, w_in, w_out, router_padded, mine, expert_count):
    total, features = x.shape
    hidden_width = w_in.shape[1]
    rows = min(256, total)
    padded = router_padded.shape[1]
    row_block = pl.BlockSpec((rows, features), lambda i: (i, 0))
    wide_block = pl.BlockSpec((rows, hidden_width), lambda i: (i, 0))

    def whole(shape):
        return pl.BlockSpec(shape, lambda i: (0, 0))

    return pl.pallas_call(
        functools.partial(
            expert_kernel, width=min(1024, hidden_width), expert_count=expert_count
        ),
        grid=(total // rows,),
        in_specs=[
            row_block,
            row_block,
            whole(w_in.shape),
            whole(w_out.shape),
            whole(router_padded.shape),
            whole(mine.shape),
        ],
        out_specs=[
            row_block,
            row_block,
            wide_block,
            wide_block,
            row_block,
            whole((features, padded)),
        ],
        out_shape=[
            jax.ShapeDtypeStruct((total, features), BF16),
            jax.ShapeDtypeStruct((total, features), BF16),
            jax.ShapeDtypeStruct((total, hidden_width), BF16),
            jax.ShapeDtypeStruct((total, hidden_width), BF16),
            jax.ShapeDtypeStruct((total, features), BF16),
            jax.ShapeDtypeStruct((features, padded), F32),
        ],
        compiler_params=pltpu.CompilerParams(vmem_limit_bytes=56 * MIB),
        cost_estimate=pl.CostEstimate(
            flops=8 * total * features * hidden_width,
            bytes_accessed=4 * features * hidden_width + 4 * total * (hidden_width + features),
            transcendentals=total * hidden_width,
        ),
    )(x, c, w_in, w_out, router_padded, mine)


def core_sum(values, dim):
    half = values.shape[dim] // 2
    core = lax.axis_index("group")
    own = lax.dynamic_slice_in_dim(values, core * half, half, dim)
    other = lax.dynamic_slice_in_dim(values, (1 - core) * half, half, dim).astype(BF16)
    return own + lax.ppermute(other, "group", [(0, 1), (1, 0)]).astype(F32)


def exchange(values):
    return lax.all_to_all(values, "expert", split_axis=0, concat_axis=0, tiled=True)


def per_device(
    tokens, gains, qkv_weight, out_weight, rel_bias, router_weight, w_in, w_out, routes, factors,
    cotangent,
):
    length, features = tokens.shape
    bucket_count = rel_bias.shape[0]
    expert_count = router_weight.shape[1]
    slot_count = 2 * length // expert_count
    chunk = slot_count // 2
    rows = min(256, length)
    gain_rows = gains.astype(F32)
    w_in, w_out = w_in[0], w_out[0]
    me = lax.axis_index("expert")
    core = lax.axis_index("group")

    routed = routes[:, 0]
    row_index = jnp.arange(length, dtype=jnp.int32)
    chosen = routed[:, None] == jnp.arange(expert_count, dtype=jnp.int32)[None, :]
    earlier = (row_index[:, None] > row_index[None, :]).astype(BF16)
    before = jnp.dot(earlier, chosen.astype(BF16), preferred_element_type=F32)
    place = jnp.sum(before * chosen.astype(F32), axis=-1).astype(jnp.int32)
    capacity = factors[0] * (length // expert_count)
    placed = jnp.where(place < capacity, place, slot_count)
    slots = jnp.arange(expert_count * chunk, dtype=jnp.int32)
    picks = []
    for number in range(2):
        inside = (placed >= number * chunk) & (placed < (number + 1) * chunk)
        target = jnp.where(inside, routed * chunk + placed - number * chunk, -1)
        picks.append((slots[:, None] == target[None, :]).astype(BF16))

    def pack(values, number):
        return jnp.dot(picks[number], values, preferred_element_type=F32).astype(BF16)

    def unpack(parts):
        return sum(
            lax.dot_general(picks[n], parts[n], TN, preferred_element_type=F32) for n in range(2)
        )

    def send(values):
        return exchange(values.reshape(expert_count, chunk, features)).reshape(-1, features)

    upstream_there = [send(pack(cotangent, n)) for n in range(2)]

    inputs = tokens.astype(F32)
    normed_in = norm_rows(inputs, gain_rows[0]).astype(BF16)
    projected = jnp.dot(normed_in, qkv_weight, preferred_element_type=F32).astype(BF16)
    attended, kept = attend(projected, bias_lines(rel_bias, length), rows)
    residual_one = inputs + jnp.dot(attended, out_weight, preferred_element_type=F32)
    hidden = norm_rows(residual_one, gain_rows[1]).astype(BF16)

    logits = jnp.dot(hidden, router_weight, preferred_element_type=F32)
    raised = jnp.exp(logits - jnp.max(logits, axis=-1, keepdims=True))
    router = raised / jnp.sum(raised, axis=-1, keepdims=True)
    gate_value = jnp.sum(router * chosen.astype(F32), axis=-1)

    hidden_there = [send(pack(hidden, n)) for n in range(2)]
    padded = -expert_count % LANES
    router_padded = jnp.pad(router_weight, ((0, 0), (0, padded)))
    mine = (jnp.arange(expert_count + padded)[None, :] == me).astype(F32)
    results = [
        run_expert(
            hidden_there[n], upstream_there[n], w_in, w_out, router_padded, mine, expert_count
        )
        for n in range(2)
    ]
    made, dmoved, act, dpre, dexp, drouter = zip(*results, strict=True)
    dmoved_back = [send(dmoved[n]) for n in range(2)]
    made, _ = lax.optimization_barrier((made, dmoved_back))
    made_back = [send(made[n]) for n in range(2)]

    def joined(left, right):
        return sum(
            lax.dot_general(left[n], right[n], TN, preferred_element_type=F32) for n in range(2)
        )

    grad_first = core_sum(joined(hidden_there, dpre), 1)[None]
    grad_second = core_sum(joined(act, dexp), 0)[None]
    grad_router = (drouter[0] + drouter[1])[:, :expert_count]

    dhidden = unpack(dmoved_back)
    upstream = cotangent.astype(F32)
    _, back_two = jax.vjp(norm_rows, residual_one, gain_rows[1])
    dres_norm, dgain_two = back_two(dhidden)
    dres = upstream + dres_norm
    dbranch = dres.astype(BF16)
    datt = lax.dot_general(dbranch, out_weight, NT, preferred_element_type=F32).astype(BF16)
    grad_out = lax.dot_general(attended, dbranch, TN, preferred_element_type=F32)
    dqkv, band, far = attend_back(projected, attended, datt, kept, rows)
    grad_proj = jnp.einsum("td,cte->dce", normed_in, dqkv, preferred_element_type=F32)
    grad_proj = grad_proj.reshape(features, 3 * features)
    dnormed = jnp.einsum(
        "cte,dce->td",
        dqkv,
        qkv_weight.reshape(features, 3, features),
        preferred_element_type=F32,
    )
    _, back_one = jax.vjp(norm_rows, inputs, gain_rows[0])
    dinput_norm, dgain_one = back_one(dnormed)
    grad_tokens = dres + dinput_norm

    brought = unpack(made_back)
    output = (residual_one + gate_value[:, None] * brought).astype(BF16)

    def scattered(values):
        return lax.psum_scatter(
            core_sum(values, 1).astype(BF16), "expert", scatter_dimension=0, tiled=True
        ).astype(F32)

    small = [
        jnp.stack([dgain_one, dgain_two], axis=0),
        grad_router,
        table_gradient(band, far, bucket_count),
    ]
    flat = lax.psum(jnp.concatenate([s.reshape(-1) for s in small]), ("group", "expert"))
    summed = []
    at = 0
    for s in small:
        summed.append(flat[at : at + s.size].reshape(s.shape))
        at += s.size
    experts = lax.axis_size("expert")
    cores = lax.axis_size("group")
    grad_gains = lax.dynamic_slice(
        summed[0], (core, me * (features // experts)), (2 // cores, features // experts)
    )
    grad_router = lax.dynamic_slice(
        summed[1],
        (me * (features // experts), core * (expert_count // cores)),
        (features // experts, expert_count // cores),
    )
    return (
        output,
        grad_tokens,
        grad_gains,
        scattered(grad_proj),
        scattered(grad_out),
        summed[2],
        grad_router,
        grad_first,
        grad_second,
    )


def solution(mesh):
    return jax.shard_map(
        per_device,
        mesh=mesh,
        in_specs=(
            P(("group", "expert"), None),
            P(),
            P(),
            P(),
            P(),
            P(),
            P("expert", None, None),
            P("expert", None, None),
            P(("group", "expert"), None),
            P(("group", "expert")),
            P(("group", "expert"), None),
        ),
        out_specs=(
            P(("group", "expert"), None),
            P(("group", "expert"), None),
            P("group", "expert"),
            P("expert", "group"),
            P("expert", "group"),
            P(),
            P("expert", "group"),
            P("expert", None, "group"),
            P("expert", "group", None),
        ),
        check_vma=False,
    )
```

time: 1250 us -> 695 us (0.56)
  matrix products: 357 us -> 114 us
  blocking collectives: 207 us -> 43.1 us
  local copies, waits for them, and re-layouts: 192 us -> 46.4 us
  Pallas kernels: 0 us -> 126 us
  waiting for transfers between devices: 344 us -> 251 us
  other arithmetic: 110 us -> 29.8 us
  starting transfers between devices: 9.82 us -> 61.6 us
    dot_general x31 -> x22, matrix products: 354 us -> 114 us  [the longest x4 37.1 us: joined(): lax.dot_general(left[n], right[n], TN, preferred_element_type=F32)]
    all_to_all x2 -> x0, blocking collectives: 165 us -> none  [the longest x1 85 us: per_device(): lax.all_to_all(dexp_send, 'expert', split_axis=0, concat_axis=0, tiled=True)]
    pallas_call x0 -> x4, Pallas kernels: none -> 126 us  [the longest x2 63 us: run_expert(): pl.pallas_call(functools.partial(expert_kernel, width=min(1024, hidden_wi...]
    unnamed x12 -> x2, waiting for transfers between devices: 91.4 us -> 0.03 us
    dot_general x2 -> x0, local copies, waits for them, and re-layouts: 60.8 us -> none  [block_scores(): jnp.einsum('cqk,ch->hqk', onehot, rel_bias, preferred_element_type=jnp.fl...]
    convert_element_type x13 -> x9, other arithmetic: 61.8 us -> 10.4 us  [the longest x2 5.1 us: scattered(): core_sum(values, 1).astype(BF16)]
    all_to_all x2 -> x8, starting transfers between devices: 9.48 us -> 60.3 us  [exchange(): lax.all_to_all(values, 'expert', split_axis=0, concat_axis=0, tiled=True)]
    convert_element_type x2 -> x3, local copies, waits for them, and re-layouts: 46.4 us -> 5.82 us  [core_sum(): lax.dynamic_slice_in_dim(values, (1 - core) * half, half, dim).astype(BF16)]
  transfers between devices with their start and end apart: 10 -> 14, of which waited for: 8 -> 6; matrix products, arithmetic and copies ran while one was open for 26% -> 24% of each run, Pallas kernels for 0% -> 13%
where the time goes in v1:
time: 695 us; the launch traced here: 688 us
  waiting for transfers between devices  251 us (36%)
  Pallas kernels  126 us (18%)
  matrix products  114 us (16%)
  starting transfers between devices  61.6 us (9%)
  local copies, waits for them, and re-layouts  46.4 us (7%)
  blocking collectives  43.1 us (6%)
  other arithmetic  29.8 us (4%)
  between operations  15.6 us (2%)
    reduce_scatter x2, waiting for transfers between devices, scattered(): lax.psum_scatter(core_sum(values, 1).astype(BF16), 'expert', scatter_dime...  159 us
    all_to_all x8, waiting for transfers between devices, exchange(): lax.all_to_all(values, 'expert', split_axis=0, concat_axis=0, tiled=True)  92 us
    pallas_call x2, Pallas kernels, run_expert(): pl.pallas_call(functools.partial(expert_kernel, width=min(1024, hidden_wi...  63 us
    all_to_all x8, starting transfers between devices, exchange(): lax.all_to_all(values, 'expert', split_axis=0, concat_axis=0, tiled=True)  60.3 us
    psum x1, blocking collectives, per_device(): lax.psum(jnp.concatenate([s.reshape(-1) for s in small]), ('group', 'expe...  43.1 us
    dot_general x4, matrix products, joined(): lax.dot_general(left[n], right[n], TN, preferred_element_type=F32)  37.1 us
    pallas_call x1, Pallas kernels, attend(): pl.pallas_call(functools.partial(attend_kernel, rows=rows), grid=(pairs,)...  35.4 us
    unnamed x70, local copies, waits for them, and re-layouts  33 us
  transfers between devices with their start and end apart: 14, of which 6 were waited for; matrix products, arithmetic and copies ran while one was open for 24% of the time, Pallas kernels for 13%

profile of v1, /device:TPU:0, one launch (start us, length us, event | category | flops | bytes accessed | tf_op | source)
XLA Modules:
  0.0 687.7 jit_solution(7951746156227526552)
XLA Ops:
  7.2 1.8 copy.38
  10.2 7.8 %convolution_convert_fusion.q_ref.k_ref.v_ref = bf16[1024,2304]{1,0:T(8,128)(2,1)} fusion(bf16[768,2304]{1,0:T(8,128)(2,1)} %param.14, bf16[1024,768]{0,1:T(8,128)(2,1)S(1)} %copy.38, f32[768]{0:T(1024)S(1)} %get-tuple-element.72, f32[1024]{0:T(1024)S(1)} %fusion.78), kind=kOutput, calls=%fused_computation.7 | convolution fusion | flops 3629383680 | bytes 9837568 | tf_op jit(solution)/shard_map/dot_general | solution.py:382
  17.9 35.4 %shard_map.187 = (bf16[1024,768]{1,0:T(8,128)(2,1)S(1)}, bf16[12,1024,1024]{2,1,0:T(8,128)(2,1)}) custom-call(bf16[1024,2304]{1,0:T(8,128)(2,1)} %convolution_convert_fusion.q_ref.k_ref.v_ref, bf16[1024,2304]{1,0:T(8,128)(2,1)} %convolution_convert_fusion.q_ref.k_ref.v_ref, bf16[1024,2304]{1,0:T(8,128)(2,1)} %convolution_convert_fusion.q_ref.k_ref.v_ref, ...), custom_call_target="tpu_custom_call" | custom-call | flops 12884901888 | bytes 31457280 | tf_op jit(solution)/shard_map/pallas_call | solution.py:65
  53.4 1.6 multiply_reduce_fusion.2
  56.6 3.1 fusion.29
  59.7 8.4 %all-to-all-start = ((bf16[16,64,768]{2,1,0:T(8,128)(2,1)}), bf16[16,64,768]{2,1,0:T(8,128)(2,1)}, u32[]{:S(2)}, u32[]{:S(2)}) async-start(bf16[16,64,768]{2,1,0:T(8,128)(2,1)} %bitcast.82), calls=%async_computation | async-start | bytes 3145728 | tf_op jit(solution)/shard_map/all_to_all | solution.py:334
  68.1 4.5 fusion.31
  72.6 29.7 %all-to-all-done = bf16[16,64,768]{2,1,0:T(8,128)(2,1)} async-done(((bf16[16,64,768]{2,1,0:T(8,128)(2,1)}), bf16[16,64,768]{2,1,0:T(8,128)(2,1)}, u32[]{:S(2)}, u32[]{:S(2)}) %all-to-all-start) | async-done | bytes 1572896 | tf_op jit(solution)/shard_map/all_to_all | solution.py:334
  102.3 7.7 %all-to-all-start.2 = ((bf16[16,64,768]{2,1,0:T(8,128)(2,1)}), bf16[16,64,768]{2,1,0:T(8,128)(2,1)}, u32[]{:S(2)}, u32[]{:S(2)}) async-start(bf16[16,64,768]{2,1,0:T(8,128)(2,1)} %bitcast.81), calls=%async_computation.2 | async-start | bytes 3145728 | tf_op jit(solution)/shard_map/all_to_all | solution.py:334
  110.0 4.5 fusion.32
  114.5 29.1 %all-to-all-done.2 = bf16[16,64,768]{2,1,0:T(8,128)(2,1)} async-done(((bf16[16,64,768]{2,1,0:T(8,128)(2,1)}), bf16[16,64,768]{2,1,0:T(8,128)(2,1)}, u32[]{:S(2)}, u32[]{:S(2)}) %all-to-all-start.2) | async-done | bytes 1572896 | tf_op jit(solution)/shard_map/all_to_all | solution.py:334
  143.6 7.2 %all-to-all-start.3 = ((bf16[16,64,768]{2,1,0:T(8,128)(2,1)}), bf16[16,64,768]{2,1,0:T(8,128)(2,1)}, u32[]{:S(2)}, u32[]{:S(2)}) async-start(bf16[16,64,768]{2,1,0:T(8,128)(2,1)} %bitcast.77), calls=%async_computation.3 | async-start | bytes 3145728 | tf_op jit(solution)/shard_map/all_to_all | solution.py:334
  150.8 2.6 copy.42
  153.5 5.8 copy.45
  159.4 0.7 pad.4.router_ref
  161.2 4.5 fusion.30
  165.7 18.8 %all-to-all-done.3 = bf16[16,64,768]{2,1,0:T(8,128)(2,1)} async-done(((bf16[16,64,768]{2,1,0:T(8,128)(2,1)}), bf16[16,64,768]{2,1,0:T(8,128)(2,1)}, u32[]{:S(2)}, u32[]{:S(2)}) %all-to-all-start.3) | async-done | bytes 1572896 | tf_op jit(solution)/shard_map/all_to_all | solution.py:334
  184.5 7.3 %all-to-all-start.1 = ((bf16[16,64,768]{2,1,0:T(8,128)(2,1)}), bf16[16,64,768]{2,1,0:T(8,128)(2,1)}, u32[]{:S(2)}, u32[]{:S(2)}) async-start(bf16[16,64,768]{2,1,0:T(8,128)(2,1)} %bitcast.80), calls=%async_computation.1 | async-start | bytes 3145728 | tf_op jit(solution)/shard_map/all_to_all | solution.py:334
  191.8 1.7 fusion.80
  194.5 0.9 fusion.49.tile_ref
  195.4 31.5 %shard_map.189 = (bf16[1024,768]{1,0:T(8,128)(2,1)}, bf16[1024,768]{1,0:T(8,128)(2,1)}, bf16[1024,3072]{1,0:T(8,128)(2,1)}, bf16[1024,3072]{1,0:T(8,128)(2,1)}, ...) custom-call(bf16[1024,768]{1,0:T(8,128)(2,1)} %bitcast.10.x_ref, bf16[1024,768]{1,0:T(8,128)(2,1)} %bitcast.12.c_ref, ...), custom_call_target="tpu_custom_call" | custom-call | flops 19327352832 | bytes 25165824 | tf_op jit(solution)/shard_map/pallas_call | solution.py:287
  226.9 7.3 %all-to-all-start.5 = ((bf16[16,64,768]{2,1,0:T(8,128)(2,1)}), bf16[16,64,768]{2,1,0:T(8,128)(2,1)}, u32[]{:S(2)}, u32[]{:S(2)}) async-start(bf16[16,64,768]{2,1,0:T(8,128)(2,1)} %bitcast.79), calls=%async_computation.5 | async-start | bytes 3145728 | tf_op jit(solution)/shard_map/all_to_all | solution.py:334
  234.2 31.5 %shard_map.188 = (bf16[1024,768]{1,0:T(8,128)(2,1)}, bf16[1024,768]{1,0:T(8,128)(2,1)}, bf16[1024,3072]{1,0:T(8,128)(2,1)}, bf16[1024,3072]{1,0:T(8,128)(2,1)}, ...) custom-call(bf16[1024,768]{1,0:T(8,128)(2,1)} %bitcast.4.x_ref, bf16[1024,768]{1,0:T(8,128)(2,1)} %bitcast.6.c_ref, ...), custom_call_target="tpu_custom_call" | custom-call | flops 19327352832 | bytes 25165824 | tf_op jit(solution)/shard_map/pallas_call | solution.py:287
  265.7 7.9 %fusion.81 = f32[768,3072]{1,0:T(8,128)S(1)} fusion(bf16[1024,768]{1,0:T(8,128)(2,1)} %bitcast.4.x_ref, bf16[1024,3072]{1,0:T(8,128)(2,1)} %get-tuple-element.41), kind=kOutput, calls=%fused_computation.140 | convolution fusion | flops 4831838208 | bytes 17301504 | tf_op jit(solution)/shard_map/dot_general | solution.py:409
  273.7 9.3 %convolution_add_fusion.1 = f32[768,3072]{1,0:T(8,128)} fusion(f32[768,3072]{1,0:T(8,128)S(1)} %fusion.81, bf16[1024,768]{1,0:T(8,128)(2,1)} %bitcast.10.x_ref, bf16[1024,3072]{1,0:T(8,128)(2,1)S(1)} %copy-done.9), kind=kOutput, calls=%fused_computation.9 | convolution fusion | flops 4834197504 | bytes 26738688 | tf_op jit(solution)/shard_map/dot_general | solution.py:409
  283.2 4.1 dynamic-slice_convert_fusion.1
  287.4 10.4 %fusion.82 = f32[3072,768]{1,0:T(8,128)} fusion(bf16[1024,3072]{1,0:T(8,128)(2,1)} %get-tuple-element.43, bf16[1024,768]{1,0:T(8,128)(2,1)S(1)} %copy-done.29), kind=kOutput, calls=%fused_computation.141 | convolution fusion | flops 4831838208 | bytes 17301504 | tf_op jit(solution)/shard_map/dot_general | solution.py:409
  297.8 7.0 %all-to-all-start.4 = ((bf16[16,64,768]{2,1,0:T(8,128)(2,1)}), bf16[16,64,768]{2,1,0:T(8,128)(2,1)}, u32[]{:S(2)}, u32[]{:S(2)}) async-start(bf16[16,64,768]{2,1,0:T(8,128)(2,1)} %bitcast.78), calls=%async_computation.4 | async-start | bytes 3145728 | tf_op jit(solution)/shard_map/all_to_all | solution.py:334
  304.8 9.4 %convolution_add_fusion = f32[3072,768]{1,0:T(8,128)S(1)} fusion(f32[3072,768]{1,0:T(8,128)} %fusion.82, bf16[1024,3072]{1,0:T(8,128)(2,1)} %get-tuple-element.45, bf16[1024,768]{1,0:T(8,128)(2,1)} %get-tuple-element.46), kind=kOutput, calls=%fused_computation.8 | convolution fusion | flops 4834197504 | bytes 26738688 | tf_op jit(solution)/shard_map/dot_general | solution.py:409
  314.3 3.7 copy-done.11
  317.9 1.6 dynamic-slice_convert_fusion
  319.8 4.9 fusion.1
  324.7 14.4 %all-to-all-done.4 = bf16[16,64,768]{2,1,0:T(8,128)(2,1)} async-done(((bf16[16,64,768]{2,1,0:T(8,128)(2,1)}), bf16[16,64,768]{2,1,0:T(8,128)(2,1)}, u32[]{:S(2)}, u32[]{:S(2)}) %all-to-all-start.4) | async-done | bytes 1572896 | tf_op jit(solution)/shard_map/all_to_all | solution.py:334
  339.1 8.5 %all-to-all-start.7 = ((bf16[16,64,768]{2,1,0:T(8,128)(2,1)}), bf16[16,64,768]{2,1,0:T(8,128)(2,1)}, u32[]{:S(2)}, u32[]{:S(2)}) async-start(bf16[16,64,768]{2,1,0:T(8,128)(2,1)} %bitcast.76), calls=%async_computation.7 | async-start | bytes 3145728 | tf_op jit(solution)/shard_map/all_to_all | solution.py:334
  347.7 6.1 multiply_reduce_fusion
  353.8 0.8 fusion.14
  354.7 2.7 convolution_convert_fusion.1.dout_ref
  357.3 27.7 %shard_map.190 = (bf16[3,1024,768]{2,1,0:T(8,128)(2,1)}, f32[12,128,384]{2,1,0:T(8,128)}, f32[12,8,128]{2,1,0:T(8,128)}) custom-call(bf16[1024,2304]{1,0:T(8,128)(2,1)} %convolution_convert_fusion.q_ref.k_ref.v_ref, bf16[1024,2304]{1,0:T(8,128)(2,1)} %convolution_convert_fusion.q_ref.k_ref.v_ref, ...), custom_call_target="tpu_custom_call" | custom-call | flops 25769803776 | bytes 39321600 | tf_op jit(solution)/shard_map/pallas_call | solution.py:156
  385.1 6.5 fusion.33
  391.6 2.9 copy-done.12
  394.5 1.4 constant_dynamic-slice_fusion
  395.8 3.9 copy.71
  399.7 3.3 fusion.46
  403.7 5.9 add_bitcast_fusion.1
  409.7 1.0 add_convert_fusion.2
  410.7 5.7 add_bitcast_fusion
  416.4 4.0 constant_dynamic-slice_fusion.1
  420.4 5.2 copy.70
  425.6 6.9 %all-to-all-start.6 = ((bf16[16,64,768]{2,1,0:T(8,128)(2,1)}), bf16[16,64,768]{2,1,0:T(8,128)(2,1)}, u32[]{:S(2)}, u32[]{:S(2)}) async-start(bf16[16,64,768]{2,1,0:T(8,128)(2,1)} %bitcast.17), calls=%async_computation.6 | async-start | bytes 3145728 | tf_op jit(solution)/shard_map/all_to_all | solution.py:334
  433.0 4.1 add_convert_fusion
  437.4 5.8 fusion.43
  443.4 9.4 %fusion.13 = (f32[768]{0:T(1024)S(1)}, f32[1024]{0:T(1024)S(1)}, f32[1024,768,1]{0,1,2:T(8,128)}) fusion(bf16[1024,768]{0,1:T(8,128)(2,1)S(1)} %copy-done.4, f32[1024]{0:T(1024)S(1)} %copy-done.22, f32[768]{0:T(1024)S(1)} %copy-done.20, bf16[3,1024,768]{2,1,0:T(8,128)(2,1)} %get-tuple-element.36, bf16[768,3,768]{0,2,1:T(8,128)(2,1)} %bitcast.75), kind=kOutput, calls=%fused_computation.32 | convolution fusion | flops 3629381888 | bytes 12990464 | tf_op jit(solution)/shard_map/cte,dce->td/dot_general | solution.py:427
  452.9 43.1 %psum.7 = f32[14208]{0:T(1024)S(1)} all-reduce(f32[14208]{0:T(1024)S(1)} %pad_maximum_fusion), channel_id=1, replica_groups=mesh['group'=2,'expert'=16] {'group','expert'}, use_global_device_ids=true, to_apply=%region_12.13 | all-reduce | flops 14208 | bytes 113664 | tf_op jit(solution)/shard_map/psum | solution.py:450
  496.0 5.4 fusion.15
  501.4 3.5 copy.56
  505.1 0.7 copy.57
  506.0 0.7 copy.58
  507.2 40.9 %reduce-scatter.5.cloned.1.call-done = bf16[48,384]{1,0:T(8,128)(2,1)} async-done(((bf16[768,384]{1,0:T(8,128)(2,1)}), bf16[48,384]{1,0:T(8,128)(2,1)}) %reduce-scatter.5.cloned.1.call-update) | async-done | bytes 36880 | tf_op jit(solution)/shard_map/reduce_scatter | solution.py:441
  548.1 1.4 convert_element_type.284
  549.5 4.9 fusion.2
  554.5 5.3 add_convert_fusion.1
  559.8 1.6 copy.55
  561.4 117.7 %reduce-scatter.3.cloned.1.call-done = bf16[48,1152]{1,0:T(8,128)(2,1)} async-done(((bf16[768,1152]{1,0:T(8,128)(2,1)}), bf16[48,1152]{1,0:T(8,128)(2,1)}) %reduce-scatter.3.cloned.1.call-update) | async-done | bytes 110608 | tf_op jit(solution)/shard_map/reduce_scatter | solution.py:441
  679.1 1.6 convert_element_type.280
  (117 shorter events, 7.1 us)
Async XLA Ops:
  7.2 46.2 %copy-start = (bf16[768,768]{1,0:T(8,128)(2,1)S(1)}, bf16[768,768]{1,0:T(8,128)(2,1)}, u32[]{:S(2)}) copy-start(bf16[768,768]{1,0:T(8,128)(2,1)} %param.15) | copy-start | bytes 3538948
  7.2 1.9 copy-start.26
  7.2 2.3 copy-start.24
  9.1 376.0 %copy-start.3 = (bf16[1024,768]{0,1:T(8,128)(2,1)}, bf16[1024,768]{0,1:T(8,128)(2,1)S(1)}, u32[]{:S(2)}) copy-start(bf16[1024,768]{0,1:T(8,128)(2,1)S(1)} %copy.38) | copy-start | bytes 4718596
  9.1 8.8 %copy-start.19 = (f32[768]{0:T(1024)}, f32[768]{0:T(1024)S(1)}, u32[]{:S(2)}) copy-start(f32[768]{0:T(1024)S(1)} %get-tuple-element.72) | copy-start | bytes 9220
  9.5 0.7 copy-start.17
  9.5 8.4 %copy-start.21 = (f32[1024]{0:T(1024)}, f32[1024]{0:T(1024)S(1)}, u32[]{:S(2)}) copy-start(f32[1024]{0:T(1024)S(1)} %fusion.78) | copy-start | bytes 12292
  53.4 1.7 copy-start.1
  53.4 1.7 copy-start.23
  55.0 4.7 copy-start.5
  56.6 3.1 copy-start.8
  59.7 42.6 %all-to-all-start = ((bf16[16,64,768]{2,1,0:T(8,128)(2,1)}), bf16[16,64,768]{2,1,0:T(8,128)(2,1)}, u32[]{:S(2)}, u32[]{:S(2)}) async-start(bf16[16,64,768]{2,1,0:T(8,128)(2,1)} %bitcast.82), calls=%async_computation | async-start | bytes 3145728 | tf_op jit(solution)/shard_map/all_to_all | solution.py:334
  102.3 41.3 %all-to-all-start.2 = ((bf16[16,64,768]{2,1,0:T(8,128)(2,1)}), bf16[16,64,768]{2,1,0:T(8,128)(2,1)}, u32[]{:S(2)}, u32[]{:S(2)}) async-start(bf16[16,64,768]{2,1,0:T(8,128)(2,1)} %bitcast.81), calls=%async_computation.2 | async-start | bytes 3145728 | tf_op jit(solution)/shard_map/all_to_all | solution.py:334
  143.6 40.9 %all-to-all-start.3 = ((bf16[16,64,768]{2,1,0:T(8,128)(2,1)}), bf16[16,64,768]{2,1,0:T(8,128)(2,1)}, u32[]{:S(2)}, u32[]{:S(2)}) async-start(bf16[16,64,768]{2,1,0:T(8,128)(2,1)} %bitcast.77), calls=%async_computation.3 | async-start | bytes 3145728 | tf_op jit(solution)/shard_map/all_to_all | solution.py:334
  153.5 5.8 copy-start.15
  184.5 42.4 %all-to-all-start.1 = ((bf16[16,64,768]{2,1,0:T(8,128)(2,1)}), bf16[16,64,768]{2,1,0:T(8,128)(2,1)}, u32[]{:S(2)}, u32[]{:S(2)}) async-start(bf16[16,64,768]{2,1,0:T(8,128)(2,1)} %bitcast.80), calls=%async_computation.1 | async-start | bytes 3145728 | tf_op jit(solution)/shard_map/all_to_all | solution.py:334
  226.9 70.9 %all-to-all-start.5 = ((bf16[16,64,768]{2,1,0:T(8,128)(2,1)}), bf16[16,64,768]{2,1,0:T(8,128)(2,1)}, u32[]{:S(2)}, u32[]{:S(2)}) async-start(bf16[16,64,768]{2,1,0:T(8,128)(2,1)} %bitcast.79), calls=%async_computation.5 | async-start | bytes 3145728 | tf_op jit(solution)/shard_map/all_to_all | solution.py:334
  265.7 7.9 %copy-start.9 = (bf16[1024,3072]{1,0:T(8,128)(2,1)S(1)}, bf16[1024,3072]{1,0:T(8,128)(2,1)}, u32[]{:S(2)}) copy-start(bf16[1024,3072]{1,0:T(8,128)(2,1)} %get-tuple-element.42) | copy-start | bytes 18874372
  273.7 9.3 %copy-start.13 = (f32[768,128]{1,0:T(8,128)S(1)}, f32[768,128]{1,0:T(8,128)}, u32[]{:S(2)}) copy-start(f32[768,128]{1,0:T(8,128)} %get-tuple-element.38) | copy-start | bytes 1179652
  273.7 9.3 %copy-start.14 = (f32[768,128]{1,0:T(8,128)S(1)}, f32[768,128]{1,0:T(8,128)}, u32[]{:S(2)}) copy-start(f32[768,128]{1,0:T(8,128)} %get-tuple-element.37) | copy-start | bytes 1179652
  283.2 4.2 copy-start.29
  287.4 116.4 %collective-permute-start.2 = (bf16[768,1536]{1,0:T(8,128)(2,1)}, bf16[768,1536]{1,0:T(8,128)(2,1)}, u32[]{:S(2)}, u32[]{:S(2)}) collective-permute-start(bf16[768,1536]{1,0:T(8,128)(2,1)} %dynamic-slice_convert_fusion.1), channel_id=1, source_target_pairs={{0,16},{16,0},{1,17},{17,1},{2,18},{18,2},{3,19},{19,3},{4,20},{20... | collective-permute-start | bytes 7077896 | tf_op jit(solution)/shard_map/ppermute | solution.py:330
  297.8 41.4 %all-to-all-start.4 = ((bf16[16,64,768]{2,1,0:T(8,128)(2,1)}), bf16[16,64,768]{2,1,0:T(8,128)(2,1)}, u32[]{:S(2)}, u32[]{:S(2)}) async-start(bf16[16,64,768]{2,1,0:T(8,128)(2,1)} %bitcast.78), calls=%async_computation.4 | async-start | bytes 3145728 | tf_op jit(solution)/shard_map/all_to_all | solution.py:334
  314.3 3.7 copy-start.11
  319.5 91.1 %collective-permute-start.3 = (bf16[1536,768]{1,0:T(8,128)(2,1)}, bf16[1536,768]{1,0:T(8,128)(2,1)}, u32[]{:S(2)}, u32[]{:S(2)}) collective-permute-start(bf16[1536,768]{1,0:T(8,128)(2,1)} %dynamic-slice_convert_fusion), channel_id=1, source_target_pairs={{0,16},{16,0},{1,17},{17,1},{2,18},{18,2},{3,19},{19,3},{4,20},{20... | collective-permute-start | bytes 7077896 | tf_op jit(solution)/shard_map/ppermute | solution.py:330
  339.1 86.5 %all-to-all-start.7 = ((bf16[16,64,768]{2,1,0:T(8,128)(2,1)}), bf16[16,64,768]{2,1,0:T(8,128)(2,1)}, u32[]{:S(2)}, u32[]{:S(2)}) async-start(bf16[16,64,768]{2,1,0:T(8,128)(2,1)} %bitcast.76), calls=%async_computation.7 | async-start | bytes 3145728 | tf_op jit(solution)/shard_map/all_to_all | solution.py:334
  347.6 200.5 %reduce-scatter.5.cloned.1.call-start = ((), (), s32[]{:S(2)}) async-start(), calls=%async_computation.11 | async-start | bytes 626688 | tf_op jit(solution)/shard_map/reduce_scatter | solution.py:441
  347.7 6.1 copy-start.6
  347.7 6.1 copy-start.10
  354.6 2.7 copy-start.7
  357.3 27.8 %copy-start.20 = (f32[768]{0:T(1024)S(1)}, f32[768]{0:T(1024)}, u32[]{:S(2)}) copy-start(f32[768]{0:T(1024)} %copy-done.19) | copy-start | bytes 9220
  357.3 27.8 %copy-start.22 = (f32[1024]{0:T(1024)S(1)}, f32[1024]{0:T(1024)}, u32[]{:S(2)}) copy-start(f32[1024]{0:T(1024)} %copy-done.21) | copy-start | bytes 12292
  391.6 2.9 copy-start.12
  394.5 5.3 copy-start.2
  399.7 33.3 %collective-permute-start = (bf16[768,1152]{1,0:T(8,128)(2,1)}, bf16[768,1152]{1,0:T(8,128)(2,1)}, u32[]{:S(2)}, u32[]{:S(2)}) collective-permute-start(bf16[768,1152]{1,0:T(8,128)(2,1)} %copy.71), channel_id=1, source_target_pairs={{0,16},{16,0},{1,17},{17,1},{2,18},{18,2},{3,19},{19,3},{4,20},{20... | collective-permute-start | bytes 5308424 | tf_op jit(solution)/shard_map/ppermute | solution.py:330
  403.1 6.5 collective-permute-start.1
  425.6 128.9 %all-to-all-start.6 = ((bf16[16,64,768]{2,1,0:T(8,128)(2,1)}), bf16[16,64,768]{2,1,0:T(8,128)(2,1)}, u32[]{:S(2)}, u32[]{:S(2)}) async-start(bf16[16,64,768]{2,1,0:T(8,128)(2,1)} %bitcast.17), calls=%async_computation.6 | async-start | bytes 3145728 | tf_op jit(solution)/shard_map/all_to_all | solution.py:334
  432.5 4.7 copy-start.16
  432.5 4.8 copy-start.27
  432.5 4.8 copy-start.28
  432.5 246.6 %reduce-scatter.3.cloned.1.call-start = ((), (), s32[]{:S(2)}) async-start(), calls=%async_computation.10 | async-start | bytes 1880064 | tf_op jit(solution)/shard_map/reduce_scatter | solution.py:441
  437.1 6.2 copy-start.4
  443.4 52.7 %copy-start.18 = (f32[1024]{0:T(1024)S(1)}, f32[1024]{0:T(1024)}, u32[]{:S(2)}) copy-start(f32[1024]{0:T(1024)} %copy-done.17) | copy-start | bytes 12292
  549.5 4.9 copy-start.25
Sparse Core Ops, SparseCore 0:
  410.8 137.3 reduce-scatter.4
  553.7 125.3 reduce-scatter.2

commit v2 on v1

--- a/solution.py
+++ b/solution.py
@@ -223,103 +223,323 @@
 
 
 def expert_kernel(
-    x_ref, c_ref, w_in_ref, w_out_ref, router_ref, mine_ref,
-    made_ref, dmoved_ref, act_ref, dpre_ref, dexp_ref, drouter_ref, *, width, expert_count,
+    hidden_ref, cot_ref, w_in_ref, w_out_ref, router_ref,
+    made_ref, back_ref, first_ref, second_ref, drouter_ref,
+    w_in, w_out, x, c, x_turned, dexp_turned, moved, act, dpre, stage_first, stage_second, load_sem, cot_sem, out_sem, sent, came, moved_sent, moved_came, core_sent,
+    core_came, stage_sem, core_ready, *, ranks, expert_count, rows, width, columns,
 ):
-    x, c = x_ref[...], c_ref[...]
-    router_weight = router_ref[...]
-    lane = lax.broadcasted_iota(jnp.int32, (1, router_weight.shape[1]), 1)
-    logits = jnp.dot(x, router_weight, preferred_element_type=F32)
-    logits = jnp.where(lane < expert_count, logits, -jnp.inf)
-    raised = jnp.exp(logits - jnp.max(logits, axis=-1, keepdims=True))
-    router = raised / jnp.sum(raised, axis=-1, keepdims=True)
-    chosen = mine_ref[...]
-    gate = jnp.sum(router * chosen, axis=-1, keepdims=True)
-    upstream = c.astype(F32)
-    dexp = (gate * upstream).astype(BF16)
-    dexp_ref[...] = dexp
-    hidden_width = w_in_ref.shape[1]
-    made = jnp.zeros(x.shape, F32)
-    dmoved = jnp.zeros(x.shape, F32)
+    features = x.shape[1]
+    slots = x.shape[0] // ranks
+    hidden_width = w_in.shape[1]
+    half = hidden_width // 2
+    per_step = rows // slots
+    core, me = lax.axis_index("group"), lax.axis_index("expert")
+    plane = 4 if ranks % 4 == 0 else 1
+    layers = ranks // plane
+
+    def partner(k, sign):
+        layer = (me // plane + layers + sign * (k // plane)) % layers
+        return layer * plane + (me % plane + plane + sign * (k % plane)) % plane
+
+    def span(k):
+        return pl.ds(pl.multiple_of(k * slots, slots), slots)
+
+    barrier = pltpu.get_barrier_semaphore()
+
+    def greet(k, carry):
+        pl.semaphore_signal(
+            barrier, inc=1, device_id=(core, partner(k, 1)), device_id_type=pl.DeviceIdType.MESH
+        )
+        return carry
+
+    lax.fori_loop(1, ranks, greet, 0)
+    pl.semaphore_signal(
+        barrier, inc=1, device_id=(1 - core, me), device_id_type=pl.DeviceIdType.MESH
+    )
+
+    loads = [
+        pltpu.make_async_copy(w_in_ref, w_in, load_sem.at[0]),
+        pltpu.make_async_copy(w_out_ref, w_out, load_sem.at[1]),
+        pltpu.make_async_copy(hidden_ref.at[me], x.at[pl.ds(0, slots)], load_sem.at[2]),
+    ]
+    for load in loads:
+        load.start()
+
+    def cot_copy(k):
+        return pltpu.make_async_copy(cot_ref.at[partner(k, -1)], c.at[span(k)], cot_sem.at[k])
+
+    def load_cot(k, carry):
+        cot_copy(k).start()
+        return carry
+
+    lax.fori_loop(0, ranks, load_cot, 0)
+    pl.semaphore_wait(barrier, ranks)
+
+    def hidden_copy(k):
+        return pltpu.make_async_remote_copy(
+            src_ref=hidden_ref.at[partner(k, 1)],
+            dst_ref=x.at[span(k)],
+            send_sem=sent.at[k],
+            recv_sem=came.at[k],
+            device_id=(core, partner(k, 1)),
+            device_id_type=pl.DeviceIdType.MESH,
+        )
+
+    def moved_copy(k):
+        return pltpu.make_async_remote_copy(
+            src_ref=moved.at[span(k)],
+            dst_ref=back_ref.at[me],
+            send_sem=moved_sent.at[k],
+            recv_sem=moved_came.at[k],
+            device_id=(core, partner(k, -1)),
+            device_id_type=pl.DeviceIdType.MESH,
+        )
+
+    def own_moved_copy():
+        return pltpu.make_async_copy(moved.at[pl.ds(0, slots)], back_ref.at[me], load_sem.at[3])
+
+    def made_copy(k):
+        return pltpu.make_async_copy(c.at[span(k)], made_ref.at[partner(k, -1)], out_sem.at[k])
+
+    def start_hidden(k, carry):
+        hidden_copy(k).start()
+        return carry
+
+    lax.fori_loop(1, ranks, start_hidden, 0)
+    for load in loads:
+        load.wait()
+    drouter_ref[...] = jnp.zeros_like(drouter_ref)
     root = (2.0 / jnp.pi) ** 0.5
-    for first in range(0, hidden_width, width):
-        part = slice(first, first + width)
-        pre = jnp.dot(x, w_in_ref[:, part], preferred_element_type=F32)
-        square = pre * pre
-        turned = jnp.tanh(pre * (root + (root * 0.044715) * square))
-        half = 0.5 + 0.5 * turned
-        act = (pre * half).astype(BF16)
-        slope = half + pre * (half * (1.0 - turned)) * (root + (3 * root * 0.044715) * square)
-        act_ref[:, part] = act
-        made = made + jnp.dot(act, w_out_ref[part, :], preferred_element_type=F32)
-        dact = lax.dot_general(dexp, w_out_ref[part, :], NT, preferred_element_type=F32)
-        dpre = (dact * slope).astype(BF16)
-        dpre_ref[:, part] = dpre
-        dmoved = dmoved + lax.dot_general(
-            dpre, w_in_ref[:, part], NT, preferred_element_type=F32
+
+    def run(first_rank):
+        block = pl.ds(pl.multiple_of(first_rank * slots, rows), rows)
+        xs = x[block, :]
+        upstream = c[block, :].astype(F32)
+        router_weight = router_ref[...]
+        lane = lax.broadcasted_iota(jnp.int32, (1, router_weight.shape[1]), 1)
+        logits = jnp.dot(xs, router_weight, preferred_element_type=F32)
+        logits = jnp.where(lane < expert_count, logits, -jnp.inf)
+        raised = jnp.exp(logits - jnp.max(logits, axis=-1, keepdims=True))
+        router = raised / jnp.sum(raised, axis=-1, keepdims=True)
+        chosen = (lane == me).astype(F32)
+        gate = jnp.sum(router * chosen, axis=-1, keepdims=True)
+        dexp = (gate * upstream).astype(BF16)
+        made = jnp.zeros((rows, features), F32)
+        dmoved = jnp.zeros((rows, features), F32)
+        for at in range(0, hidden_width, width):
+            part = slice(at, at + width)
+            pre = jnp.dot(xs, w_in[:, part], preferred_element_type=F32)
+            square = pre * pre
+            turned = jnp.tanh(pre * (root + (root * 0.044715) * square))
+            upper = 0.5 + 0.5 * turned
+            active = (pre * upper).astype(BF16)
+            slope = upper + pre * (upper * (1.0 - turned)) * (
+                root + (3 * root * 0.044715) * square
+            )
+            act[block, part] = active
+            made = made + jnp.dot(active, w_out[part, :], preferred_element_type=F32)
+            dact = lax.dot_general(dexp, w_out[part, :], NT, preferred_element_type=F32)
+            dpart = (dact * slope).astype(BF16)
+            dpre[block, part] = dpart
+            dmoved = dmoved + lax.dot_general(
+                dpart, w_in[:, part], NT, preferred_element_type=F32
+            )
+        made = made.astype(BF16)
+        c[block, :] = made
+        dgate = jnp.sum(upstream * made.astype(F32), axis=-1, keepdims=True)
+        dlogits = (dgate * gate * (chosen - router)).astype(BF16)
+        dmoved = dmoved + lax.dot_general(dlogits, router_weight, NT, preferred_element_type=F32)
+        moved[block, :] = dmoved.astype(BF16)
+        xt = xs.T
+        x_turned[:, block] = xt
+        dexp_turned[:, block] = dexp.T
+        drouter_ref[...] += jnp.dot(xt, dlogits, preferred_element_type=F32)
+
+    def step(number, carry):
+        first_rank = number * per_step
+        for inner in range(per_step):
+            k = first_rank + inner
+            cot_copy(k).wait()
+
+            @pl.when(k > 0)
+            def _(k=k):
+                hidden_copy(k).wait_recv()
+
+        run(first_rank)
+        for inner in range(per_step):
+            k = first_rank + inner
+            made_copy(k).start()
+
+            @pl.when(k > 0)
+            def _(k=k):
+                moved_copy(k).start()
+
+        @pl.when(number == 0)
+        def _():
+            own_moved_copy().start()
+
+        return carry
+
+    lax.fori_loop(0, ranks // per_step, step, 0)
+
+    other = 1 - core
+    across = features // columns
+
+    def landed_first(n):
+        return pl.ds(n // across * features, features), pl.ds(n % across * columns, columns)
+
+    def first_copy(n):
+        part = pl.ds(n * columns, columns)
+        return pltpu.make_async_remote_copy(
+            src_ref=w_in.at[:, part],
+            dst_ref=c.at[landed_first(n)],
+            send_sem=core_sent.at[0, n],
+            recv_sem=core_came.at[0, n],
+            device_id=(other, me),
+            device_id_type=pl.DeviceIdType.MESH,
         )
-    made = made.astype(BF16)
-    made_ref[...] = made
-    dgate = jnp.sum(upstream * made.astype(F32), axis=-1, keepdims=True)
-    dlogits = (dgate * gate * (chosen - router)).astype(BF16)
-    dmoved_ref[...] = (
-        dmoved + lax.dot_general(dlogits, router_weight, NT, preferred_element_type=F32)
-    ).astype(BF16)
-
-    @pl.when(pl.program_id(0) == 0)
-    def _():
-        drouter_ref[...] = jnp.zeros_like(drouter_ref)
-
-    drouter_ref[...] += lax.dot_general(x, dlogits, TN, preferred_element_type=F32)
-
-
-def run_expert(x, c, w_in, w_out, router_padded, mine, expert_count):
-    total, features = x.shape
+
+    def second_copy(n):
+        part = pl.ds(n * columns, columns)
+        return pltpu.make_async_remote_copy(
+            src_ref=w_out.at[part],
+            dst_ref=x.at[part],
+            send_sem=core_sent.at[1, n],
+            recv_sem=core_came.at[1, n],
+            device_id=(other, me),
+            device_id_type=pl.DeviceIdType.MESH,
+        )
+
+    def product(turned, wide, part):
+        return jnp.dot(turned[...], wide[:, part], preferred_element_type=F32)
+
+    def made_out(k, carry):
+        made_copy(k).wait()
+        return carry
+
+    lax.fori_loop(0, ranks, made_out, 0)
+    pl.semaphore_signal(
+        core_ready, inc=1, device_id=(other, me), device_id_type=pl.DeviceIdType.MESH
+    )
+    tiles = half // columns
+    for n in range(tiles):
+        part = pl.ds(pl.multiple_of(other * half + n * columns, columns), columns)
+        w_in[:, n * columns : (n + 1) * columns] = product(x_turned, dpre, part).astype(BF16)
+        if n == 0:
+            pl.semaphore_wait(core_ready, 1)
+        first_copy(n).start()
+        w_out[n * columns : (n + 1) * columns, :] = product(dexp_turned, act, part).T.astype(BF16)
+        second_copy(n).start()
+    stores = []
+    for n in range(tiles):
+        part = pl.ds(pl.multiple_of(core * half + n * columns, columns), columns)
+        here = slice(n * columns, (n + 1) * columns)
+        own = product(x_turned, dpre, part)
+        first_copy(n).wait_recv()
+        if n:
+            stores[2 * n - 2].wait()
+        stage_first[...] = own + c[landed_first(n)].astype(F32)
+        stores.append(
+            pltpu.make_async_copy(
+                stage_first, first_ref.at[:, pl.ds(n * columns, columns)],
+                stage_sem.at[0, n],
+            )
+        )
+        stores[-1].start()
+        own = product(dexp_turned, act, part).T
+        second_copy(n).wait_recv()
+        if n:
+            stores[2 * n - 1].wait()
+        stage_second[...] = own + x[here, :].astype(F32)
+        stores.append(
+            pltpu.make_async_copy(
+                stage_second, second_ref.at[pl.ds(n * columns, columns)],
+                stage_sem.at[1, n],
+            )
+        )
+        stores[-1].start()
+    for store in stores[-2:]:
+        store.wait()
+    for n in range(tiles):
+        first_copy(n).wait_send()
+        second_copy(n).wait_send()
+
+    def finish(k, carry):
+        @pl.when(k > 0)
+        def _():
+            hidden_copy(k).wait_send()
+            moved_copy(k).wait_send()
+            moved_copy(k).wait_recv()
+
+        return carry
+
+    lax.fori_loop(0, ranks, finish, 0)
+    own_moved_copy().wait()
+
+
+def run_expert(hidden, cot, w_in, w_out, router_padded, expert_count):
+    ranks, slots, features = hidden.shape
     hidden_width = w_in.shape[1]
-    rows = min(256, total)
+    rows = max(min(256, ranks * slots), slots)
+    total = ranks * slots
     padded = router_padded.shape[1]
-    row_block = pl.BlockSpec((rows, features), lambda i: (i, 0))
-    wide_block = pl.BlockSpec((rows, hidden_width), lambda i: (i, 0))
-
-    def whole(shape):
-        return pl.BlockSpec(shape, lambda i: (0, 0))
-
+    half = hidden_width // 2
+    columns = min(256, half)
+    tiles = half // columns
+    any_ref = pl.BlockSpec(memory_space=pl.ANY)
+    vmem = pl.BlockSpec(memory_space=pltpu.VMEM)
+    dma = pltpu.SemaphoreType.DMA
     return pl.pallas_call(
         functools.partial(
-            expert_kernel, width=min(1024, hidden_width), expert_count=expert_count
+            expert_kernel,
+            ranks=ranks,
+            expert_count=expert_count,
+            rows=rows,
+            width=min(512, hidden_width),
+            columns=columns,
         ),
-        grid=(total // rows,),
-        in_specs=[
-            row_block,
-            row_block,
-            whole(w_in.shape),
-            whole(w_out.shape),
-            whole(router_padded.shape),
-            whole(mine.shape),
-        ],
-        out_specs=[
-            row_block,
-            row_block,
-            wide_block,
-            wide_block,
-            row_block,
-            whole((features, padded)),
-        ],
+        in_specs=[any_ref, any_ref, any_ref, any_ref, vmem],
+        out_specs=[any_ref, any_ref, any_ref, any_ref, vmem],
         out_shape=[
-            jax.ShapeDtypeStruct((total, features), BF16),
-            jax.ShapeDtypeStruct((total, features), BF16),
-            jax.ShapeDtypeStruct((total, hidden_width), BF16),
-            jax.ShapeDtypeStruct((total, hidden_width), BF16),
-            jax.ShapeDtypeStruct((total, features), BF16),
+            jax.ShapeDtypeStruct((ranks, slots, features), BF16),
+            jax.ShapeDtypeStruct((ranks, slots, features), BF16),
+            jax.ShapeDtypeStruct((features, half), F32),
+            jax.ShapeDtypeStruct((half, features), F32),
             jax.ShapeDtypeStruct((features, padded), F32),
         ],
-        compiler_params=pltpu.CompilerParams(vmem_limit_bytes=56 * MIB),
+        scratch_shapes=[
+            pltpu.VMEM((features, hidden_width), BF16),
+            pltpu.VMEM((hidden_width, features), BF16),
+            pltpu.VMEM((total, features), BF16),
+            pltpu.VMEM((total, features), BF16),
+            pltpu.VMEM((features, total), BF16),
+            pltpu.VMEM((features, total), BF16),
+            pltpu.VMEM((total, features), BF16),
+            pltpu.VMEM((total, hidden_width), BF16),
+            pltpu.VMEM((total, hidden_width), BF16),
+            pltpu.VMEM((features, columns), F32),
+            pltpu.VMEM((columns, features), F32),
+            dma((4,)),
+            dma((ranks,)),
+            dma((ranks,)),
+            dma((ranks,)),
+            dma((ranks,)),
+            dma((ranks,)),
+            dma((ranks,)),
+            dma((2, tiles)),
+            dma((2, tiles)),
+            dma((2, tiles)),
+            pltpu.SemaphoreType.REGULAR,
+        ],
+        compiler_params=pltpu.CompilerParams(
+            collective_id=1, has_side_effects=True, vmem_limit_bytes=63 * MIB
+        ),
         cost_estimate=pl.CostEstimate(
-            flops=8 * total * features * hidden_width,
-            bytes_accessed=4 * features * hidden_width + 4 * total * (hidden_width + features),
+            flops=12 * total * features * hidden_width,
+            bytes_accessed=8 * features * hidden_width + 8 * total * features,
             transcendentals=total * hidden_width,
         ),
-    )(x, c, w_in, w_out, router_padded, mine)
+    )(hidden, cot, w_in, w_out, router_padded)
 
 
 def core_sum(values, dim):
@@ -342,7 +562,6 @@
     bucket_count = rel_bias.shape[0]
     expert_count = router_weight.shape[1]
     slot_count = 2 * length // expert_count
-    chunk = slot_count // 2
     rows = min(256, length)
     gain_rows = gains.astype(F32)
     w_in, w_out = w_in[0], w_out[0]
@@ -356,26 +575,20 @@
     before = jnp.dot(earlier, chosen.astype(BF16), preferred_element_type=F32)
     place = jnp.sum(before * chosen.astype(F32), axis=-1).astype(jnp.int32)
     capacity = factors[0] * (length // expert_count)
-    placed = jnp.where(place < capacity, place, slot_count)
-    slots = jnp.arange(expert_count * chunk, dtype=jnp.int32)
-    picks = []
-    for number in range(2):
-        inside = (placed >= number * chunk) & (placed < (number + 1) * chunk)
-        target = jnp.where(inside, routed * chunk + placed - number * chunk, -1)
-        picks.append((slots[:, None] == target[None, :]).astype(BF16))
-
-    def pack(values, number):
-        return jnp.dot(picks[number], values, preferred_element_type=F32).astype(BF16)
-
-    def unpack(parts):
-        return sum(
-            lax.dot_general(picks[n], parts[n], TN, preferred_element_type=F32) for n in range(2)
+    target = jnp.where(place < capacity, routed * slot_count + place, -1)
+    slots = jnp.arange(expert_count * slot_count, dtype=jnp.int32)
+    picks = (slots[:, None] == target[None, :]).astype(BF16)
+
+    def pack(values):
+        packed = jnp.dot(picks, values, preferred_element_type=F32).astype(BF16)
+        return packed.reshape(expert_count, slot_count, features)
+
+    def unpack(values):
+        return lax.dot_general(
+            picks, values.reshape(-1, features), TN, preferred_element_type=F32
         )
 
-    def send(values):
-        return exchange(values.reshape(expert_count, chunk, features)).reshape(-1, features)
-
-    upstream_there = [send(pack(cotangent, n)) for n in range(2)]
+    upstream_there = exchange(pack(cotangent))
 
     inputs = tokens.astype(F32)
     normed_in = norm_rows(inputs, gain_rows[0]).astype(BF16)
@@ -389,29 +602,14 @@
     router = raised / jnp.sum(raised, axis=-1, keepdims=True)
     gate_value = jnp.sum(router * chosen.astype(F32), axis=-1)
 
-    hidden_there = [send(pack(hidden, n)) for n in range(2)]
     padded = -expert_count % LANES
     router_padded = jnp.pad(router_weight, ((0, 0), (0, padded)))
-    mine = (jnp.arange(expert_count + padded)[None, :] == me).astype(F32)
-    results = [
-        run_expert(
-            hidden_there[n], upstream_there[n], w_in, w_out, router_padded, mine, expert_count
-        )
-        for n in range(2)
-    ]
-    made, dmoved, act, dpre, dexp, drouter = zip(*results, strict=True)
-    dmoved_back = [send(dmoved[n]) for n in range(2)]
-    made, _ = lax.optimization_barrier((made, dmoved_back))
-    made_back = [send(made[n]) for n in range(2)]
-
-    def joined(left, right):
-        return sum(
-            lax.dot_general(left[n], right[n], TN, preferred_element_type=F32) for n in range(2)
-        )
-
-    grad_first = core_sum(joined(hidden_there, dpre), 1)[None]
-    grad_second = core_sum(joined(act, dexp), 0)[None]
-    grad_router = (drouter[0] + drouter[1])[:, :expert_count]
+    hidden, upstream_there = lax.optimization_barrier((hidden, upstream_there))
+    made, dmoved_back, grad_first, grad_second, drouter = run_expert(
+        pack(hidden), upstream_there, w_in, w_out, router_padded, expert_count
+    )
+    made_back = exchange(made)
+    grad_router = drouter[:, :expert_count]
 
     dhidden = unpack(dmoved_back)
     upstream = cotangent.astype(F32)
@@ -471,8 +669,8 @@
         scattered(grad_out),
         summed[2],
         grad_router,
-        grad_first,
-        grad_second,
+        grad_first[None],
+        grad_second[None],
     )
 
 

time: 695 us -> 624 us (0.90)
  Pallas kernels: 126 us -> 226 us
  waiting for transfers between devices: 251 us -> 174 us
  matrix products: 114 us -> 65 us
  starting transfers between devices: 61.6 us -> 33.8 us
    pallas_call x2 -> x1, Pallas kernels: 63 us -> 163 us  [run_expert(): pl.pallas_call(functools.partial(expert_kernel, ranks=ranks, expert_count...]
    all_to_all x8 -> x2, waiting for transfers between devices: 92 us -> 9.37 us  [exchange(): lax.all_to_all(values, 'expert', split_axis=0, concat_axis=0, tiled=True)]
    dot_general x12 -> x4, matrix products: 75 us -> 25.2 us  [the longest x2 13.5 us: unpack(): lax.dot_general(picks, values.reshape(-1, features), TN, preferred_elemen...]
    all_to_all x8 -> x2, starting transfers between devices: 60.3 us -> 32.8 us  [exchange(): lax.all_to_all(values, 'expert', split_axis=0, concat_axis=0, tiled=True)]
    broadcast_in_dim x2 -> x0, other arithmetic: 11.6 us -> none  [the longest x1 5.94 us: per_device(): grad_first = core_sum(joined(hidden_there, dpre), 1)[None]]
    unnamed x70 -> x76, local copies, waits for them, and re-layouts: 33 us -> 33.2 us
  transfers between devices with their start and end apart: 14 -> 6, of which waited for: 6 -> 4; matrix products, arithmetic and copies ran while one was open for 24% -> 15% of each run, Pallas kernels for 13% -> 10%
where the time goes in v2:
time: 624 us; the launch traced here: 620 us
  Pallas kernels  226 us (36%)
  waiting for transfers between devices  174 us (28%)
  matrix products  65 us (10%)
  blocking collectives  41.5 us (7%)
  local copies, waits for them, and re-layouts  41.4 us (7%)
  starting transfers between devices  33.8 us (5%)
  other arithmetic  23.1 us (4%)
  between operations  15.4 us (2%)
    reduce_scatter x2, waiting for transfers between devices, scattered(): lax.psum_scatter(core_sum(values, 1).astype(BF16), 'expert', scatter_dime...  163 us
    pallas_call x1, Pallas kernels, run_expert(): pl.pallas_call(functools.partial(expert_kernel, ranks=ranks, expert_count...  163 us
    psum x1, blocking collectives, per_device(): lax.psum(jnp.concatenate([s.reshape(-1) for s in small]), ('group', 'expe...  41.5 us
    pallas_call x1, Pallas kernels, attend(): pl.pallas_call(functools.partial(attend_kernel, rows=rows), grid=(pairs,)...  35.3 us
    unnamed x76, local copies, waits for them, and re-layouts  33.2 us
    all_to_all x2, starting transfers between devices, exchange(): lax.all_to_all(values, 'expert', split_axis=0, concat_axis=0, tiled=True)  32.8 us
    pallas_call x1, Pallas kernels, attend_back(): pl.pallas_call(functools.partial(attend_back_kernel, rows=rows), grid=(pa...  27.7 us
    dot_general x2, matrix products, unpack(): lax.dot_general(picks, values.reshape(-1, features), TN, preferred_elemen...  13.5 us
  transfers between devices with their start and end apart: 6, of which 4 were waited for; matrix products, arithmetic and copies ran while one was open for 15% of the time, Pallas kernels for 10%

profile of v2, /device:TPU:0, one launch (start us, length us, event | category | flops | bytes accessed | tf_op | source)
XLA Modules:
  0.0 620.2 jit_solution(6868866822176791525)
XLA Ops:
  7.2 1.3 fusion.25
  9.1 0.7 add_select_fusion.1
  9.8 6.5 %fusion.12 = bf16[2048,768]{1,0:T(8,128)(2,1)} fusion(bf16[1024,768]{1,0:T(8,128)(2,1)} %param.22, s32[1024]{0:T(1024)S(1)} %add_select_fusion.1), kind=kOutput, calls=%fused_computation.24 | convolution fusion | flops 3224895488 | bytes 4722688 | tf_op jit(solution)/shard_map/dot_general | solution.py:583
  16.3 9.0 %all-to-all-start = ((bf16[16,128,768]{2,1,0:T(8,128)(2,1)}), bf16[16,128,768]{2,1,0:T(8,128)(2,1)}, u32[]{:S(2)}, u32[]{:S(2)}) async-start(bf16[16,128,768]{2,1,0:T(8,128)(2,1)} %bitcast.3), calls=%async_computation | async-start | bytes 6291456 | tf_op jit(solution)/shard_map/all_to_all | solution.py:554
  25.4 1.6 copy.40
  27.0 0.7 copy.37
  28.2 0.8 pad.4.router_ref
  29.4 0.6 copy-done.21
  30.0 7.8 %convolution_convert_fusion.q_ref.k_ref.v_ref = bf16[1024,2304]{1,0:T(8,128)(2,1)} fusion(bf16[768,2304]{1,0:T(8,128)(2,1)} %param.14, bf16[1024,768]{0,1:T(8,128)(2,1)S(1)} %copy.37, f32[768]{0:T(1024)S(1)} %get-tuple-element.58, f32[1024]{0:T(1024)S(1)} %fusion.67), kind=kOutput, calls=%fused_computation.12 | convolution fusion | flops 3629383680 | bytes 9837568 | tf_op jit(solution)/shard_map/dot_general | solution.py:595
  37.8 35.3 %shard_map.187 = (bf16[1024,768]{1,0:T(8,128)(2,1)S(1)}, bf16[12,1024,1024]{2,1,0:T(8,128)(2,1)}) custom-call(bf16[1024,2304]{1,0:T(8,128)(2,1)} %convolution_convert_fusion.q_ref.k_ref.v_ref, bf16[1024,2304]{1,0:T(8,128)(2,1)} %convolution_convert_fusion.q_ref.k_ref.v_ref, bf16[1024,2304]{1,0:T(8,128)(2,1)} %convolution_convert_fusion.q_ref.k_ref.v_ref, ...), custom_call_target="tpu_custom_call" | custom-call | flops 12884901888 | bytes 31457280 | tf_op jit(solution)/shard_map/pallas_call | solution.py:65
  73.1 1.7 multiply_reduce_fusion.2
  74.8 1.1 fusion.38.tile_ref
  75.9 0.7 copy-done.7
  76.9 9.4 %all-to-all-done.cot_ref = bf16[16,128,768]{2,1,0:T(8,128)(2,1)} async-done(((bf16[16,128,768]{2,1,0:T(8,128)(2,1)}), bf16[16,128,768]{2,1,0:T(8,128)(2,1)}, u32[]{:S(2)}, u32[]{:S(2)}) %all-to-all-start) | async-done | bytes 3145760 | tf_op jit(solution)/shard_map/all_to_all | solution.py:554
  86.3 5.3 fusion.13
  91.5 163.3 %shard_map.188 = (bf16[16,128,768]{2,1,0:T(8,128)(2,1)}, bf16[16,128,768]{2,1,0:T(8,128)(2,1)}, f32[768,1536]{1,0:T(8,128)}, f32[1536,768]{1,0:T(8,128)}, f32[768,128]{1,0:T(8,128)}) custom-call(bf16[16,128,768]{2,1,0:T(8,128)(2,1)} %bitcast.62, bf16[16,128,768]{2,1,0:T(8,128)(2,1)} %all-to-all-done.cot_ref, bf16[768,3072]{1,0:T(8,128)(2,1)} %bitcast.59, ...), custom_call_target="tpu_custom_call" | custom-call | flops 57982058496 | bytes 31457280 | tf_op jit(solution)/shard_map/pallas_call | solution.py:492
  254.9 23.7 %all-to-all-start.1 = ((bf16[16,128,768]{2,1,0:T(8,128)(2,1)}), bf16[16,128,768]{2,1,0:T(8,128)(2,1)}, u32[]{:S(2)}, u32[]{:S(2)}) async-start(bf16[16,128,768]{2,1,0:T(8,128)(2,1)} %get-tuple-element.24), calls=%async_computation.1 | async-start | bytes 6291456 | tf_op jit(solution)/shard_map/all_to_all | solution.py:554
  278.6 0.5 reduce-scatter.5.cloned.1.call-start
  279.2 6.9 %multiply_reduce_fusion = (f32[768]{0:T(1024)}, f32[1024]{0:T(1024)S(1)}, f32[1024,768]{0,1:T(8,128)S(1)}) fusion(f32[1024,768]{0,1:T(8,128)S(1)} %copy-done.8, f32[1024]{0:T(1024)S(1)} %fusion.68, f32[768]{0:T(1024)S(1)} %get-tuple-element.57, bf16[2048,768]{1,0:T(8,128)(2,1)} %bitcast.61, s32[1024]{0:T(1024)S(1)} %add_select_fusion.1), kind=kOutput, calls=%fused_computation.35 | convolution fusion | flops 3228039424 | bytes 9455616 | tf_op jit(solution)/shard_map/dot_general | solution.py:587
  286.1 0.8 fusion.16
  287.0 0.4 copy-done.29
  287.4 2.6 convolution_convert_fusion.1.dout_ref
  290.0 27.7 %shard_map.189 = (bf16[3,1024,768]{2,1,0:T(8,128)(2,1)}, f32[12,128,384]{2,1,0:T(8,128)}, f32[12,8,128]{2,1,0:T(8,128)}) custom-call(bf16[1024,2304]{1,0:T(8,128)(2,1)} %convolution_convert_fusion.q_ref.k_ref.v_ref, bf16[1024,2304]{1,0:T(8,128)(2,1)} %convolution_convert_fusion.q_ref.k_ref.v_ref, ...), custom_call_target="tpu_custom_call" | custom-call | flops 25769803776 | bytes 39321600 | tf_op jit(solution)/shard_map/pallas_call | solution.py:156
  317.7 6.6 %fusion.22 = f32[768,3,768]{0,2,1:T(8,128)S(1)} fusion(bf16[3,1024,768]{2,1,0:T(8,128)(2,1)} %get-tuple-element.27, bf16[1024,768]{0,1:T(8,128)(2,1)S(1)} %copy-done.5, f32[768]{0:T(1024)S(1)} %get-tuple-element.58, f32[1024]{0:T(1024)S(1)} %fusion.67), kind=kOutput, calls=%fused_computation.42 | convolution fusion | flops 3627024384 | bytes 13376512 | tf_op jit(solution)/shard_map/td,cte->dce/dot_general | solution.py:623
  324.3 2.9 copy-done.14
  327.3 2.3 copy.67
  329.6 3.4 fusion.35
  333.0 1.4 copy-done.18
  334.4 0.9 dynamic-slice_convert_fusion
  335.3 0.5 collective-permute-start.1
  335.8 0.5 compare_convert_fusion
  336.3 0.6 iota_add_fusion.1
  336.9 0.9 collective-permute-done.1
  337.8 2.4 add_convert_fusion.2
  340.2 0.5 iota_add_fusion.2
  340.7 3.8 copy.42
  344.5 2.2 constant_dynamic-slice_fusion.1
  346.7 3.0 copy.66
  349.7 4.2 add_convert_fusion
  353.9 1.2 fusion.69
  355.2 0.6 select_reduce_fusion
  355.8 0.7 iota_compare_fusion.30
  356.5 0.9 fusion.41
  357.4 1.0 select_reduce_fusion.2
  358.3 5.7 fusion.32
  364.4 0.7 reshape.277
  365.1 9.5 %fusion.15 = (f32[768]{0:T(1024)S(1)}, f32[1024]{0:T(1024)S(1)}, f32[1024,768,1]{0,1,2:T(8,128)}) fusion(bf16[1024,768]{0,1:T(8,128)(2,1)S(1)} %copy-done.6, f32[1024]{0:T(1024)S(1)} %fusion.67, f32[768]{0:T(1024)S(1)} %get-tuple-element.58, bf16[3,1024,768]{2,1,0:T(8,128)(2,1)} %get-tuple-element.27, bf16[768,3,768]{0,2,1:T(8,128)(2,1)} %bitcast.54), kind=kOutput, calls=%fused_computation.27 | convolution fusion | flops 3629381888 | bytes 12990464 | tf_op jit(solution)/shard_map/cte,dce->td/dot_general | solution.py:625
  374.7 41.5 %psum.7 = f32[14208]{0:T(1024)S(1)} all-reduce(f32[14208]{0:T(1024)S(1)} %pad_maximum_fusion), channel_id=1, replica_groups=mesh['group'=2,'expert'=16] {'group','expert'}, use_global_device_ids=true, to_apply=%region_12.13 | all-reduce | flops 14208 | bytes 113664 | tf_op jit(solution)/shard_map/psum | solution.py:648
  416.2 0.6 slice.54
  416.8 5.4 fusion.17
  422.2 3.7 copy.54
  426.0 0.7 copy.55
  426.7 1.0 reshape.284
  427.6 0.7 dynamic_slice.23
  428.3 1.4 copy.56
  429.7 0.6 dynamic_slice.18
  430.3 33.5 %reduce-scatter.5.cloned.1.call-done = bf16[48,384]{1,0:T(8,128)(2,1)} async-done(((bf16[768,384]{1,0:T(8,128)(2,1)}), bf16[48,384]{1,0:T(8,128)(2,1)}) %reduce-scatter.5.cloned.1.call-update) | async-done | bytes 36880 | tf_op jit(solution)/shard_map/reduce_scatter | solution.py:639
  463.8 1.4 convert_element_type.256
  465.2 129.8 %reduce-scatter.3.cloned.1.call-done = bf16[48,1152]{1,0:T(8,128)(2,1)} async-done(((bf16[768,1152]{1,0:T(8,128)(2,1)}), bf16[48,1152]{1,0:T(8,128)(2,1)}) %reduce-scatter.3.cloned.1.call-update) | async-done | bytes 110608 | tf_op jit(solution)/shard_map/reduce_scatter | solution.py:639
  595.0 1.6 convert_element_type.252
  596.6 6.6 %add_convert_fusion.1 = bf16[1024,768]{0,1:T(8,128)(2,1)} fusion(f32[1024,768]{0,1:T(8,128)S(1)} %copy-done.9, bf16[2048,768]{1,0:T(8,128)(2,1)} %bitcast.7, s32[1024]{0:T(1024)S(1)} %copy-done.25, f32[1024]{0:T(1024)S(1)} %copy-done.26), kind=kOutput, calls=%fused_computation.37 | convolution fusion | flops 3225681920 | bytes 7872512 | tf_op jit(solution)/shard_map/dot_general | solution.py:587
  603.2 2.6 copy.53
  605.8 5.0 copy.79
  610.9 2.2 copy.80
  (93 shorter events, 2.1 us)
Async XLA Ops:
  7.2 20.6 %copy-start = (bf16[32,12]{0,1:T(8,128)(2,1)S(1)}, bf16[32,12]{0,1:T(8,128)(2,1)}, u32[]{:S(2)}) copy-start(bf16[32,12]{0,1:T(8,128)(2,1)} %param.16) | copy-start | bytes 2308
  9.8 269.3 %copy-start.24 = (s32[1024]{0:T(1024)}, s32[1024]{0:T(1024)S(1)}, u32[]{:S(2)}) copy-start(s32[1024]{0:T(1024)S(1)} %add_select_fusion.1) | copy-start | bytes 12292
  16.3 9.0 %copy-start.16 = (bf16[1024,768]{1,0:T(8,128)(2,1)S(1)}, bf16[1024,768]{1,0:T(8,128)(2,1)}, u32[]{:S(2)}) copy-start(bf16[1024,768]{1,0:T(8,128)(2,1)} %param.22) | copy-start | bytes 4718596
  16.3 70.0 %all-to-all-start = ((bf16[16,128,768]{2,1,0:T(8,128)(2,1)}), bf16[16,128,768]{2,1,0:T(8,128)(2,1)}, u32[]{:S(2)}, u32[]{:S(2)}) async-start(bf16[16,128,768]{2,1,0:T(8,128)(2,1)} %bitcast.3), calls=%async_computation | async-start | bytes 6291456 | tf_op jit(solution)/shard_map/all_to_all | solution.py:554
  25.3 1.7 copy-start.17
  25.4 2.4 copy-start.27
  25.4 2.7 copy-start.20
  27.8 45.3 %copy-start.4 = (bf16[1024,768]{0,1:T(8,128)(2,1)}, bf16[1024,768]{0,1:T(8,128)(2,1)S(1)}, u32[]{:S(2)}) copy-start(bf16[1024,768]{0,1:T(8,128)(2,1)S(1)} %copy.37) | copy-start | bytes 4718596
  29.4 0.6 copy-start.21
  37.8 35.3 %copy-start.28 = (bf16[768,768]{1,0:T(8,128)(2,1)S(1)}, bf16[768,768]{1,0:T(8,128)(2,1)}, u32[]{:S(2)}) copy-start(bf16[768,768]{1,0:T(8,128)(2,1)} %param.15) | copy-start | bytes 3538948
  73.1 1.7 copy-start.2
  74.8 1.8 copy-start.7
  76.9 14.6 %copy-start.11 = (bf16[1024,768]{0,1:T(8,128)(2,1)}, bf16[1024,768]{0,1:T(8,128)(2,1)S(1)}, u32[]{:S(2)}) copy-start(bf16[1024,768]{0,1:T(8,128)(2,1)S(1)} %multiply_convert_fusion) | copy-start | bytes 4718596
  254.9 24.3 %copy-start.8 = (f32[1024,768]{0,1:T(8,128)S(1)}, f32[1024,768]{0,1:T(8,128)}, u32[]{:S(2)}) copy-start(f32[1024,768]{0,1:T(8,128)} %copy-done.7) | copy-start | bytes 9437188
  254.9 341.7 %all-to-all-start.1 = ((bf16[16,128,768]{2,1,0:T(8,128)(2,1)}), bf16[16,128,768]{2,1,0:T(8,128)(2,1)}, u32[]{:S(2)}, u32[]{:S(2)}) async-start(bf16[16,128,768]{2,1,0:T(8,128)(2,1)} %get-tuple-element.24), calls=%async_computation.1 | async-start | bytes 6291456 | tf_op jit(solution)/shard_map/all_to_all | solution.py:554
  278.6 185.2 %reduce-scatter.5.cloned.1.call-start = ((), (), s32[]{:S(2)}) async-start(), calls=%async_computation.5 | async-start | bytes 626688 | tf_op jit(solution)/shard_map/reduce_scatter | solution.py:639
  279.2 6.9 %copy-start.13 = (bf16[1024,768]{0,1:T(8,128)(2,1)S(1)}, bf16[1024,768]{0,1:T(8,128)(2,1)}, u32[]{:S(2)}) copy-start(bf16[1024,768]{0,1:T(8,128)(2,1)} %copy.40) | copy-start | bytes 4718596
  286.1 1.3 copy-start.29
  287.4 2.6 copy-start.10
  290.0 27.7 %copy-start.5 = (bf16[1024,768]{0,1:T(8,128)(2,1)S(1)}, bf16[1024,768]{0,1:T(8,128)(2,1)}, u32[]{:S(2)}) copy-start(bf16[1024,768]{0,1:T(8,128)(2,1)} %copy-done.4) | copy-start | bytes 4718596
  324.2 2.9 copy-start.14
  327.2 2.5 copy-start.3
  329.6 20.1 %collective-permute-start = (bf16[768,1152]{1,0:T(8,128)(2,1)}, bf16[768,1152]{1,0:T(8,128)(2,1)}, u32[]{:S(2)}, u32[]{:S(2)}) collective-permute-start(bf16[768,1152]{1,0:T(8,128)(2,1)} %copy.67), channel_id=1, source_target_pairs={{0,16},{16,0},{1,17},{17,1},{2,18},{18,2},{3,19},{19,3},{4,20},{20... | collective-permute-start | bytes 5308424 | tf_op jit(solution)/shard_map/ppermute | solution.py:550
  333.0 1.4 copy-start.18
  334.4 6.3 %copy-start.15 = (bf16[768,2304]{1,0:T(8,128)(2,1)S(1)}, bf16[768,2304]{1,0:T(8,128)(2,1)}, u32[]{:S(2)}) copy-start(bf16[768,2304]{1,0:T(8,128)(2,1)} %param.14) | copy-start | bytes 10616836
  335.3 2.5 collective-permute-start.1
  340.2 254.9 %reduce-scatter.3.cloned.1.call-start = ((), (), s32[]{:S(2)}) async-start(), calls=%async_computation.4 | async-start | bytes 1880064 | tf_op jit(solution)/shard_map/reduce_scatter | solution.py:639
  349.7 4.3 copy-start.12
  353.9 1.3 copy-start.23
  353.9 10.3 %copy-start.19 = (f32[768,128]{1,0:T(8,128)S(1)}, f32[768,128]{1,0:T(8,128)}, u32[]{:S(2)}) copy-start(f32[768,128]{1,0:T(8,128)} %get-tuple-element.28) | copy-start | bytes 1179652
  353.9 11.2 %copy-start.6 = (bf16[1024,768]{0,1:T(8,128)(2,1)S(1)}, bf16[1024,768]{0,1:T(8,128)(2,1)}, u32[]{:S(2)}) copy-start(bf16[1024,768]{0,1:T(8,128)(2,1)} %copy-done.4) | copy-start | bytes 4718596
  365.1 51.7 %copy-start.22 = (f32[1024]{0:T(1024)S(1)}, f32[1024]{0:T(1024)}, u32[]{:S(2)}) copy-start(f32[1024]{0:T(1024)} %copy-done.21) | copy-start | bytes 12292
  422.2 174.5 %copy-start.9 = (f32[1024,768]{0,1:T(8,128)S(1)}, f32[1024,768]{0,1:T(8,128)}, u32[]{:S(2)}) copy-start(f32[1024,768]{0,1:T(8,128)} %copy-done.7) | copy-start | bytes 9437188
  422.2 174.5 %copy-start.25 = (s32[1024]{0:T(1024)S(1)}, s32[1024]{0:T(1024)}, u32[]{:S(2)}) copy-start(s32[1024]{0:T(1024)} %copy-done.24) | copy-start | bytes 12292
  422.2 174.5 %copy-start.26 = (f32[1024]{0:T(1024)S(1)}, f32[1024]{0:T(1024)}, u32[]{:S(2)}) copy-start(f32[1024]{0:T(1024)} %select_reduce_fusion) | copy-start | bytes 12292
  603.2 7.6 %slice-start = ((s8[4718592]{0:T(1024)(128)(4,1)}), s8[524288]{0:T(1024)(128)(4,1)S(1)}, s32[]{:S(2)}) async-start(s8[4718592]{0:T(1024)(128)(4,1)} %bitcast.48), calls=%async_computation.6 | async-start | bytes 1048576
  605.8 5.0 slice-start.1
  605.8 7.2 %copy-start.1 = (bf16[32,12]{0,1:T(8,128)(2,1)S(1)}, bf16[32,12]{0,1:T(8,128)(2,1)}, u32[]{:S(2)}) copy-start(bf16[32,12]{0,1:T(8,128)(2,1)} %param.16) | copy-start | bytes 2308
Sparse Core Ops, SparseCore 0:
  340.3 123.4 reduce-scatter.4
  469.4 125.5 reduce-scatter.2

commit v3 on v2

--- a/solution.py
+++ b/solution.py
@@ -542,6 +542,437 @@
     )(hidden, cot, w_in, w_out, router_padded)
 
 
+def tail_kernel(
+    q_ref, k_ref, v_ref, out_ref, dout_ref, kept_ref, wq_ref, wk_ref, wv_ref, tile_ref,
+    normed_ref, tokens_ref, dres_ref, gain_ref, dgain_ref, bucket_ref, first_ref,
+    tokens_grad_ref, dense_ref, early_ref, small_ref,
+    dscores, dnormed, lines, own, core_out, core_in, plane_out, plane_in, layer_out, layer_in,
+    early_core, early_own, early_plane_out, early_plane_in, early_layer_out, early_layer_in,
+    small_out, small_in, load_sem, core_sent, core_came, plane_sent, plane_came, layer_sent,
+    layer_came, small_sent, small_came, *, rows, ranks, plane,
+):
+    length, features = tokens_ref.shape
+    tiles = length // LANES
+    inner = rows // LANES
+    layers = ranks // plane
+    slab = features // ranks
+    heads = 2 * (pl.num_programs(0) - 1)
+    groups = (pl.num_programs(0) - 1) // 2
+    step = pl.program_id(0)
+    core, me = lax.axis_index("group"), lax.axis_index("expert")
+    other = 1 - core
+    layer, spot = me // plane, me % plane
+    mesh = pl.DeviceIdType.MESH
+
+    def in_plane(k, sign):
+        return (spot + plane + sign * k) % plane
+
+    def in_line(k, sign):
+        return (layer + layers + sign * k) % layers
+
+    def rank_of(a_layer, a_spot):
+        return a_layer * plane + a_spot
+
+    def core_copy(unit):
+        early = unit == 0
+        return pltpu.make_async_remote_copy(
+            src_ref=first_ref.at[other] if early else core_out.at[unit - 1],
+            dst_ref=early_core if early else core_in.at[unit - 1],
+            send_sem=core_sent.at[unit],
+            recv_sem=core_came.at[unit],
+            device_id=(other, me),
+            device_id_type=mesh,
+        )
+
+    def plane_copy(unit, k):
+        early = unit == 0
+        source = early_plane_out if early else plane_out.at[unit - 1]
+        return pltpu.make_async_remote_copy(
+            src_ref=source.at[:, in_plane(k, 1)],
+            dst_ref=early_plane_in.at[k - 1] if early else plane_in.at[unit - 1, k - 1],
+            send_sem=plane_sent.at[unit, k],
+            recv_sem=plane_came.at[unit, k],
+            device_id=(core, rank_of(layer, in_plane(k, 1))),
+            device_id_type=mesh,
+        )
+
+    def layer_copy(unit, k):
+        early = unit == 0
+        source = early_layer_out if early else layer_out.at[unit - 1]
+        return pltpu.make_async_remote_copy(
+            src_ref=source.at[in_line(k, 1)],
+            dst_ref=early_layer_in.at[k - 1] if early else layer_in.at[unit - 1, k - 1],
+            send_sem=layer_sent.at[unit, k],
+            recv_sem=layer_came.at[unit, k],
+            device_id=(core, rank_of(in_line(k, 1), spot)),
+            device_id_type=mesh,
+        )
+
+    def peer(number):
+        return (core + number // ranks) % 2, (me + number) % ranks
+
+    def small_copy(number):
+        return pltpu.make_async_remote_copy(
+            src_ref=small_out,
+            dst_ref=small_in.at[number],
+            send_sem=small_sent.at[number],
+            recv_sem=small_came.at[number],
+            device_id=peer(number),
+            device_id_type=mesh,
+        )
+
+    def own_load():
+        return pltpu.make_async_copy(first_ref.at[core], early_own, load_sem.at[0])
+
+    def sum_cores(unit):
+        core_copy(unit).wait_recv()
+        if unit == 0:
+            own_load().wait()
+            summed = early_own[...].astype(F32) + early_core[...].astype(F32)
+            early_plane_out[...] = summed.astype(BF16).reshape(early_plane_out.shape)
+        else:
+            summed = own[unit % 2] + core_in[unit - 1].astype(F32)
+            plane_out[unit - 1] = summed.astype(BF16).reshape(plane_out.shape[1:])
+        for k in range(1, plane):
+            plane_copy(unit, k).start()
+
+    def sum_planes(unit):
+        summed = (early_plane_out[:, spot] if unit == 0 else plane_out[unit - 1, :, spot]).astype(F32)
+        for k in range(1, plane):
+            plane_copy(unit, k).wait_recv()
+            came = early_plane_in[k - 1] if unit == 0 else plane_in[unit - 1, k - 1]
+            summed = summed + came.astype(F32)
+        if unit == 0:
+            early_layer_out[...] = summed.astype(BF16)
+        else:
+            layer_out[unit - 1] = summed.astype(BF16)
+        for k in range(1, layers):
+            layer_copy(unit, k).start()
+
+    def sum_layers(unit):
+        summed = (early_layer_out[layer] if unit == 0 else layer_out[unit - 1, layer]).astype(F32)
+        for k in range(1, layers):
+            layer_copy(unit, k).wait_recv()
+            came = early_layer_in[k - 1] if unit == 0 else layer_in[unit - 1, k - 1]
+            summed = summed + came.astype(F32)
+        if unit == 0:
+            early_ref[...] = summed
+        else:
+            group = unit - 1
+            base = core * (groups * LANES)
+            keys_at = other * (2 * groups * LANES) + group * LANES
+            for part, at in enumerate(
+                (base + group * LANES, base + (groups + group) * LANES, keys_at)
+            ):
+                dense_ref[:, pl.ds(pl.multiple_of(at, LANES), LANES)] = summed[
+                    :, part * LANES : (part + 1) * LANES
+                ]
+
+    @pl.when(step == 0)
+    def _():
+        own_load().start()
+        barrier = pltpu.get_barrier_semaphore()
+
+        def greet(number, carry):
+            pl.semaphore_signal(barrier, inc=1, device_id=peer(number), device_id_type=mesh)
+            return carry
+
+        lax.fori_loop(1, 2 * ranks, greet, 0)
+        dnormed[...] = jnp.zeros_like(dnormed)
+        pl.semaphore_wait(barrier, 2 * ranks - 1)
+        core_copy(0).start()
+
+    @pl.when(step < 2 * groups)
+    def _():
+        lane = lax.broadcasted_iota(jnp.int32, (1, LANES), 1)
+        queries, values, dout = q_ref[...], v_ref[...], dout_ref[...]
+        widened = jnp.concatenate([k_ref[...], tile_ref[...]], axis=1)
+        dout_wide = dout.astype(F32)
+        product = dout_wide * out_ref[...].astype(F32)
+        dout_turned, queries_turned = dout.T, queries.T
+        mirror = (
+            lax.broadcasted_iota(jnp.int32, (LANES, LANES), 0)
+            + lax.broadcasted_iota(jnp.int32, (LANES, LANES), 1)
+            == LANES - 1
+        ).astype(F32)
+        dqueries = [[], []]
+        dkeys, dvalues = [], []
+        for head in range(2):
+            mine = (lane < HEAD) if head == 0 else (lane >= HEAD)
+            inner_sum = jnp.sum(jnp.where(mine, product, 0.0), axis=1, keepdims=True)
+            masked = jnp.where(mine, dout_wide, 0.0).astype(BF16)
+            bands = [jnp.zeros((LANES, LANES), F32) for _ in range(3)]
+            before = jnp.zeros((1, LANES), F32)
+            after = jnp.zeros((1, LANES), F32)
+            for part_of in range(length // rows):
+                first = part_of * rows
+                block = pl.ds(first, rows)
+                dprob = lax.dot_general(
+                    masked[first : first + rows], values, NT, preferred_element_type=F32
+                )
+                scores = kept_ref[head, block, :].astype(F32) * (
+                    dprob - inner_sum[first : first + rows]
+                )
+                rounded = scores.astype(BF16)
+                dscores[block, :] = rounded
+                both = jnp.dot(rounded, widened, preferred_element_type=F32)
+                dqueries[head].append(both[:, :LANES])
+                for part in range(inner):
+                    tile = part_of * inner + part
+                    here = slice(part * LANES, (part + 1) * LANES)
+                    for at in range(3):
+                        there = tile - 1 + at
+                        if 0 <= there < tiles:
+                            bands[at] = bands[at] + scores[here, there * LANES : (there + 1) * LANES]
+                    sums = jnp.sum(both[here, LANES:], axis=0, keepdims=True)
+                    before = before + jnp.where(lane <= tile - 2, sums, 0.0)
+                    after = after + jnp.where((lane >= tile + 2) & (lane < tiles), sums, 0.0)
+            band = jnp.concatenate([*bands, jnp.zeros((LANES, LANES), F32)], axis=1)
+            band = jnp.dot(
+                mirror, band, preferred_element_type=F32, precision=lax.Precision.HIGHEST
+            )
+            band = pltpu.roll(band, 3 * LANES + 1, 1, stride=1, stride_axis=0)
+            near = jnp.sum(band, axis=0, keepdims=True)
+            pair = step % 2 * groups + step // 2
+            lines[pl.ds(2 * pair + head, 1), :] = jnp.concatenate([near, before, after], axis=1)
+            half = slice(HEAD * head, HEAD * head + HEAD)
+            dkeys.append(
+                jnp.dot(queries_turned[half], dscores[...], preferred_element_type=F32)
+            )
+            dvalues.append(jnp.dot(dout_turned[half], kept_ref[head], preferred_element_type=F32))
+        scale = HEAD**-0.5
+        dq = jnp.concatenate(
+            [
+                (jnp.where(lane < HEAD, left, right) * scale).astype(BF16)
+                for left, right in zip(*dqueries, strict=True)
+            ],
+            axis=0,
+        )
+        dk = (jnp.concatenate(dkeys, axis=0) * scale).T.astype(BF16)
+        dv = jnp.concatenate(dvalues, axis=0).T.astype(BF16)
+        joined = jnp.concatenate([dq, dk, dv], axis=1)
+        weights = jnp.concatenate([wq_ref[...], wk_ref[...], wv_ref[...]], axis=1)
+        dnormed[...] += lax.dot_general(joined, weights, NT, preferred_element_type=F32)
+        dense = jnp.dot(normed_ref[...], joined, preferred_element_type=F32)
+        dwq, dwk, dwv = dense[:, :LANES], dense[:, LANES : 2 * LANES], dense[:, 2 * LANES :]
+        own_first, away_first = jnp.where(core == 0, dwq, dwv), jnp.where(core == 0, dwv, dwq)
+        for now in range(2 * groups):
+
+            @pl.when(step == now)
+            def _(now=now):
+                unit, part = now // 2 + 1, now % 2
+                at = slice(part * LANES, (part + 1) * LANES)
+                own[unit % 2, :, at] = own_first
+                core_out[unit - 1, :, at] = away_first.astype(BF16)
+
+                @pl.when(core == part)
+                def _():
+                    own[unit % 2, :, 2 * LANES :] = dwk
+
+                @pl.when(core != part)
+                def _():
+                    core_out[unit - 1, :, 2 * LANES :] = dwk.astype(BF16)
+
+                if part == 1:
+                    core_copy(unit).start()
+
+    last = 2 * groups
+    plan = {}
+    for unit in range(groups + 1):
+        made = 0 if unit == 0 else 2 * unit - 1
+        plan.setdefault(min(made + 1, last), []).append((sum_cores, unit))
+        plan.setdefault(min(made + 3, last), []).append((sum_planes, unit))
+        plan.setdefault(min(made + 5, last), []).append((sum_layers, unit))
+    order = [sum_layers, sum_planes, sum_cores]
+    for now in range(1, last):
+
+        @pl.when(step == now)
+        def _(now=now):
+            for action, unit in sorted(plan.get(now, []), key=lambda p: order.index(p[0])):
+                action(unit)
+
+    @pl.when(step == last)
+    def _():
+        todo = plan.get(last, [])
+        for action, unit in todo:
+            if action is sum_cores:
+                action(unit)
+        for action, unit in todo:
+            if action is sum_planes and unit < groups:
+                action(unit)
+        gain = gain_ref[...]
+        inputs = tokens_ref[...].astype(F32)
+        spread = lax.rsqrt(jnp.mean(inputs * inputs, axis=1, keepdims=True) + EPSILON)
+        back = dnormed[...]
+        scaled = inputs * spread
+        dgain = jnp.sum(back * scaled, axis=0, keepdims=True)
+        moved = back * gain
+        tokens_grad_ref[...] = dres_ref[...] + spread * (
+            moved - scaled * jnp.mean(moved * scaled, axis=1, keepdims=True)
+        )
+        table = jnp.dot(
+            lines[...], bucket_ref[...], preferred_element_type=F32, precision=lax.Precision.HIGHEST
+        )
+        small_out[0 : lines.shape[0], :] = table
+        base = lines.shape[0]
+        wide = features // LANES
+        for part in range(wide):
+            small_out[base + part : base + part + 1, :] = dgain[
+                :, part * LANES : (part + 1) * LANES
+            ]
+        small_out[base + wide : base + 2 * wide, :] = dgain_ref[...]
+        if small_out.shape[0] > base + 2 * wide:
+            small_out[base + 2 * wide :, :] = jnp.zeros(
+                (small_out.shape[0] - base - 2 * wide, LANES), F32
+            )
+
+        def start_small(number, carry):
+            small_copy(number).start()
+            return carry
+
+        lax.fori_loop(1, 2 * ranks, start_small, 0)
+        for action, unit in todo:
+            if action is sum_planes and unit == groups:
+                action(unit)
+        for action, unit in todo:
+            if action is sum_layers:
+                action(unit)
+        small_ref[...] = small_out[...]
+
+        def add_small(number, carry):
+            small_copy(number).wait_recv()
+            small_ref[...] += small_in[number]
+            return carry
+
+        lax.fori_loop(1, 2 * ranks, add_small, 0)
+
+        def drop_small(number, carry):
+            small_copy(number).wait_send()
+            return carry
+
+        lax.fori_loop(1, 2 * ranks, drop_small, 0)
+        for unit in range(groups + 1):
+            core_copy(unit).wait_send()
+            for k in range(1, plane):
+                plane_copy(unit, k).wait_send()
+            for k in range(1, layers):
+                layer_copy(unit, k).wait_send()
+
+
+def run_tail(
+    projected, attended, datt, kept, qkv_weight, normed_turned, tokens, dres, gain, dgain, first, ranks,
+    bucket_count, rows,
+):
+    length, features = tokens.shape
+    heads = kept.shape[0]
+    pairs = heads // 2
+    groups = pairs // 2
+    plane = 4
+    layers = ranks // plane
+    slab = features // ranks
+    early = first.shape[2]
+    late = 3 * LANES
+    tile_of = (
+        jnp.arange(length)[:, None] // LANES == jnp.arange(LANES)[None, :]
+    ).astype(BF16)
+    at = jnp.arange(4 * LANES, dtype=jnp.int32)
+    relative = jnp.where(at < 3 * LANES, at - LANES, at - 5 * LANES)
+    ends = bucket_index(jnp.array([-length, length], jnp.int32))
+    bucket = jnp.concatenate([bucket_index(relative), jnp.repeat(ends, LANES)])
+    bucket_of = (bucket[:, None] == jnp.arange(LANES)[None, :]).astype(F32)
+    line_rows = heads + -heads % 4
+    small_rows = line_rows + 2 * (features // LANES)
+    small_rows += -small_rows % 8
+
+    def pair_of(i):
+        i = jnp.minimum(i, pairs - 1)
+        return i % 2 * groups + i // 2
+
+    def column(shape, offset):
+        return pl.BlockSpec(shape, lambda i: (0, offset + pair_of(i)))
+
+    def whole(shape):
+        return pl.BlockSpec(shape, lambda i: (0, 0), pipeline_mode=pl.Buffered(1))
+
+    dma = pltpu.SemaphoreType.DMA
+    units = groups + 1
+    return pl.pallas_call(
+        functools.partial(tail_kernel, rows=rows, ranks=ranks, plane=plane),
+        grid=(pairs + 1,),
+        in_specs=[
+            column((length, LANES), 0),
+            column((length, LANES), pairs),
+            column((length, LANES), 2 * pairs),
+            column((length, LANES), 0),
+            column((length, LANES), 0),
+            pl.BlockSpec((2, length, length), lambda i: (pair_of(i), 0, 0)),
+            column((features, LANES), 0),
+            column((features, LANES), pairs),
+            column((features, LANES), 2 * pairs),
+            whole((length, LANES)),
+            whole((features, length)),
+            whole((length, features)),
+            whole((length, features)),
+            whole((1, features)),
+            whole(dgain.shape),
+            whole(bucket_of.shape),
+            pl.BlockSpec(memory_space=pl.ANY),
+        ],
+        out_specs=[
+            whole((length, features)),
+            whole((slab, groups * late)),
+            whole((slab, early)),
+            whole((small_rows, LANES)),
+        ],
+        out_shape=[
+            jax.ShapeDtypeStruct((length, features), F32),
+            jax.ShapeDtypeStruct((slab, groups * late), F32),
+            jax.ShapeDtypeStruct((slab, early), F32),
+            jax.ShapeDtypeStruct((small_rows, LANES), F32),
+        ],
+        scratch_shapes=[
+            pltpu.VMEM((length, length), BF16),
+            pltpu.VMEM((length, features), F32),
+            pltpu.VMEM((line_rows, 6 * LANES), F32),
+            pltpu.VMEM((2, features, late), F32),
+            pltpu.VMEM((groups, features, late), BF16),
+            pltpu.VMEM((groups, features, late), BF16),
+            pltpu.VMEM((groups, layers, plane, slab, late), BF16),
+            pltpu.VMEM((groups, plane - 1, layers, slab, late), BF16),
+            pltpu.VMEM((groups, layers, slab, late), BF16),
+            pltpu.VMEM((groups, layers - 1, slab, late), BF16),
+            pltpu.VMEM((features, early), BF16),
+            pltpu.VMEM((features, early), BF16),
+            pltpu.VMEM((layers, plane, slab, early), BF16),
+            pltpu.VMEM((plane - 1, layers, slab, early), BF16),
+            pltpu.VMEM((layers, slab, early), BF16),
+            pltpu.VMEM((layers - 1, slab, early), BF16),
+            pltpu.VMEM((small_rows, LANES), F32),
+            pltpu.VMEM((2 * ranks, small_rows, LANES), F32),
+            dma((1,)),
+            dma((units,)),
+            dma((units,)),
+            dma((units, plane)),
+            dma((units, plane)),
+            dma((units, layers)),
+            dma((units, layers)),
+            dma((2 * ranks,)),
+            dma((2 * ranks,)),
+        ],
+        compiler_params=pltpu.CompilerParams(
+            collective_id=2, has_side_effects=True, vmem_limit_bytes=62 * MIB
+        ),
+        cost_estimate=pl.CostEstimate(
+            flops=36 * heads * length * length * HEAD,
+            bytes_accessed=2 * heads * length * length + 30 * length * features,
+            transcendentals=0,
+        ),
+    )(
+        projected, projected, projected, attended, datt, kept, qkv_weight, qkv_weight, qkv_weight,
+        tile_of, normed_turned, tokens, dres, gain, dgain, bucket_of, first,
+    )
+
+
 def core_sum(values, dim):
     half = values.shape[dim] // 2
     core = lax.axis_index("group")
@@ -611,6 +1042,9 @@
     made_back = exchange(made)
     grad_router = drouter[:, :expert_count]
 
+    def finish():
+        return (residual_one + gate_value[:, None] * unpack(made_back)).astype(BF16)
+
     dhidden = unpack(dmoved_back)
     upstream = cotangent.astype(F32)
     _, back_two = jax.vjp(norm_rows, residual_one, gain_rows[1])
@@ -618,6 +1052,38 @@
     dres = upstream + dres_norm
     dbranch = dres.astype(BF16)
     datt = lax.dot_general(dbranch, out_weight, NT, preferred_element_type=F32).astype(BF16)
+    experts = lax.axis_size("expert")
+    cores = lax.axis_size("group")
+    slab = features // experts
+    gain_at = (core, me * slab)
+    if experts == 16 and cores == 2 and expert_count <= 2 * LANES and features % (16 * experts) == 0:
+        dense_out = jnp.einsum(
+            "td,tce->cde",
+            attended,
+            dbranch.reshape(length, cores, features // cores),
+            preferred_element_type=F32,
+        )
+        router_half = jnp.moveaxis(grad_router.reshape(features, cores, -1), 1, 0)
+        router_half = jnp.pad(router_half, ((0, 0), (0, 0), (0, LANES - router_half.shape[2])))
+        first = jnp.concatenate([dense_out, router_half], axis=2).astype(BF16)
+        grad_tokens, grad_qkv, early, small = run_tail(
+            projected, attended, datt, kept, qkv_weight, normed_in.T, tokens, dres, gain_rows[:1],
+            dgain_two.reshape(-1, LANES), first, experts, bucket_count, rows,
+        )
+        heads = rel_bias.shape[1]
+        gain_sums = small[heads + -heads % 4 :][: 2 * features // LANES].reshape(2, features)
+        return (
+            finish(),
+            grad_tokens,
+            lax.dynamic_slice(gain_sums, gain_at, (2 // cores, slab)),
+            grad_qkv,
+            early[:, : features // cores],
+            small[:heads, :bucket_count].T,
+            early[:, features // cores : features // cores + expert_count // cores],
+            grad_first[None],
+            grad_second[None],
+        )
+
     grad_out = lax.dot_general(attended, dbranch, TN, preferred_element_type=F32)
     dqkv, band, far = attend_back(projected, attended, datt, kept, rows)
     grad_proj = jnp.einsum("td,cte->dce", normed_in, dqkv, preferred_element_type=F32)
@@ -632,9 +1098,6 @@
     dinput_norm, dgain_one = back_one(dnormed)
     grad_tokens = dres + dinput_norm
 
-    brought = unpack(made_back)
-    output = (residual_one + gate_value[:, None] * brought).astype(BF16)
-
     def scattered(values):
         return lax.psum_scatter(
             core_sum(values, 1).astype(BF16), "expert", scatter_dimension=0, tiled=True
@@ -651,18 +1114,14 @@
     for s in small:
         summed.append(flat[at : at + s.size].reshape(s.shape))
         at += s.size
-    experts = lax.axis_size("expert")
-    cores = lax.axis_size("group")
-    grad_gains = lax.dynamic_slice(
-        summed[0], (core, me * (features // experts)), (2 // cores, features // experts)
-    )
+    grad_gains = lax.dynamic_slice(summed[0], gain_at, (2 // cores, slab))
     grad_router = lax.dynamic_slice(
         summed[1],
-        (me * (features // experts), core * (expert_count // cores)),
-        (features // experts, expert_count // cores),
+        (me * slab, core * (expert_count // cores)),
+        (slab, expert_count // cores),
     )
     return (
-        output,
+        finish(),
         grad_tokens,
         grad_gains,
         scattered(grad_proj),

time: 624 us -> 401 us (0.64)
  waiting for transfers between devices: 174 us -> 12 us
  Pallas kernels: 226 us -> 276 us
  blocking collectives: 41.5 us -> 0 us
  matrix products: 65 us -> 43.1 us
  local copies, waits for them, and re-layouts: 41.4 us -> 23.4 us
  other arithmetic: 23.1 us -> 8.76 us
  between operations: 15.4 us -> 1.93 us
    reduce_scatter x2 -> x0, waiting for transfers between devices: 163 us -> none  [scattered(): lax.psum_scatter(core_sum(values, 1).astype(BF16), 'expert', scatter_dime...]
    pallas_call x1, Pallas kernels: 27.7 us -> 77.4 us  [run_tail(): pl.pallas_call(functools.partial(tail_kernel, rows=rows, ranks=ranks, pla...]
    psum x1 -> x0, blocking collectives: 41.5 us -> none  [per_device(): lax.psum(jnp.concatenate([s.reshape(-1) for s in small]), ('group', 'expe...]
    unnamed x76 -> x60, local copies, waits for them, and re-layouts: 33.2 us -> 9.94 us
    dot_general x4 -> x1, matrix products: 25.1 us -> 2.86 us  [per_device(): jnp.einsum('td,tce->cde', attended, dbranch.reshape(length, cores, featur...]
    add x3 -> x0, other arithmetic: 6.71 us -> none  [the longest x1 5.36 us: per_device(): grad_tokens = dres + dinput_norm]
  transfers between devices with their start and end apart: 6 -> 2, of which waited for: 4 -> 1; matrix products, arithmetic and copies ran while one was open for 15% -> 11% of each run, Pallas kernels for 10% -> 28%
where the time goes in v3:
time: 401 us; the launch traced here: 398 us
  Pallas kernels  276 us (69%)
  matrix products  43.1 us (11%)
  starting transfers between devices  32.4 us (8%)
  local copies, waits for them, and re-layouts  23.4 us (6%)
  waiting for transfers between devices  12 us (3%)
  other arithmetic  8.76 us (2%)
    pallas_call x1, Pallas kernels, run_expert(): pl.pallas_call(functools.partial(expert_kernel, ranks=ranks, expert_count...  163 us
    pallas_call x1, Pallas kernels, run_tail(): pl.pallas_call(functools.partial(tail_kernel, rows=rows, ranks=ranks, pla...  77.4 us
    pallas_call x1, Pallas kernels, attend(): pl.pallas_call(functools.partial(attend_kernel, rows=rows), grid=(pairs,)...  35.3 us
    all_to_all x2, starting transfers between devices, exchange(): lax.all_to_all(values, 'expert', split_axis=0, concat_axis=0, tiled=True)  32.4 us
    dot_general x2, matrix products, unpack(): lax.dot_general(picks, values.reshape(-1, features), TN, preferred_elemen...  14.9 us
    all_to_all x2, waiting for transfers between devices, exchange(): lax.all_to_all(values, 'expert', split_axis=0, concat_axis=0, tiled=True)  12 us
    dot_general x2, matrix products, pack(): packed = jnp.dot(picks, values, preferred_element_type=F32).astype(BF16)  11.5 us
    unnamed x60, local copies, waits for them, and re-layouts  9.94 us
  transfers between devices with their start and end apart: 2, of which 1 were waited for; matrix products, arithmetic and copies ran while one was open for 11% of the time, Pallas kernels for 28%

profile of v3, /device:TPU:0, one launch (start us, length us, event | category | flops | bytes accessed | tf_op | source)
XLA Modules:
  0.0 397.6 jit_solution(15876513299959843685)
XLA Ops:
  0.6 0.0 copy-start
  1.3 1.3 fusion.26
  2.6 0.7 add_select_fusion.1
  3.3 6.5 %fusion.9 = bf16[2048,768]{1,0:T(8,128)(2,1)} fusion(bf16[1024,768]{1,0:T(8,128)(2,1)} %param.22, s32[1024]{0:T(1024)S(1)} %add_select_fusion.1), kind=kOutput, calls=%fused_computation.16 | convolution fusion | flops 3224895488 | bytes 4722688 | tf_op jit(solution)/shard_map/dot_general | solution.py:1014
  9.8 8.7 %all-to-all-start = ((bf16[16,128,768]{2,1,0:T(8,128)(2,1)}), bf16[16,128,768]{2,1,0:T(8,128)(2,1)}, u32[]{:S(2)}, u32[]{:S(2)}) async-start(bf16[16,128,768]{2,1,0:T(8,128)(2,1)} %bitcast.50), calls=%async_computation | async-start | bytes 6291456 | tf_op jit(solution)/shard_map/all_to_all | solution.py:985
  18.5 0.0 copy-done.16
  18.5 0.2 convolution_bitcast_fusion
  18.7 0.1 broadcast_in_dim.14.line_ref
  18.8 0.0 copy-done.12
  18.8 0.2 copy.30
  18.9 0.7 pad.9.router_ref
  19.7 0.4 fusion.11
  20.1 7.7 %convolution_convert_fusion.q_ref.k_ref.v_ref = bf16[1024,2304]{1,0:T(8,128)(2,1)} fusion(bf16[768,2304]{1,0:T(8,128)(2,1)} %wv_ref.1, bf16[1024,768]{1,0:T(8,128)(2,1)S(1)} %copy-done.6, f32[768]{0:T(1024)S(1)} %get-tuple-element.56, f32[1024]{0:T(1024)S(1)} %add_rsqrt_fusion), kind=kOutput, calls=%fused_computation.5 | convolution fusion | flops 3629383680 | bytes 9837568 | tf_op jit(solution)/shard_map/dot_general | solution.py:1026
  27.8 35.3 %shard_map.187 = (bf16[1024,768]{1,0:T(8,128)(2,1)S(1)}, bf16[12,1024,1024]{2,1,0:T(8,128)(2,1)}) custom-call(bf16[1024,2304]{1,0:T(8,128)(2,1)} %convolution_convert_fusion.q_ref.k_ref.v_ref, bf16[1024,2304]{1,0:T(8,128)(2,1)} %convolution_convert_fusion.q_ref.k_ref.v_ref, bf16[1024,2304]{1,0:T(8,128)(2,1)} %convolution_convert_fusion.q_ref.k_ref.v_ref, ...), custom_call_target="tpu_custom_call" | custom-call | flops 12884901888 | bytes 31457280 | tf_op jit(solution)/shard_map/pallas_call | solution.py:65
  63.2 1.5 multiply_reduce_fusion.2
  64.7 0.0 copy-start.4
  64.7 0.0 copy-start.14
  64.7 0.0 copy-start.22
  64.8 0.3 multiply_convert_fusion
  65.1 0.5 fusion.54
  65.6 0.7 copy-done.4
  66.4 0.1 broadcast_bitcast_fusion
  66.5 0.9 fusion.27.tile_ref
  67.4 12.0 %all-to-all-done.cot_ref = bf16[16,128,768]{2,1,0:T(8,128)(2,1)} async-done(((bf16[16,128,768]{2,1,0:T(8,128)(2,1)}), bf16[16,128,768]{2,1,0:T(8,128)(2,1)}, u32[]{:S(2)}, u32[]{:S(2)}) %all-to-all-start) | async-done | bytes 3145760 | tf_op jit(solution)/shard_map/all_to_all | solution.py:985
  79.4 5.1 %fusion.10 = bf16[2048,768]{1,0:T(8,128)(2,1)} fusion(bf16[1024,768]{1,0:T(8,128)(2,1)S(1)} %multiply_convert_fusion, s32[1024]{0:T(1024)S(1)} %add_select_fusion.1), kind=kOutput, calls=%fused_computation.17 | convolution fusion | flops 3224895488 | bytes 4722688 | tf_op jit(solution)/shard_map/dot_general | solution.py:1014
  84.5 163.3 %shard_map.188 = (bf16[16,128,768]{2,1,0:T(8,128)(2,1)}, bf16[16,128,768]{2,1,0:T(8,128)(2,1)}, f32[768,1536]{1,0:T(8,128)}, f32[1536,768]{1,0:T(8,128)}, f32[768,128]{1,0:T(8,128)}) custom-call(bf16[16,128,768]{2,1,0:T(8,128)(2,1)} %bitcast.60, bf16[16,128,768]{2,1,0:T(8,128)(2,1)} %all-to-all-done.cot_ref, bf16[768,3072]{1,0:T(8,128)(2,1)} %bitcast.57, ...), custom_call_target="tpu_custom_call" | custom-call | flops 57982058496 | bytes 31457280 | tf_op jit(solution)/shard_map/pallas_call | solution.py:492
  247.8 0.0 copy-start.13
  247.8 0.0 copy-start.5
  247.8 23.7 %all-to-all-start.1 = ((bf16[16,128,768]{2,1,0:T(8,128)(2,1)}), bf16[16,128,768]{2,1,0:T(8,128)(2,1)}, u32[]{:S(2)}, u32[]{:S(2)}) async-start(bf16[16,128,768]{2,1,0:T(8,128)(2,1)} %get-tuple-element.25), calls=%async_computation.1 | async-start | bytes 6291456 | tf_op jit(solution)/shard_map/all_to_all | solution.py:985
  271.6 0.6 slice.31.gain_ref
  272.2 0.6 select_reduce_fusion
  272.8 0.9 fusion.30.bucket_ref
  273.8 1.0 slice.38
  274.8 0.7 copy.35
  275.5 1.0 copy.36
  276.5 0.0 copy-start.15
  276.5 0.0 copy-start.7
  276.5 0.0 copy-start.10
  276.5 7.2 %multiply_reduce_fusion = (f32[768]{0:T(1024)}, f32[1024]{0:T(1024)S(1)}, f32[1024,768]{1,0:T(8,128)S(1)}) fusion(f32[1024,768]{1,0:T(8,128)S(1)} %copy-done.5, f32[1024]{0:T(1024)S(1)} %fusion.47, f32[768]{0:T(1024)S(1)} %get-tuple-element.55, bf16[2048,768]{1,0:T(8,128)(2,1)} %bitcast.59, s32[1024]{0:T(1024)} %copy-done.17), kind=kOutput, calls=%fused_computation.23 | convolution fusion | flops 3228039424 | bytes 9455616 | tf_op jit(solution)/shard_map/dot_general | solution.py:1018
  283.8 3.4 fusion.52
  287.2 2.7 copy.37.normed_ref
  290.0 1.7 copy.42
  291.6 2.9 fusion.22
  294.5 0.0 copy-start.21
  294.5 1.4 fusion.16.first_ref
  295.9 0.2 copy-done.21
  296.1 2.6 convolution_convert_fusion.1.dout_ref
  298.7 77.4 %shard_map.189 = (f32[1024,768]{1,0:T(8,128)}, f32[48,1152]{1,0:T(8,128)}, f32[48,512]{1,0:T(8,128)}, f32[24,128]{1,0:T(8,128)}) custom-call(bf16[1024,2304]{1,0:T(8,128)(2,1)} %convolution_convert_fusion.q_ref.k_ref.v_ref, bf16[1024,2304]{1,0:T(8,128)(2,1)} %convolution_convert_fusion.q_ref.k_ref.v_ref, ...), custom_call_target="tpu_custom_call" | custom-call | flops 28991029248 | bytes 48758784 | tf_op jit(solution)/shard_map/pallas_call | solution.py:899
  376.1 0.7 slice.30
  376.8 1.5 slice.28
  378.3 0.7 slice.27
  379.1 0.7 copy.38
  379.7 0.6 dynamic_slice.3
  380.3 1.3 slice_bitcast_fusion
  381.6 0.0 all-to-all-done.1
  381.6 0.0 slice-start.3
  381.6 7.6 %add_convert_fusion = bf16[1024,768]{1,0:T(8,128)(2,1)} fusion(f32[1024,768]{1,0:T(8,128)} %copy-done.4, bf16[2048,768]{1,0:T(8,128)(2,1)} %bitcast.7, s32[1024]{0:T(1024)S(1)} %copy-done.18, f32[1024]{0:T(1024)S(1)} %copy-done.19), kind=kOutput, calls=%fused_computation.25 | convolution fusion | flops 3225681920 | bytes 7872512 | tf_op jit(solution)/shard_map/dot_general | solution.py:1018
  389.3 1.7 copy.48
  391.0 0.7 copy.49
  391.7 0.0 copy-start.1
  391.7 2.4 copy.50
  394.1 0.7 slice-done
  394.8 0.4 slice-done.1
  395.2 2.2 copy.51
  (49 shorter events, 0.2 us)
Async XLA Ops:
  0.6 17.9 %copy-start = (bf16[32,12]{0,1:T(8,128)(2,1)S(1)}, bf16[32,12]{0,1:T(8,128)(2,1)}, u32[]{:S(2)}) copy-start(bf16[32,12]{0,1:T(8,128)(2,1)} %param.16) | copy-start | bytes 2308
  3.3 76.1 %copy-start.17 = (s32[1024]{0:T(1024)}, s32[1024]{0:T(1024)S(1)}, u32[]{:S(2)}) copy-start(s32[1024]{0:T(1024)S(1)} %add_select_fusion.1) | copy-start | bytes 12292
  9.8 8.7 %copy-start.16 = (bf16[2,768]{1,0:T(2,128)(2,1)S(1)}, bf16[2,768]{1,0:T(2,128)(2,1)}, u32[]{:S(2)}) copy-start(bf16[2,768]{1,0:T(2,128)(2,1)} %param.13) | copy-start | bytes 9220
  9.8 9.0 %copy-start.12 = (bf16[768,16]{0,1:T(8,128)(2,1)S(1)}, bf16[768,16]{0,1:T(8,128)(2,1)}, u32[]{:S(2)}) copy-start(bf16[768,16]{0,1:T(8,128)(2,1)} %param.17) | copy-start | bytes 73732
  9.8 9.9 %copy-start.6 = (bf16[1024,768]{1,0:T(8,128)(2,1)S(1)}, bf16[1024,768]{1,0:T(8,128)(2,1)}, u32[]{:S(2)}) copy-start(bf16[1024,768]{1,0:T(8,128)(2,1)} %tokens_ref.1) | copy-start | bytes 4718596
  9.8 69.6 %all-to-all-start = ((bf16[16,128,768]{2,1,0:T(8,128)(2,1)}), bf16[16,128,768]{2,1,0:T(8,128)(2,1)}, u32[]{:S(2)}, u32[]{:S(2)}) async-start(bf16[16,128,768]{2,1,0:T(8,128)(2,1)} %bitcast.50), calls=%async_computation | async-start | bytes 6291456 | tf_op jit(solution)/shard_map/all_to_all | solution.py:985
  27.8 35.3 %copy-start.20 = (bf16[768,768]{1,0:T(8,128)(2,1)S(1)}, bf16[768,768]{1,0:T(8,128)(2,1)}, u32[]{:S(2)}) copy-start(bf16[768,768]{1,0:T(8,128)(2,1)} %param.15) | copy-start | bytes 3538948
  63.2 1.5 copy-start.2
  64.7 1.7 copy-start.4
  64.7 1.7 copy-start.14
  64.7 1.7 copy-start.22
  247.8 24.4 %copy-start.13 = (s32[1024,1]{0,1:T(1,128)S(1)}, s32[1024,1]{0,1:T(1,128)}, u32[]{:S(2)}) copy-start(s32[1024,1]{0,1:T(1,128)} %param.20) | copy-start | bytes 12292
  247.8 28.7 %copy-start.5 = (f32[1024,768]{1,0:T(8,128)S(1)}, f32[1024,768]{1,0:T(8,128)}, u32[]{:S(2)}) copy-start(f32[1024,768]{1,0:T(8,128)} %copy-done.4) | copy-start | bytes 9437188
  247.8 133.8 %all-to-all-start.1 = ((bf16[16,128,768]{2,1,0:T(8,128)(2,1)}), bf16[16,128,768]{2,1,0:T(8,128)(2,1)}, u32[]{:S(2)}, u32[]{:S(2)}) async-start(bf16[16,128,768]{2,1,0:T(8,128)(2,1)} %get-tuple-element.25), calls=%async_computation.1 | async-start | bytes 6291456 | tf_op jit(solution)/shard_map/all_to_all | solution.py:985
  276.5 7.3 %copy-start.15 = (f32[1024]{0:T(1024)S(1)}, f32[1024]{0:T(1024)}, u32[]{:S(2)}) copy-start(f32[1024]{0:T(1024)} %copy-done.14) | copy-start | bytes 12292
  276.5 7.3 %copy-start.7 = (bf16[1024,768]{1,0:T(8,128)(2,1)S(1)}, bf16[1024,768]{1,0:T(8,128)(2,1)}, u32[]{:S(2)}) copy-start(bf16[1024,768]{1,0:T(8,128)(2,1)} %tokens_ref.1) | copy-start | bytes 4718596
  276.5 7.3 %copy-start.10 = (bf16[1024,768]{1,0:T(8,128)(2,1)S(1)}, bf16[1024,768]{1,0:T(8,128)(2,1)}, u32[]{:S(2)}) copy-start(bf16[1024,768]{1,0:T(8,128)(2,1)} %param.22) | copy-start | bytes 4718596
  287.2 2.7 copy-start.8
  287.2 4.4 %copy-start.3 = (bf16[1024,768]{1,0:T(8,128)(2,1)S(1)}, bf16[1024,768]{1,0:T(8,128)(2,1)}, u32[]{:S(2)}) copy-start(bf16[1024,768]{1,0:T(8,128)(2,1)} %copy-done.2) | copy-start | bytes 4718596
  294.5 1.6 copy-start.21
  298.7 82.9 %copy-start.18 = (s32[1024]{0:T(1024)S(1)}, s32[1024]{0:T(1024)}, u32[]{:S(2)}) copy-start(s32[1024]{0:T(1024)} %copy-done.17) | copy-start | bytes 12292
  298.7 82.9 %copy-start.19 = (f32[1024]{0:T(1024)S(1)}, f32[1024]{0:T(1024)}, u32[]{:S(2)}) copy-start(f32[1024]{0:T(1024)} %select_reduce_fusion) | copy-start | bytes 12292
  381.6 10.0 %slice-start.2 = ((s8[4718592]{0:T(1024)(128)(4,1)}), s8[4194304]{0:T(1024)(128)(4,1)S(1)}, s32[]{:S(2)}) async-start(s8[4718592]{0:T(1024)(128)(4,1)} %bitcast.47), calls=%async_computation.4 | async-start | bytes 8388608
  381.6 7.7 %copy-start.9 = (f32[1024,768]{1,0:T(8,128)S(1)}, f32[1024,768]{1,0:T(8,128)}, u32[]{:S(2)}) copy-start(f32[1024,768]{1,0:T(8,128)} %get-tuple-element.75) | copy-start | bytes 9437188
  381.6 10.0 %slice-start.3 = ((s8[4718592]{0:T(1024)(128)(4,1)}), s8[524288]{0:T(1024)(128)(4,1)S(1)}, s32[]{:S(2)}) async-start(s8[4718592]{0:T(1024)(128)(4,1)} %bitcast.47), calls=%async_computation.5 | async-start | bytes 1048576
  389.3 1.7 copy-start.11
  391.0 3.8 slice-start
  391.6 3.5 slice-start.1
  391.7 5.7 %copy-start.1 = (bf16[32,12]{0,1:T(8,128)(2,1)S(1)}, bf16[32,12]{0,1:T(8,128)(2,1)}, u32[]{:S(2)}) copy-start(bf16[32,12]{0,1:T(8,128)(2,1)} %param.16) | copy-start | bytes 2308

commit v4 on v3

--- a/solution.py
+++ b/solution.py
@@ -370,7 +370,7 @@
             k = first_rank + inner
             made_copy(k).start()
 
-            @pl.when(k > 0)
+            @pl.when((k > 0) & (k < plane))
             def _(k=k):
                 moved_copy(k).start()
 
@@ -381,6 +381,12 @@
         return carry
 
     lax.fori_loop(0, ranks // per_step, step, 0)
+
+    def start_moved(k, carry):
+        moved_copy(k).start()
+        return carry
+
+    lax.fori_loop(plane, ranks, start_moved, 0)
 
     other = 1 - core
     across = features // columns
@@ -543,21 +549,22 @@
 
 
 def tail_kernel(
-    q_ref, k_ref, v_ref, out_ref, dout_ref, kept_ref, wq_ref, wk_ref, wv_ref, tile_ref,
-    normed_ref, tokens_ref, dres_ref, gain_ref, dgain_ref, bucket_ref, first_ref,
-    tokens_grad_ref, dense_ref, early_ref, small_ref,
+    q_ref, k_ref, v_ref, kept_ref, wq_ref, wk_ref, wv_ref, tile_ref, gain_ref, bucket_ref,
+    drouter_ref, target_ref, gate_ref, normed_hbm, tokens_hbm, cot_hbm, residual_hbm, attended_hbm,
+    out_weight_hbm, moved_hbm, made_hbm,
+    tokens_grad_ref, dense_ref, early_ref, router_ref, small_ref, output_hbm, came_hbm,
+    normed, narrow, attended, out_weight, slots, datt,
     dscores, dnormed, lines, own, core_out, core_in, plane_out, plane_in, layer_out, layer_in,
-    early_core, early_own, early_plane_out, early_plane_in, early_layer_out, early_layer_in,
-    small_out, small_in, load_sem, core_sent, core_came, plane_sent, plane_came, layer_sent,
-    layer_came, small_sent, small_came, *, rows, ranks, plane,
+    early_out, early_core, early_own, early_plane_out, early_plane_in, early_layer_out,
+    early_layer_in, small_out, small_in, load_sem, made_sent, made_came, core_sent, core_came,
+    plane_sent, plane_came, layer_sent, layer_came, small_sent, small_came, *, rows, ranks, plane,
 ):
-    length, features = tokens_ref.shape
+    length, features = narrow.shape
     tiles = length // LANES
     inner = rows // LANES
     layers = ranks // plane
-    slab = features // ranks
-    heads = 2 * (pl.num_programs(0) - 1)
-    groups = (pl.num_programs(0) - 1) // 2
+    groups = (pl.num_programs(0) - 2) // 2
+    per_slot = slots.shape[0] // ranks
     step = pl.program_id(0)
     core, me = lax.axis_index("group"), lax.axis_index("expert")
     other = 1 - core
@@ -576,7 +583,7 @@
     def core_copy(unit):
         early = unit == 0
         return pltpu.make_async_remote_copy(
-            src_ref=first_ref.at[other] if early else core_out.at[unit - 1],
+            src_ref=early_out if early else core_out.at[unit - 1],
             dst_ref=early_core if early else core_in.at[unit - 1],
             send_sem=core_sent.at[unit],
             recv_sem=core_came.at[unit],
@@ -608,26 +615,81 @@
             device_id_type=mesh,
         )
 
-    def peer(number):
-        return (core + number // ranks) % 2, (me + number) % ranks
-
     def small_copy(number):
+        if number == 0:
+            there = (other, me)
+        elif number < plane:
+            there = (core, rank_of(layer, in_plane(number, 1)))
+        else:
+            there = (core, rank_of(in_line(number - plane + 1, 1), spot))
         return pltpu.make_async_remote_copy(
-            src_ref=small_out,
+            src_ref=small_out.at[min(number, 1) + number // plane],
             dst_ref=small_in.at[number],
             send_sem=small_sent.at[number],
             recv_sem=small_came.at[number],
-            device_id=peer(number),
+            device_id=there,
             device_id_type=mesh,
         )
 
-    def own_load():
-        return pltpu.make_async_copy(first_ref.at[core], early_own, load_sem.at[0])
+    def small_start(stage, first, end):
+        for number in range(first, end):
+            small_copy(number).start()
+
+    def small_add(stage, first, end):
+        total = small_out[stage]
+        for number in range(first, end):
+            small_copy(number).wait_recv()
+            total = total + small_in[number]
+        return total
+
+    def partner(number):
+        return rank_of(in_line(number // plane, 1), in_plane(number % plane, 1))
+
+    def made_copy(number):
+        return pltpu.make_async_remote_copy(
+            src_ref=made_hbm.at[partner(number)],
+            dst_ref=came_hbm.at[me],
+            send_sem=made_sent.at[number],
+            recv_sem=made_came.at[number],
+            device_id=(core, partner(number)),
+            device_id_type=mesh,
+        )
+
+    def load(source, target, number):
+        return pltpu.make_async_copy(source, target, load_sem.at[number])
+
+    def moved_load(number):
+        part = pl.ds(pl.multiple_of(number * per_slot, per_slot), per_slot)
+        return pltpu.make_async_copy(moved_hbm.at[number], slots.at[part], load_sem.at[8])
+
+    def came_load(number):
+        part = pl.ds(pl.multiple_of(number * per_slot, per_slot), per_slot)
+        return pltpu.make_async_copy(came_hbm.at[number], slots.at[part], load_sem.at[9])
+
+    def own_made():
+        return load(made_hbm.at[me], came_hbm.at[me], 7)
+
+    def each(first, last, action):
+        def run(number, carry):
+            action(number)
+            return carry
+
+        lax.fori_loop(first, last, run, 0)
+
+    def taken(block):
+        total = jnp.zeros((rows, features), F32)
+        width = 4 * LANES
+        for first in range(0, slots.shape[0], width):
+            at = first + lax.broadcasted_iota(jnp.int32, (1, width), 1)
+            picks = (target_ref[block, :] == at).astype(F32).astype(BF16)
+            total = total + jnp.dot(
+                picks, slots[first : first + width, :], preferred_element_type=F32
+            )
+        return total
 
     def sum_cores(unit):
         core_copy(unit).wait_recv()
         if unit == 0:
-            own_load().wait()
             summed = early_own[...].astype(F32) + early_core[...].astype(F32)
             early_plane_out[...] = summed.astype(BF16).reshape(early_plane_out.shape)
         else:
@@ -656,7 +718,8 @@
             came = early_layer_in[k - 1] if unit == 0 else layer_in[unit - 1, k - 1]
             summed = summed + came.astype(F32)
         if unit == 0:
-            early_ref[...] = summed
+            early_ref[...] = summed[:, : early_ref.shape[1]]
+            router_ref[...] = summed[:, early_ref.shape[1] :]
         else:
             group = unit - 1
             base = core * (groups * LANES)
@@ -670,25 +733,84 @@
 
     @pl.when(step == 0)
     def _():
-        own_load().start()
+        each(0, ranks, lambda number: moved_load(number).start())
+        load(residual_hbm, dnormed, 0).start()
+        load(cot_hbm, narrow, 1).start()
+        load(out_weight_hbm, out_weight, 2).start()
+        load(attended_hbm, attended, 3).start()
+        load(normed_hbm, normed, 4).start()
+        own_made().start()
         barrier = pltpu.get_barrier_semaphore()
-
-        def greet(number, carry):
-            pl.semaphore_signal(barrier, inc=1, device_id=peer(number), device_id_type=mesh)
-            return carry
-
-        lax.fori_loop(1, 2 * ranks, greet, 0)
+        each(
+            1,
+            ranks,
+            lambda number: pl.semaphore_signal(
+                barrier, inc=1, device_id=(core, partner(number)), device_id_type=mesh
+            ),
+        )
+        pl.semaphore_signal(barrier, inc=1, device_id=(other, me), device_id_type=mesh)
+        pl.semaphore_wait(barrier, ranks)
+
+    middle = min(3 * plane, ranks)
+    for now, (first, end) in enumerate(((plane, middle), (middle, ranks), (1, plane))):
+
+        @pl.when(step == now)
+        def _(first=first, end=end):
+            each(first, end, lambda number: made_copy(number).start())
+
+    @pl.when(step == 0)
+    def _():
+        each(0, ranks, lambda number: moved_load(number).wait())
+        load(residual_hbm, dnormed, 0).wait()
+        load(cot_hbm, narrow, 1).wait()
+        load(out_weight_hbm, out_weight, 2).wait()
+
+        def branch(number, dgain):
+            block = pl.ds(pl.multiple_of(number * rows, rows), rows)
+            back = taken(block)
+            residual = dnormed[block, :]
+            spread = lax.rsqrt(jnp.mean(residual * residual, axis=1, keepdims=True) + EPSILON)
+            scaled = residual * spread
+            moved = back * gain_ref[1:2, :]
+            dres = narrow[block, :].astype(F32) + spread * (
+                moved - scaled * jnp.mean(moved * scaled, axis=1, keepdims=True)
+            )
+            tokens_grad_ref[block, :] = dres
+            dbranch = dres.astype(BF16)
+            dscores[block, :features] = dbranch
+            datt[block, :] = lax.dot_general(
+                dbranch, out_weight[...], NT, preferred_element_type=F32
+            ).astype(BF16)
+            return dgain + jnp.sum(back * scaled, axis=0, keepdims=True)
+
+        dgain = lax.fori_loop(0, length // rows, branch, jnp.zeros((1, features), F32))
+        for part in range(features // LANES):
+            at = lines.shape[0] + features // LANES + part
+            small_out[0, at : at + 1, :] = dgain[:, part * LANES : (part + 1) * LANES]
+        load(attended_hbm, attended, 3).wait()
+        load(normed_hbm, normed, 4).wait()
+        load(tokens_hbm, narrow, 5).start()
+        dense = lax.dot_general(
+            attended[...], dscores[:, :features], TN, preferred_element_type=F32
+        )
+        half = features // 2
+        early_own[:, :half] = jnp.where(core == 0, dense[:, :half], dense[:, half:]).astype(BF16)
+        early_out[:, :half] = jnp.where(core == 0, dense[:, half:], dense[:, :half]).astype(BF16)
+        drouter = drouter_ref[...].astype(BF16)
+        early_own[:, half:] = drouter
+        early_out[:, half:] = drouter
+        core_copy(0).start()
         dnormed[...] = jnp.zeros_like(dnormed)
-        pl.semaphore_wait(barrier, 2 * ranks - 1)
-        core_copy(0).start()
-
-    @pl.when(step < 2 * groups)
+
+    @pl.when((step > 0) & (step <= 2 * groups))
     def _():
         lane = lax.broadcasted_iota(jnp.int32, (1, LANES), 1)
-        queries, values, dout = q_ref[...], v_ref[...], dout_ref[...]
+        pair = (step - 1) % 2 * groups + (step - 1) // 2
+        columns = pl.ds(pl.multiple_of(pair * LANES, LANES), LANES)
+        queries, values, dout = q_ref[...], v_ref[...], datt[:, columns]
         widened = jnp.concatenate([k_ref[...], tile_ref[...]], axis=1)
         dout_wide = dout.astype(F32)
-        product = dout_wide * out_ref[...].astype(F32)
+        product = dout_wide * attended[:, columns].astype(F32)
         dout_turned, queries_turned = dout.T, queries.T
         mirror = (
             lax.broadcasted_iota(jnp.int32, (LANES, LANES), 0)
@@ -733,7 +855,6 @@
             )
             band = pltpu.roll(band, 3 * LANES + 1, 1, stride=1, stride_axis=0)
             near = jnp.sum(band, axis=0, keepdims=True)
-            pair = step % 2 * groups + step // 2
             lines[pl.ds(2 * pair + head, 1), :] = jnp.concatenate([near, before, after], axis=1)
             half = slice(HEAD * head, HEAD * head + HEAD)
             dkeys.append(
@@ -753,12 +874,12 @@
         joined = jnp.concatenate([dq, dk, dv], axis=1)
         weights = jnp.concatenate([wq_ref[...], wk_ref[...], wv_ref[...]], axis=1)
         dnormed[...] += lax.dot_general(joined, weights, NT, preferred_element_type=F32)
-        dense = jnp.dot(normed_ref[...], joined, preferred_element_type=F32)
+        dense = jnp.dot(normed[...], joined, preferred_element_type=F32)
         dwq, dwk, dwv = dense[:, :LANES], dense[:, LANES : 2 * LANES], dense[:, 2 * LANES :]
         own_first, away_first = jnp.where(core == 0, dwq, dwv), jnp.where(core == 0, dwv, dwq)
         for now in range(2 * groups):
 
-            @pl.when(step == now)
+            @pl.when(step == now + 1)
             def _(now=now):
                 unit, part = now // 2 + 1, now % 2
                 at = slice(part * LANES, (part + 1) * LANES)
@@ -776,13 +897,12 @@
                 if part == 1:
                     core_copy(unit).start()
 
-    last = 2 * groups
+    last = 2 * groups + 1
     plan = {}
     for unit in range(groups + 1):
-        made = 0 if unit == 0 else 2 * unit - 1
-        plan.setdefault(min(made + 1, last), []).append((sum_cores, unit))
-        plan.setdefault(min(made + 3, last), []).append((sum_planes, unit))
-        plan.setdefault(min(made + 5, last), []).append((sum_layers, unit))
+        plan.setdefault(min(2 * unit + 1, last), []).append((sum_cores, unit))
+        plan.setdefault(min(2 * unit + 4, last), []).append((sum_planes, unit))
+        plan.setdefault(last, []).append((sum_layers, unit))
     order = [sum_layers, sum_planes, sum_cores]
     for now in range(1, last):
 
@@ -800,57 +920,62 @@
         for action, unit in todo:
             if action is sum_planes and unit < groups:
                 action(unit)
-        gain = gain_ref[...]
-        inputs = tokens_ref[...].astype(F32)
+        load(tokens_hbm, narrow, 5).wait()
+        gain = gain_ref[0:1, :]
+        inputs = narrow[...].astype(F32)
         spread = lax.rsqrt(jnp.mean(inputs * inputs, axis=1, keepdims=True) + EPSILON)
         back = dnormed[...]
         scaled = inputs * spread
         dgain = jnp.sum(back * scaled, axis=0, keepdims=True)
         moved = back * gain
-        tokens_grad_ref[...] = dres_ref[...] + spread * (
+        tokens_grad_ref[...] = tokens_grad_ref[...] + spread * (
             moved - scaled * jnp.mean(moved * scaled, axis=1, keepdims=True)
         )
         table = jnp.dot(
             lines[...], bucket_ref[...], preferred_element_type=F32, precision=lax.Precision.HIGHEST
         )
-        small_out[0 : lines.shape[0], :] = table
+        small_out[0, 0 : lines.shape[0], :] = table
         base = lines.shape[0]
         wide = features // LANES
         for part in range(wide):
-            small_out[base + part : base + part + 1, :] = dgain[
+            small_out[0, base + part : base + part + 1, :] = dgain[
                 :, part * LANES : (part + 1) * LANES
             ]
-        small_out[base + wide : base + 2 * wide, :] = dgain_ref[...]
-        if small_out.shape[0] > base + 2 * wide:
-            small_out[base + 2 * wide :, :] = jnp.zeros(
-                (small_out.shape[0] - base - 2 * wide, LANES), F32
+        if small_out.shape[1] > base + 2 * wide:
+            small_out[0, base + 2 * wide :, :] = jnp.zeros(
+                (small_out.shape[1] - base - 2 * wide, LANES), F32
             )
 
-        def start_small(number, carry):
-            small_copy(number).start()
-            return carry
-
-        lax.fori_loop(1, 2 * ranks, start_small, 0)
+        small_start(0, 0, 1)
+        load(residual_hbm, dnormed, 6).start()
         for action, unit in todo:
             if action is sum_planes and unit == groups:
                 action(unit)
+        small_out[1] = small_add(0, 0, 1)
+        small_start(1, 1, plane)
+        own_made().wait()
+        each(1, ranks, lambda number: made_copy(number).wait_recv())
+        each(0, ranks, lambda number: came_load(number).start())
+        each(0, ranks, lambda number: came_load(number).wait())
+        load(residual_hbm, dnormed, 6).wait()
+
+        def finish(number, carry):
+            block = pl.ds(pl.multiple_of(number * rows, rows), rows)
+            datt[block, :] = (dnormed[block, :] + gate_ref[block, :] * taken(block)).astype(BF16)
+            return carry
+
+        lax.fori_loop(0, length // rows, finish, 0)
+        load(datt, output_hbm, 10).start()
+        small_out[2] = small_add(1, 1, plane)
+        small_start(2, plane, plane + layers - 1)
         for action, unit in todo:
             if action is sum_layers:
                 action(unit)
-        small_ref[...] = small_out[...]
-
-        def add_small(number, carry):
-            small_copy(number).wait_recv()
-            small_ref[...] += small_in[number]
-            return carry
-
-        lax.fori_loop(1, 2 * ranks, add_small, 0)
-
-        def drop_small(number, carry):
+        small_ref[...] = small_add(2, plane, plane + layers - 1)
+        for number in range(plane + layers - 1):
             small_copy(number).wait_send()
-            return carry
-
-        lax.fori_loop(1, 2 * ranks, drop_small, 0)
+        each(1, ranks, lambda number: made_copy(number).wait_send())
+        load(datt, output_hbm, 10).wait()
         for unit in range(groups + 1):
             core_copy(unit).wait_send()
             for k in range(1, plane):
@@ -860,17 +985,18 @@
 
 
 def run_tail(
-    projected, attended, datt, kept, qkv_weight, normed_turned, tokens, dres, gain, dgain, first, ranks,
-    bucket_count, rows,
+    projected, attended, kept, qkv_weight, out_weight, normed_turned, tokens, cotangent, residual, gains,
+    drouter, target, gate, moved, made, rows,
 ):
     length, features = tokens.shape
     heads = kept.shape[0]
+    ranks = made.shape[0]
     pairs = heads // 2
     groups = pairs // 2
     plane = 4
     layers = ranks // plane
     slab = features // ranks
-    early = first.shape[2]
+    early = features // 2 + LANES
     late = 3 * LANES
     tile_of = (
         jnp.arange(length)[:, None] // LANES == jnp.arange(LANES)[None, :]
@@ -885,7 +1011,7 @@
     small_rows += -small_rows % 8
 
     def pair_of(i):
-        i = jnp.minimum(i, pairs - 1)
+        i = jnp.clip(i - 1, 0, pairs - 1)
         return i % 2 * groups + i // 2
 
     def column(shape, offset):
@@ -895,42 +1021,52 @@
         return pl.BlockSpec(shape, lambda i: (0, 0), pipeline_mode=pl.Buffered(1))
 
     dma = pltpu.SemaphoreType.DMA
+    any_ref = pl.BlockSpec(memory_space=pl.ANY)
     units = groups + 1
     return pl.pallas_call(
         functools.partial(tail_kernel, rows=rows, ranks=ranks, plane=plane),
-        grid=(pairs + 1,),
+        grid=(pairs + 2,),
         in_specs=[
             column((length, LANES), 0),
             column((length, LANES), pairs),
             column((length, LANES), 2 * pairs),
-            column((length, LANES), 0),
-            column((length, LANES), 0),
             pl.BlockSpec((2, length, length), lambda i: (pair_of(i), 0, 0)),
             column((features, LANES), 0),
             column((features, LANES), pairs),
             column((features, LANES), 2 * pairs),
             whole((length, LANES)),
-            whole((features, length)),
-            whole((length, features)),
-            whole((length, features)),
-            whole((1, features)),
-            whole(dgain.shape),
+            whole(gains.shape),
             whole(bucket_of.shape),
-            pl.BlockSpec(memory_space=pl.ANY),
+            whole((features, LANES)),
+            whole((length, 1)),
+            whole((length, 1)),
+            *[any_ref] * 8,
         ],
         out_specs=[
             whole((length, features)),
             whole((slab, groups * late)),
-            whole((slab, early)),
+            whole((slab, features // 2)),
+            whole((slab, LANES)),
             whole((small_rows, LANES)),
+            any_ref,
+            any_ref,
         ],
         out_shape=[
             jax.ShapeDtypeStruct((length, features), F32),
             jax.ShapeDtypeStruct((slab, groups * late), F32),
-            jax.ShapeDtypeStruct((slab, early), F32),
+            jax.ShapeDtypeStruct((slab, features // 2), F32),
+            jax.ShapeDtypeStruct((slab, LANES), F32),
             jax.ShapeDtypeStruct((small_rows, LANES), F32),
+            jax.ShapeDtypeStruct((length, features), BF16),
+            jax.ShapeDtypeStruct(made.shape, BF16),
         ],
         scratch_shapes=[
+            pltpu.VMEM((features, length), BF16),
+            pltpu.VMEM((length, features), BF16),
+            pltpu.VMEM((length, features), BF16),
+            pltpu.VMEM((features, features), BF16),
+            pltpu.VMEM((ranks * made.shape[1], features), BF16),
+            pltpu.VMEM((length, features), BF16),
             pltpu.VMEM((length, length), BF16),
             pltpu.VMEM((length, features), F32),
             pltpu.VMEM((line_rows, 6 * LANES), F32),
@@ -943,21 +1079,24 @@
             pltpu.VMEM((groups, layers - 1, slab, late), BF16),
             pltpu.VMEM((features, early), BF16),
             pltpu.VMEM((features, early), BF16),
+            pltpu.VMEM((features, early), BF16),
             pltpu.VMEM((layers, plane, slab, early), BF16),
             pltpu.VMEM((plane - 1, layers, slab, early), BF16),
             pltpu.VMEM((layers, slab, early), BF16),
             pltpu.VMEM((layers - 1, slab, early), BF16),
-            pltpu.VMEM((small_rows, LANES), F32),
-            pltpu.VMEM((2 * ranks, small_rows, LANES), F32),
-            dma((1,)),
+            pltpu.VMEM((3, small_rows, LANES), F32),
+            pltpu.VMEM((plane + layers - 1, small_rows, LANES), F32),
+            dma((11,)),
+            dma((ranks,)),
+            dma((ranks,)),
             dma((units,)),
             dma((units,)),
             dma((units, plane)),
             dma((units, plane)),
             dma((units, layers)),
             dma((units, layers)),
-            dma((2 * ranks,)),
-            dma((2 * ranks,)),
+            dma((plane + layers - 1,)),
+            dma((plane + layers - 1,)),
         ],
         compiler_params=pltpu.CompilerParams(
             collective_id=2, has_side_effects=True, vmem_limit_bytes=62 * MIB
@@ -968,8 +1107,9 @@
             transcendentals=0,
         ),
     )(
-        projected, projected, projected, attended, datt, kept, qkv_weight, qkv_weight, qkv_weight,
-        tile_of, normed_turned, tokens, dres, gain, dgain, bucket_of, first,
+        projected, projected, projected, kept, qkv_weight, qkv_weight, qkv_weight, tile_of, gains,
+        bucket_of, drouter, target, gate, normed_turned, tokens, cotangent, residual, attended,
+        out_weight, moved, made,
     )
 
 
@@ -1035,15 +1175,37 @@
 
     padded = -expert_count % LANES
     router_padded = jnp.pad(router_weight, ((0, 0), (0, padded)))
-    hidden, upstream_there = lax.optimization_barrier((hidden, upstream_there))
+    packed, normed_turned = lax.optimization_barrier((pack(hidden), normed_in.T))
     made, dmoved_back, grad_first, grad_second, drouter = run_expert(
-        pack(hidden), upstream_there, w_in, w_out, router_padded, expert_count
+        packed, upstream_there, w_in, w_out, router_padded, expert_count
     )
+    experts = lax.axis_size("expert")
+    cores = lax.axis_size("group")
+    slab = features // experts
+    gain_at = (core, me * slab)
+    router_at = (core * (expert_count // cores),)
+    if experts == 16 and cores == 2 and features % (16 * experts) == 0:
+        grad_tokens, grad_qkv, grad_out, router_sums, small, output, _ = run_tail(
+            projected, attended, kept, qkv_weight, out_weight, normed_turned, tokens, cotangent,
+            residual_one, gain_rows, drouter, target[:, None], gate_value[:, None], dmoved_back, made,
+            rows,
+        )
+        heads = rel_bias.shape[1]
+        gain_sums = small[heads + -heads % 4 :][: 2 * features // LANES].reshape(2, features)
+        return (
+            output,
+            grad_tokens,
+            lax.dynamic_slice(gain_sums, gain_at, (2 // cores, slab)),
+            grad_qkv,
+            grad_out,
+            small[:heads, :bucket_count].T,
+            lax.dynamic_slice(router_sums, (0, *router_at), (slab, expert_count // cores)),
+            grad_first[None],
+            grad_second[None],
+        )
+
     made_back = exchange(made)
     grad_router = drouter[:, :expert_count]
-
-    def finish():
-        return (residual_one + gate_value[:, None] * unpack(made_back)).astype(BF16)
 
     dhidden = unpack(dmoved_back)
     upstream = cotangent.astype(F32)
@@ -1052,38 +1214,6 @@
     dres = upstream + dres_norm
     dbranch = dres.astype(BF16)
     datt = lax.dot_general(dbranch, out_weight, NT, preferred_element_type=F32).astype(BF16)
-    experts = lax.axis_size("expert")
-    cores = lax.axis_size("group")
-    slab = features // experts
-    gain_at = (core, me * slab)
-    if experts == 16 and cores == 2 and expert_count <= 2 * LANES and features % (16 * experts) == 0:
-        dense_out = jnp.einsum(
-            "td,tce->cde",
-            attended,
-            dbranch.reshape(length, cores, features // cores),
-            preferred_element_type=F32,
-        )
-        router_half = jnp.moveaxis(grad_router.reshape(features, cores, -1), 1, 0)
-        router_half = jnp.pad(router_half, ((0, 0), (0, 0), (0, LANES - router_half.shape[2])))
-        first = jnp.concatenate([dense_out, router_half], axis=2).astype(BF16)
-        grad_tokens, grad_qkv, early, small = run_tail(
-            projected, attended, datt, kept, qkv_weight, normed_in.T, tokens, dres, gain_rows[:1],
-            dgain_two.reshape(-1, LANES), first, experts, bucket_count, rows,
-        )
-        heads = rel_bias.shape[1]
-        gain_sums = small[heads + -heads % 4 :][: 2 * features // LANES].reshape(2, features)
-        return (
-            finish(),
-            grad_tokens,
-            lax.dynamic_slice(gain_sums, gain_at, (2 // cores, slab)),
-            grad_qkv,
-            early[:, : features // cores],
-            small[:heads, :bucket_count].T,
-            early[:, features // cores : features // cores + expert_count // cores],
-            grad_first[None],
-            grad_second[None],
-        )
-
     grad_out = lax.dot_general(attended, dbranch, TN, preferred_element_type=F32)
     dqkv, band, far = attend_back(projected, attended, datt, kept, rows)
     grad_proj = jnp.einsum("td,cte->dce", normed_in, dqkv, preferred_element_type=F32)
@@ -1098,6 +1228,9 @@
     dinput_norm, dgain_one = back_one(dnormed)
     grad_tokens = dres + dinput_norm
 
+    brought = unpack(made_back)
+    output = (residual_one + gate_value[:, None] * brought).astype(BF16)
+
     def scattered(values):
         return lax.psum_scatter(
             core_sum(values, 1).astype(BF16), "expert", scatter_dimension=0, tiled=True
@@ -1116,12 +1249,10 @@
         at += s.size
     grad_gains = lax.dynamic_slice(summed[0], gain_at, (2 // cores, slab))
     grad_router = lax.dynamic_slice(
-        summed[1],
-        (me * slab, core * (expert_count // cores)),
-        (slab, expert_count // cores),
+        summed[1], (me * slab, *router_at), (slab, expert_count // cores)
     )
     return (
-        finish(),
+        output,
         grad_tokens,
         grad_gains,
         scattered(grad_proj),

time: 401 us -> 365 us (0.910)
  Pallas kernels: 276 us -> 301 us
  starting transfers between devices: 32.4 us -> 8.67 us
  matrix products: 43.1 us -> 23.2 us
  waiting for transfers between devices: 12 us -> 0.01 us
  other arithmetic: 8.76 us -> 4.3 us
    all_to_all x2 -> x1, starting transfers between devices: 32.4 us -> 8.67 us  [exchange(): lax.all_to_all(values, 'expert', split_axis=0, concat_axis=0, tiled=True)]
    pallas_call x1, Pallas kernels: 77.4 us -> 99.7 us  [run_tail(): pl.pallas_call(functools.partial(tail_kernel, rows=rows, ranks=ranks, pla...]
    dot_general x4 -> x0, matrix products: 20.3 us -> none  [the longest x2 14.9 us: unpack(): lax.dot_general(picks, values.reshape(-1, features), TN, preferred_elemen...]
    all_to_all x2 -> x1, waiting for transfers between devices: 12 us -> 0.01 us  [exchange(): lax.all_to_all(values, 'expert', split_axis=0, concat_axis=0, tiled=True)]
    unnamed x60 -> x44, local copies, waits for them, and re-layouts: 9.94 us -> 14.9 us
    slice x5 -> x0, local copies, waits for them, and re-layouts: 4.6 us -> none  [the longest x2 1.74 us: per_device(): grad_router = drouter[:, :expert_count]]
  transfers between devices with their start and end apart: 2 -> 1, of which waited for: 1 -> 0; matrix products, arithmetic and copies ran while one was open for 11% -> 6% of each run, Pallas kernels for 28% -> 10%
where the time goes in v4:
time: 365 us; the launch traced here: 362 us
  Pallas kernels  301 us (82%)
  matrix products  23.2 us (6%)
  local copies, waits for them, and re-layouts  22.7 us (6%)
  starting transfers between devices  8.67 us (2%)
  other arithmetic  4.3 us (1%)
    pallas_call x1, Pallas kernels, run_expert(): pl.pallas_call(functools.partial(expert_kernel, ranks=ranks, expert_count...  166 us
    pallas_call x1, Pallas kernels, run_tail(): pl.pallas_call(functools.partial(tail_kernel, rows=rows, ranks=ranks, pla...  99.7 us
    pallas_call x1, Pallas kernels, attend(): pl.pallas_call(functools.partial(attend_kernel, rows=rows), grid=(pairs,)...  35.4 us
    unnamed x44, local copies, waits for them, and re-layouts  14.9 us
    dot_general x2, matrix products, pack(): packed = jnp.dot(picks, values, preferred_element_type=F32).astype(BF16)  12 us
    all_to_all x1, starting transfers between devices, exchange(): lax.all_to_all(values, 'expert', split_axis=0, concat_axis=0, tiled=True)  8.67 us
    dot_general x1, matrix products, per_device(): jnp.dot(normed_in, qkv_weight, preferred_element_type=F32).astype(BF16)  7.7 us
  transfers between devices with their start and end apart: 1, of which 0 were waited for; matrix products, arithmetic and copies ran while one was open for 6% of the time, Pallas kernels for 10%

profile of v4, /device:TPU:0, one launch (start us, length us, event | category | flops | bytes accessed | tf_op | source)
XLA Modules:
  0.0 361.6 jit_solution(9986036420003504521)
XLA Ops:
  0.6 0.0 copy-start
  0.7 1.3 fusion.11
  2.6 0.7 add_select_fusion.2
  3.3 6.5 %fusion.6 = bf16[2048,768]{1,0:T(8,128)(2,1)} fusion(bf16[1024,768]{1,0:T(8,128)(2,1)} %cot_hbm.1, s32[1024]{0:T(1024)S(1)} %add_select_fusion.2), kind=kOutput, calls=%fused_computation.12 | convolution fusion | flops 3224895488 | bytes 4722688 | tf_op jit(solution)/shard_map/dot_general | solution.py:1154
  9.8 0.0 copy-start.3
  9.8 0.0 copy-start.9
  9.8 8.7 %all-to-all-start = ((bf16[16,128,768]{2,1,0:T(8,128)(2,1)}), bf16[16,128,768]{2,1,0:T(8,128)(2,1)}, u32[]{:S(2)}, u32[]{:S(2)}) async-start(bf16[16,128,768]{2,1,0:T(8,128)(2,1)} %bitcast.28), calls=%async_computation | async-start | bytes 6291456 | tf_op jit(solution)/shard_map/all_to_all | solution.py:1125
  18.5 0.0 copy-done.3
  18.5 0.4 fusion.7
  18.8 0.0 copy-done
  18.9 0.2 convolution_bitcast_fusion
  19.0 0.0 copy-done.13
  19.1 0.0 copy-start.12
  19.1 0.1 broadcast_in_dim.12.line_ref
  19.2 0.0 copy-done.9
  19.2 0.2 copy.37
  19.4 7.7 %convolution_convert_fusion.q_ref.k_ref.v_ref = bf16[1024,2304]{1,0:T(8,128)(2,1)} fusion(bf16[768,2304]{1,0:T(8,128)(2,1)} %wv_ref.1, bf16[1024,768]{1,0:T(8,128)(2,1)S(1)} %copy-done.3, f32[768]{0:T(1024)S(1)} %get-tuple-element.67, f32[1024]{0:T(1024)S(1)} %add_rsqrt_fusion.1), kind=kOutput, calls=%fused_computation.3 | convolution fusion | flops 3629383680 | bytes 9837568 | tf_op jit(solution)/shard_map/dot_general | solution.py:1166
  27.1 0.0 copy-done.12
  27.1 0.0 copy-start.14
  27.1 35.4 %shard_map.187 = (bf16[1024,768]{1,0:T(8,128)(2,1)S(1)}, bf16[12,1024,1024]{2,1,0:T(8,128)(2,1)}) custom-call(bf16[1024,2304]{1,0:T(8,128)(2,1)} %convolution_convert_fusion.q_ref.k_ref.v_ref, bf16[1024,2304]{1,0:T(8,128)(2,1)} %convolution_convert_fusion.q_ref.k_ref.v_ref, bf16[1024,2304]{1,0:T(8,128)(2,1)} %convolution_convert_fusion.q_ref.k_ref.v_ref, ...), custom_call_target="tpu_custom_call" | custom-call | flops 12884901888 | bytes 31457280 | tf_op jit(solution)/shard_map/pallas_call | solution.py:65
  62.4 0.0 copy-start.2
  62.4 0.0 copy-done.14
  62.4 1.5 multiply_reduce_fusion
  64.0 0.0 copy-done.2
  64.0 0.0 copy-start.5
  64.0 0.0 copy-start.11
  64.0 1.6 copy-done.5
  65.7 0.6 fusion.37
  66.3 0.0 copy-done.11
  66.4 1.0 copy.41.gate_ref
  67.4 0.4 fusion.13
  67.8 1.5 copy-done.6
  69.3 5.5 %fusion.5 = bf16[2048,768]{1,0:T(8,128)(2,1)} fusion(s32[1024]{0:T(1024)S(1)} %add_select_fusion.2, f32[1024,768]{1,0:T(8,128)S(1)} %copy-done.6, f32[768]{0:T(1024)S(1)} %get-tuple-element.66, f32[1024]{0:T(1024)S(1)} %add_rsqrt_fusion), kind=kOutput, calls=%fused_computation.11 | convolution fusion | flops 3227254784 | bytes 6302720 | tf_op jit(solution)/shard_map/dot_general | solution.py:1154
  74.8 1.8 copy.42.normed_hbm
  76.6 0.2 copy.38
  76.8 0.2 copy.39
  77.1 0.7 pad.4.router_ref
  77.8 0.0 copy-done.15
  77.8 0.1 broadcast_bitcast_fusion
  77.9 0.9 fusion.12.tile_ref
  78.8 0.9 fusion.15.bucket_ref
  79.7 0.9 add_select_fusion.target_ref
  80.6 0.0 all-to-all-done.cot_ref
  80.6 165.8 %shard_map.188 = (bf16[16,128,768]{2,1,0:T(8,128)(2,1)}, bf16[16,128,768]{2,1,0:T(8,128)(2,1)}, f32[768,1536]{1,0:T(8,128)}, f32[1536,768]{1,0:T(8,128)}, f32[768,128]{1,0:T(8,128)}) custom-call(bf16[16,128,768]{2,1,0:T(8,128)(2,1)} %bitcast.36, bf16[16,128,768]{2,1,0:T(8,128)(2,1)} %all-to-all-done.cot_ref, bf16[768,3072]{1,0:T(8,128)(2,1)} %bitcast.34, ...), custom_call_target="tpu_custom_call" | custom-call | flops 57982058496 | bytes 31457280 | tf_op jit(solution)/shard_map/pallas_call | solution.py:498
  246.4 99.7 %shard_map.189 = (f32[1024,768]{1,0:T(8,128)}, f32[48,1152]{1,0:T(8,128)}, f32[48,384]{1,0:T(8,128)}, f32[48,128]{1,0:T(8,128)}, f32[24,128]{1,0:T(8,128)}, /*in...) custom-call(bf16[1024,2304]{1,0:T(8,128)(2,1)} %convolution_convert_fusion.q_ref.k_ref.v_ref, ...), custom_call_target="tpu_custom_call" | custom-call | flops 28991029248 | bytes 48758784 | tf_op jit(solution)/shard_map/pallas_call | solution.py:1026
  346.1 0.0 copy-start.7
  346.1 0.9 slice.14
  347.0 1.4 slice_bitcast_fusion
  348.4 0.8 constant_dynamic-slice_fusion
  349.2 0.7 copy.43
  349.9 0.6 dynamic_slice.6
  350.5 2.7 copy.52
  353.1 0.0 copy-done.7
  353.1 1.7 copy.53
  354.8 0.0 copy-done.8
  354.8 0.7 copy.54
  355.5 0.0 copy-done.10
  355.5 0.6 copy.55
  356.1 0.7 copy-done.4
  356.9 2.2 copy.56
  359.1 0.0 slice-done
  359.1 0.2 slice-done.1
  359.2 2.2 copy.57
  361.4 0.0 copy-done.1
  (23 shorter events, 0.2 us)
Async XLA Ops:
  0.6 18.2 %copy-start = (bf16[32,12]{0,1:T(8,128)(2,1)S(1)}, bf16[32,12]{0,1:T(8,128)(2,1)}, u32[]{:S(2)}) copy-start(bf16[32,12]{0,1:T(8,128)(2,1)} %param.16) | copy-start | bytes 2308
  9.8 8.7 %copy-start.3 = (bf16[1024,768]{1,0:T(8,128)(2,1)S(1)}, bf16[1024,768]{1,0:T(8,128)(2,1)}, u32[]{:S(2)}) copy-start(bf16[1024,768]{1,0:T(8,128)(2,1)} %tokens_hbm.1) | copy-start | bytes 4718596
  9.8 9.3 %copy-start.13 = (bf16[2,768]{1,0:T(2,128)(2,1)S(1)}, bf16[2,768]{1,0:T(2,128)(2,1)}, u32[]{:S(2)}) copy-start(bf16[2,768]{1,0:T(2,128)(2,1)} %param.13) | copy-start | bytes 9220
  9.8 9.4 %copy-start.9 = (bf16[768,16]{0,1:T(8,128)(2,1)S(1)}, bf16[768,16]{0,1:T(8,128)(2,1)}, u32[]{:S(2)}) copy-start(bf16[768,16]{0,1:T(8,128)(2,1)} %param.17) | copy-start | bytes 73732
  9.8 70.8 %all-to-all-start = ((bf16[16,128,768]{2,1,0:T(8,128)(2,1)}), bf16[16,128,768]{2,1,0:T(8,128)(2,1)}, u32[]{:S(2)}, u32[]{:S(2)}) async-start(bf16[16,128,768]{2,1,0:T(8,128)(2,1)} %bitcast.28), calls=%async_computation | async-start | bytes 6291456 | tf_op jit(solution)/shard_map/all_to_all | solution.py:1125
  19.1 8.0 %copy-start.12 = (f32[2,768]{1,0:T(2,128)}, f32[2,768]{1,0:T(2,128)S(1)}, u32[]{:S(2)}) copy-start(f32[2,768]{1,0:T(2,128)S(1)} %convert_element_type.151.gain_ref) | copy-start | bytes 18436
  27.1 35.4 %copy-start.14 = (bf16[768,768]{1,0:T(8,128)(2,1)S(1)}, bf16[768,768]{1,0:T(8,128)(2,1)}, u32[]{:S(2)}) copy-start(bf16[768,768]{1,0:T(8,128)(2,1)} %out_weight_hbm.1) | copy-start | bytes 3538948
  62.4 1.5 copy-start.2
  64.0 1.7 copy-start.5
  64.0 2.3 copy-start.11
  67.4 1.9 copy-start.6
  74.8 3.0 copy-start.15
  346.1 7.0 %copy-start.7 = (f32[1024,768]{1,0:T(8,128)S(1)}, f32[1024,768]{1,0:T(8,128)}, u32[]{:S(2)}) copy-start(f32[1024,768]{1,0:T(8,128)} %get-tuple-element.82) | copy-start | bytes 9437188
  353.1 1.7 copy-start.8
  353.1 2.4 copy-start.10
  353.1 3.7 %copy-start.4 = (f32[768,1536]{1,0:T(8,128)S(1)}, f32[768,1536]{1,0:T(8,128)}, u32[]{:S(2)}) copy-start(f32[768,1536]{1,0:T(8,128)} %get-tuple-element.37) | copy-start | bytes 14155780
  355.5 3.6 slice-start
  356.9 2.4 slice-start.1
  356.9 4.5 %copy-start.1 = (bf16[32,12]{0,1:T(8,128)(2,1)S(1)}, bf16[32,12]{0,1:T(8,128)(2,1)}, u32[]{:S(2)}) copy-start(bf16[32,12]{0,1:T(8,128)(2,1)} %param.16) | copy-start | bytes 2308

commit v5 on v4

--- a/solution.py
+++ b/solution.py
@@ -222,6 +222,22 @@
     return LANES
 
 
+def turned(me, k, ranks, plane, sign):
+    if plane == 1:
+        return (me + ranks + sign * k) % ranks
+    layer, side = me // plane, me % plane
+    far, near = k // plane, k % plane
+    if ranks // plane % 4:
+        layers = ranks // plane
+        to_layer = (layer + layers + sign * far) % layers
+    else:
+        sets = ranks // plane // 4
+        low = (layer % 4 // 2 + far % 4 // 2) % 2 * 2 + (layer + far) % 2
+        to_layer = (layer // 4 + sets + sign * (far // 4)) % sets * 4 + low
+    to_side = (side // 2 + near // 2) % 2 * 2 + (side + near) % 2
+    return to_layer * plane + to_side
+
+
 def expert_kernel(
     hidden_ref, cot_ref, w_in_ref, w_out_ref, router_ref,
     made_ref, back_ref, first_ref, second_ref, drouter_ref,
@@ -235,11 +251,9 @@
     per_step = rows // slots
     core, me = lax.axis_index("group"), lax.axis_index("expert")
     plane = 4 if ranks % 4 == 0 else 1
-    layers = ranks // plane
 
     def partner(k, sign):
-        layer = (me // plane + layers + sign * (k // plane)) % layers
-        return layer * plane + (me % plane + plane + sign * (k % plane)) % plane
+        return turned(me, k, ranks, plane, sign)
 
     def span(k):
         return pl.ds(pl.multiple_of(k * slots, slots), slots)
@@ -355,6 +369,8 @@
         dexp_turned[:, block] = dexp.T
         drouter_ref[...] += jnp.dot(xt, dlogits, preferred_element_type=F32)
 
+    last = ranks // per_step - 1
+
     def step(number, carry):
         first_rank = number * per_step
         for inner in range(per_step):
@@ -365,12 +381,20 @@
             def _(k=k):
                 hidden_copy(k).wait_recv()
 
+        @pl.when(number == last)
+        def _():
+            def start_moved(k, carry):
+                moved_copy(k).start()
+                return carry
+
+            lax.fori_loop(plane, first_rank, start_moved, 0)
+
         run(first_rank)
         for inner in range(per_step):
             k = first_rank + inner
             made_copy(k).start()
 
-            @pl.when((k > 0) & (k < plane))
+            @pl.when((k > 0) & ((k < plane) | (number == last)))
             def _(k=k):
                 moved_copy(k).start()
 
@@ -381,12 +405,6 @@
         return carry
 
     lax.fori_loop(0, ranks // per_step, step, 0)
-
-    def start_moved(k, carry):
-        moved_copy(k).start()
-        return carry
-
-    lax.fori_loop(plane, ranks, start_moved, 0)
 
     other = 1 - core
     across = features // columns
@@ -643,7 +661,7 @@
         return total
 
     def partner(number):
-        return rank_of(in_line(number // plane, 1), in_plane(number % plane, 1))
+        return turned(me, number, ranks, plane, 1)
 
     def made_copy(number):
         return pltpu.make_async_remote_copy(

time: 365 us -> 349 us (0.956)
  Pallas kernels: 301 us -> 285 us
    pallas_call x1, Pallas kernels: 166 us -> 155 us  [run_expert(): pl.pallas_call(functools.partial(expert_kernel, ranks=ranks, expert_count...]
    pallas_call x1, Pallas kernels: 99.7 us -> 95 us  [run_tail(): pl.pallas_call(functools.partial(tail_kernel, rows=rows, ranks=ranks, pla...]
  transfers between devices with their start and end apart: 1 -> 1, of which waited for: 0 -> 0; matrix products, arithmetic and copies ran while one was open for 6% -> 7% of each run, Pallas kernels for 10% -> 10%
where the time goes in v5:
time: 349 us; the launch traced here: 346 us
  Pallas kernels  285 us (82%)
  matrix products  23.2 us (7%)
  local copies, waits for them, and re-layouts  22.7 us (7%)
  starting transfers between devices  8.67 us (2%)
  other arithmetic  4.3 us (1%)
    pallas_call x1, Pallas kernels, run_expert(): pl.pallas_call(functools.partial(expert_kernel, ranks=ranks, expert_count...  155 us
    pallas_call x1, Pallas kernels, run_tail(): pl.pallas_call(functools.partial(tail_kernel, rows=rows, ranks=ranks, pla...  95 us
    pallas_call x1, Pallas kernels, attend(): pl.pallas_call(functools.partial(attend_kernel, rows=rows), grid=(pairs,)...  35.4 us
    unnamed x44, local copies, waits for them, and re-layouts  14.9 us
    dot_general x2, matrix products, pack(): packed = jnp.dot(picks, values, preferred_element_type=F32).astype(BF16)  12 us
    all_to_all x1, starting transfers between devices, exchange(): lax.all_to_all(values, 'expert', split_axis=0, concat_axis=0, tiled=True)  8.67 us
    dot_general x1, matrix products, per_device(): jnp.dot(normed_in, qkv_weight, preferred_element_type=F32).astype(BF16)  7.7 us
  transfers between devices with their start and end apart: 1, of which 0 were waited for; matrix products, arithmetic and copies ran while one was open for 7% of the time, Pallas kernels for 10%

profile of v5, /device:TPU:0, one launch (start us, length us, event | category | flops | bytes accessed | tf_op | source)
XLA Modules:
  0.0 345.7 jit_solution(15669610886081710357)
XLA Ops:
  0.6 0.0 copy-start
  0.7 1.3 fusion.11
  2.6 0.7 add_select_fusion.2
  3.3 6.5 %fusion.6 = bf16[2048,768]{1,0:T(8,128)(2,1)} fusion(bf16[1024,768]{1,0:T(8,128)(2,1)} %cot_hbm.1, s32[1024]{0:T(1024)S(1)} %add_select_fusion.2), kind=kOutput, calls=%fused_computation.12 | convolution fusion | flops 3224895488 | bytes 4722688 | tf_op jit(solution)/shard_map/dot_general | solution.py:1172
  9.8 0.0 copy-start.3
  9.8 0.0 copy-start.13
  9.8 0.0 copy-start.9
  9.8 8.7 %all-to-all-start = ((bf16[16,128,768]{2,1,0:T(8,128)(2,1)}), bf16[16,128,768]{2,1,0:T(8,128)(2,1)}, u32[]{:S(2)}, u32[]{:S(2)}) async-start(bf16[16,128,768]{2,1,0:T(8,128)(2,1)} %bitcast.28), calls=%async_computation | async-start | bytes 6291456 | tf_op jit(solution)/shard_map/all_to_all | solution.py:1143
  18.5 0.0 copy-done.3
  18.5 0.4 fusion.7
  18.8 0.0 copy-done
  18.9 0.2 convolution_bitcast_fusion
  19.0 0.0 copy-done.13
  19.1 0.0 copy-start.12
  19.1 0.1 broadcast_in_dim.12.line_ref
  19.2 0.0 copy-done.9
  19.2 0.2 copy.37
  19.4 7.7 %convolution_convert_fusion.q_ref.k_ref.v_ref = bf16[1024,2304]{1,0:T(8,128)(2,1)} fusion(bf16[768,2304]{1,0:T(8,128)(2,1)} %wv_ref.1, bf16[1024,768]{1,0:T(8,128)(2,1)S(1)} %copy-done.3, f32[768]{0:T(1024)S(1)} %get-tuple-element.67, f32[1024]{0:T(1024)S(1)} %add_rsqrt_fusion.1), kind=kOutput, calls=%fused_computation.3 | convolution fusion | flops 3629383680 | bytes 9837568 | tf_op jit(solution)/shard_map/dot_general | solution.py:1184
  27.1 0.0 copy-done.12
  27.1 0.0 copy-start.14
  27.1 35.4 %shard_map.187 = (bf16[1024,768]{1,0:T(8,128)(2,1)S(1)}, bf16[12,1024,1024]{2,1,0:T(8,128)(2,1)}) custom-call(bf16[1024,2304]{1,0:T(8,128)(2,1)} %convolution_convert_fusion.q_ref.k_ref.v_ref, bf16[1024,2304]{1,0:T(8,128)(2,1)} %convolution_convert_fusion.q_ref.k_ref.v_ref, bf16[1024,2304]{1,0:T(8,128)(2,1)} %convolution_convert_fusion.q_ref.k_ref.v_ref, ...), custom_call_target="tpu_custom_call" | custom-call | flops 12884901888 | bytes 31457280 | tf_op jit(solution)/shard_map/pallas_call | solution.py:65
  62.4 0.0 copy-done.14
  62.4 1.5 multiply_reduce_fusion
  64.0 0.0 copy-done.2
  64.0 0.0 copy-start.5
  64.0 0.0 copy-start.11
  64.0 1.6 copy-done.5
  65.7 0.6 fusion.37
  66.3 0.0 copy-done.11
  66.4 1.0 copy.41.gate_ref
  67.4 0.4 fusion.13
  67.8 1.5 copy-done.6
  69.3 5.5 %fusion.5 = bf16[2048,768]{1,0:T(8,128)(2,1)} fusion(s32[1024]{0:T(1024)S(1)} %add_select_fusion.2, f32[1024,768]{1,0:T(8,128)S(1)} %copy-done.6, f32[768]{0:T(1024)S(1)} %get-tuple-element.66, f32[1024]{0:T(1024)S(1)} %add_rsqrt_fusion), kind=kOutput, calls=%fused_computation.11 | convolution fusion | flops 3227254784 | bytes 6302720 | tf_op jit(solution)/shard_map/dot_general | solution.py:1172
  74.8 1.8 copy.42.normed_hbm
  76.6 0.2 copy.38
  76.8 0.2 copy.39
  77.1 0.7 pad.4.router_ref
  77.8 0.0 copy-done.15
  77.8 0.1 broadcast_bitcast_fusion
  77.9 0.9 fusion.12.tile_ref
  78.8 0.9 fusion.15.bucket_ref
  79.7 0.9 add_select_fusion.target_ref
  80.6 0.0 all-to-all-done.cot_ref
  80.6 154.6 %shard_map.188 = (bf16[16,128,768]{2,1,0:T(8,128)(2,1)}, bf16[16,128,768]{2,1,0:T(8,128)(2,1)}, f32[768,1536]{1,0:T(8,128)}, f32[1536,768]{1,0:T(8,128)}, f32[768,128]{1,0:T(8,128)}) custom-call(bf16[16,128,768]{2,1,0:T(8,128)(2,1)} %bitcast.36, bf16[16,128,768]{2,1,0:T(8,128)(2,1)} %all-to-all-done.cot_ref, bf16[768,3072]{1,0:T(8,128)(2,1)} %bitcast.34, ...), custom_call_target="tpu_custom_call" | custom-call | flops 57982058496 | bytes 31457280 | tf_op jit(solution)/shard_map/pallas_call | solution.py:516
  235.2 95.0 %shard_map.189 = (f32[1024,768]{1,0:T(8,128)}, f32[48,1152]{1,0:T(8,128)}, f32[48,384]{1,0:T(8,128)}, f32[48,128]{1,0:T(8,128)}, f32[24,128]{1,0:T(8,128)}, /*in...) custom-call(bf16[1024,2304]{1,0:T(8,128)(2,1)} %convolution_convert_fusion.q_ref.k_ref.v_ref, ...), custom_call_target="tpu_custom_call" | custom-call | flops 28991029248 | bytes 48758784 | tf_op jit(solution)/shard_map/pallas_call | solution.py:1044
  330.2 0.0 copy-start.7
  330.2 0.9 slice.14
  331.1 1.4 slice_bitcast_fusion
  332.5 0.8 constant_dynamic-slice_fusion
  333.3 0.7 copy.43
  334.0 0.6 dynamic_slice.6
  334.6 2.7 copy.52
  337.2 0.0 copy-done.7
  337.2 1.7 copy.53
  338.9 0.0 copy-done.8
  338.9 0.7 copy.54
  339.6 0.0 copy-done.10
  339.6 0.6 copy.55
  340.2 0.7 copy-done.4
  341.0 2.2 copy.56
  343.2 0.0 slice-done
  343.2 0.2 slice-done.1
  343.3 2.2 copy.57
  345.5 0.0 copy-done.1
  (23 shorter events, 0.2 us)
Async XLA Ops:
  0.6 18.2 %copy-start = (bf16[32,12]{0,1:T(8,128)(2,1)S(1)}, bf16[32,12]{0,1:T(8,128)(2,1)}, u32[]{:S(2)}) copy-start(bf16[32,12]{0,1:T(8,128)(2,1)} %param.16) | copy-start | bytes 2308
  9.8 8.7 %copy-start.3 = (bf16[1024,768]{1,0:T(8,128)(2,1)S(1)}, bf16[1024,768]{1,0:T(8,128)(2,1)}, u32[]{:S(2)}) copy-start(bf16[1024,768]{1,0:T(8,128)(2,1)} %tokens_hbm.1) | copy-start | bytes 4718596
  9.8 9.3 %copy-start.13 = (bf16[2,768]{1,0:T(2,128)(2,1)S(1)}, bf16[2,768]{1,0:T(2,128)(2,1)}, u32[]{:S(2)}) copy-start(bf16[2,768]{1,0:T(2,128)(2,1)} %param.13) | copy-start | bytes 9220
  9.8 9.4 %copy-start.9 = (bf16[768,16]{0,1:T(8,128)(2,1)S(1)}, bf16[768,16]{0,1:T(8,128)(2,1)}, u32[]{:S(2)}) copy-start(bf16[768,16]{0,1:T(8,128)(2,1)} %param.17) | copy-start | bytes 73732
  9.8 70.8 %all-to-all-start = ((bf16[16,128,768]{2,1,0:T(8,128)(2,1)}), bf16[16,128,768]{2,1,0:T(8,128)(2,1)}, u32[]{:S(2)}, u32[]{:S(2)}) async-start(bf16[16,128,768]{2,1,0:T(8,128)(2,1)} %bitcast.28), calls=%async_computation | async-start | bytes 6291456 | tf_op jit(solution)/shard_map/all_to_all | solution.py:1143
  19.1 8.0 %copy-start.12 = (f32[2,768]{1,0:T(2,128)}, f32[2,768]{1,0:T(2,128)S(1)}, u32[]{:S(2)}) copy-start(f32[2,768]{1,0:T(2,128)S(1)} %convert_element_type.151.gain_ref) | copy-start | bytes 18436
  27.1 35.4 %copy-start.14 = (bf16[768,768]{1,0:T(8,128)(2,1)S(1)}, bf16[768,768]{1,0:T(8,128)(2,1)}, u32[]{:S(2)}) copy-start(bf16[768,768]{1,0:T(8,128)(2,1)} %out_weight_hbm.1) | copy-start | bytes 3538948
  62.4 1.5 copy-start.2
  64.0 1.7 copy-start.5
  64.0 2.3 copy-start.11
  67.4 1.9 copy-start.6
  74.8 3.0 copy-start.15
  330.2 7.0 %copy-start.7 = (f32[1024,768]{1,0:T(8,128)S(1)}, f32[1024,768]{1,0:T(8,128)}, u32[]{:S(2)}) copy-start(f32[1024,768]{1,0:T(8,128)} %get-tuple-element.82) | copy-start | bytes 9437188
  337.2 1.7 copy-start.8
  337.2 2.4 copy-start.10
  337.2 3.7 %copy-start.4 = (f32[768,1536]{1,0:T(8,128)S(1)}, f32[768,1536]{1,0:T(8,128)}, u32[]{:S(2)}) copy-start(f32[768,1536]{1,0:T(8,128)} %get-tuple-element.37) | copy-start | bytes 14155780
  339.6 3.6 %slice-start = ((s8[4718592]{0:T(1024)(128)(4,1)}), s8[4194304]{0:T(1024)(128)(4,1)S(1)}, s32[]{:S(2)}) async-start(s8[4718592]{0:T(1024)(128)(4,1)} %bitcast.24), calls=%async_computation.1 | async-start | bytes 8388608
  341.0 2.4 slice-start.1
  341.0 4.5 %copy-start.1 = (bf16[32,12]{0,1:T(8,128)(2,1)S(1)}, bf16[32,12]{0,1:T(8,128)(2,1)}, u32[]{:S(2)}) copy-start(bf16[32,12]{0,1:T(8,128)(2,1)} %param.16) | copy-start | bytes 2308
